TPU v7x, 256 devices: a whole 4x4x8 slice. The times are simulated.
256 devices in a mesh: lon: 32 (over z, y_hi, core), lat: 4 (over x), lev: 2 (over y_lo).
Axes of the slice: x: 4, y: 4 (y_hi: 2, y_lo: 2; y = y_hi * 2 + y_lo), z: 8, core: 2. Of those that a mesh axis runs over, the one named last changes fastest.
Arguments:
- fields: bfloat16 [2, 4, 48, 768, 192], P(None, 'lev', 'lat', 'lon'), may hold values from -6 to 6
- upstream: bfloat16 [2, 4, 48, 768, 192], P(None, 'lev', 'lat', 'lon'), may hold values from -6 to 6
- qkv_weight: bfloat16 [192, 576], replicated, may hold values from -0.4375 to 0.4375
- out_weight: bfloat16 [192, 192], replicated, may hold values from -0.4375 to 0.4375
- earth_bias: float32 [2, 8, 6, 3312], P('lev', 'lat'), may hold values from -6 to 260
Outputs:
- field_grad: float32 [2, 4, 48, 768, 192], P(None, 'lev', 'lat', 'lon')
- qkv_grad: float32 [192, 576], replicated
- out_grad: float32 [192, 192], replicated
- bias_grad: float32 [2, 8, 6, 3312], P('lev', 'lat')
All inputs are finite; a program needn't handle non-finite values.
Results may differ from a plain program's by a relative error of at most 0.0085.
Values may be sent and summed in bfloat16 or wider, within the bound.
No kernel may reach another device: no remote copies, remote signals or barrier semaphores. Data moves between devices by JAX's collectives and lax.ppermute only.
A program may use at most 128 MiB of HBM per device.

v0:
```python
import math

import jax
import jax.numpy as jnp
from jax import lax
from jax.sharding import PartitionSpec as P

HEADS = 6
WZ = 2
WH = 6
WW = 12
WIN = 144
PAIRS = 3312


NEG_FILL = -1e30
EPS = 1e-05


def from_behind(x, axis, by):
    devices = lax.axis_size(axis)
    return lax.ppermute(x, axis, [(i, (i + by) % devices) for i in range(devices)])


def as_sent(x):
    return jax.tree.map(lambda a: a.astype(jnp.bfloat16) if a.dtype == jnp.float32 else a, x)


def offset_onehot():
    first_pos = jnp.arange(WW, dtype=jnp.int32)[:, None]
    second_pos = jnp.arange(WW, dtype=jnp.int32)[None, :]
    offset = (first_pos - second_pos + WW - 1).reshape(WW * WW)
    return (offset[:, None] == jnp.arange(2 * WW - 1, dtype=jnp.int32)[None, :]).astype(jnp.float32)


def expand_pairs(pair_table):
    leading = pair_table.shape[:-1]
    lead_count = len(leading)
    gridded = pair_table.reshape(leading + (WZ, WZ, WH, WH, 2 * WW - 1))
    spread = jnp.dot(gridded, offset_onehot().T, precision=lax.Precision.HIGHEST)
    spread = spread.reshape(leading + (WZ, WZ, WH, WH, WW, WW))
    axes_order = tuple(range(lead_count)) + tuple(
        (lead_count + position for position in (0, 2, 4, 1, 3, 5))
    )
    return spread.transpose(axes_order).reshape(leading + (WIN, WIN))


def fold_pairs(score_grads):
    leading = score_grads.shape[:-2]
    lead_count = len(leading)
    unfolded = score_grads.reshape(leading + (WZ, WH, WW, WZ, WH, WW))
    axes_order = tuple(range(lead_count)) + tuple(
        (lead_count + position for position in (0, 3, 1, 4, 2, 5))
    )
    unfolded = unfolded.transpose(axes_order).reshape(leading + (WZ, WZ, WH, WH, WW * WW))
    folded = jnp.dot(unfolded, offset_onehot(), precision=lax.Precision.HIGHEST)
    return folded.reshape(leading + (PAIRS,))


def window_backward(raw_tokens, up_tokens, bias_full, allowed, qkv_weight, out_weight):
    windows_n, window_len, channels = raw_tokens.shape
    head_size = channels // HEADS
    scaling = head_size ** (-0.5)
    widened = raw_tokens.astype(jnp.float32)
    average = jnp.mean(widened, axis=-1, keepdims=True)
    centred = widened - average
    inv_std = lax.rsqrt(jnp.mean(centred * centred, axis=-1, keepdims=True) + EPS)
    normed = centred * inv_std
    normed_low = normed.astype(jnp.bfloat16).reshape(windows_n * window_len, channels)
    packed = jnp.dot(normed_low, qkv_weight, preferred_element_type=jnp.float32).astype(
        jnp.bfloat16
    )
    packed = packed.reshape(windows_n, window_len, 3, HEADS, head_size).transpose(2, 0, 3, 1, 4)
    query_heads = packed[0]
    key_heads = packed[1]
    value_heads = packed[2]
    scores = (
        jnp.einsum("nhqd,nhkd->nhqk", query_heads, key_heads, preferred_element_type=jnp.float32)
        * scaling
        + bias_full
    )
    scores = jnp.where(allowed[:, None], scores, NEG_FILL)
    highest = jnp.max(scores, axis=-1, keepdims=True)
    expos = jnp.exp(scores - highest)
    attn_probs = expos / jnp.sum(expos, axis=-1, keepdims=True)
    probs_low = attn_probs.astype(jnp.bfloat16)
    attended = jnp.einsum(
        "nhqk,nhkd->nhqd", probs_low, value_heads, preferred_element_type=jnp.float32
    ).astype(jnp.bfloat16)
    attended = attended.transpose(0, 2, 1, 3).reshape(windows_n * window_len, channels)
    up_rows = up_tokens.reshape(windows_n * window_len, channels)
    out_part = jnp.dot(attended.T, up_rows, preferred_element_type=jnp.float32)
    grad_att = jnp.dot(up_rows, out_weight.T, preferred_element_type=jnp.float32).astype(
        jnp.bfloat16
    )
    grad_att = grad_att.reshape(windows_n, window_len, HEADS, head_size).transpose(0, 2, 1, 3)
    grad_probs = jnp.einsum(
        "nhqd,nhkd->nhqk", grad_att, value_heads, preferred_element_type=jnp.float32
    )
    grad_values = jnp.einsum(
        "nhqk,nhqd->nhkd", probs_low, grad_att, preferred_element_type=jnp.float32
    )
    inner_sum = jnp.sum(attn_probs * grad_probs, axis=-1, keepdims=True)
    grad_scores = attn_probs * (grad_probs - inner_sum)
    scores_low = grad_scores.astype(jnp.bfloat16)
    grad_queries = (
        jnp.einsum("nhqk,nhkd->nhqd", scores_low, key_heads, preferred_element_type=jnp.float32)
        * scaling
    )
    grad_keys = (
        jnp.einsum("nhqk,nhqd->nhkd", scores_low, query_heads, preferred_element_type=jnp.float32)
        * scaling
    )
    grad_packed = jnp.stack([grad_queries, grad_keys, grad_values], axis=0).astype(jnp.bfloat16)
    grad_packed = grad_packed.transpose(1, 3, 0, 2, 4).reshape(windows_n * window_len, 3 * channels)
    qkv_part = jnp.dot(normed_low.T, grad_packed, preferred_element_type=jnp.float32)
    grad_units = jnp.dot(grad_packed, qkv_weight.T, preferred_element_type=jnp.float32)
    grad_units = grad_units.reshape(windows_n, window_len, channels)
    centre_grad = jnp.mean(grad_units, axis=-1, keepdims=True)
    along_normed = jnp.mean(grad_units * normed, axis=-1, keepdims=True)
    grad_raw = inv_std * (grad_units - centre_grad - normed * along_normed)
    return (grad_raw, qkv_part, out_part, grad_scores)


def body(fields, upstream, qkv_weight, out_weight, earth_bias):
    samples, levels, lat_rows, lon_cols, channels = fields.shape
    lev_half = WZ // 2
    lat_half = WH // 2
    lon_half = WW // 2
    keep_cols = lon_cols - lon_half
    received = from_behind((fields[:, :, :, :lon_half], upstream[:, :, :, :lon_half]), "lon", -1)
    moved_fields = jnp.concatenate([fields[:, :, :, lon_half:], received[0]], axis=3)
    moved_up = jnp.concatenate([upstream[:, :, :, lon_half:], received[1]], axis=3)
    lat_in = from_behind((moved_fields[:, :, :lat_half], moved_up[:, :, :lat_half]), "lat", -1)
    moved_fields = jnp.concatenate([moved_fields[:, :, lat_half:], lat_in[0]], axis=2)
    moved_up = jnp.concatenate([moved_up[:, :, lat_half:], lat_in[1]], axis=2)
    lev_in = from_behind((moved_fields[:, :lev_half], moved_up[:, :lev_half]), "lev", -1)
    moved_fields = jnp.concatenate([moved_fields[:, lev_half:], lev_in[0]], axis=1)
    moved_up = jnp.concatenate([moved_up[:, lev_half:], lev_in[1]], axis=1)
    lev_windows = levels // WZ
    lat_windows = lat_rows // WH
    lon_windows = lon_cols // WW
    window_count = lev_windows * lat_windows * lon_windows

    def to_windows(volume):
        volume = volume.reshape(
            samples, lev_windows, WZ, lat_windows, WH, lon_windows, WW, channels
        )
        return volume.transpose(0, 1, 3, 5, 2, 4, 6, 7).reshape(
            samples, window_count, WIN, channels
        )

    lev_global = lax.axis_index("lev") * levels + jnp.arange(levels, dtype=jnp.int32)
    lev_flag = (
        (lev_global >= lax.axis_size("lev") * levels - lev_half)
        .astype(jnp.int32)
        .reshape(lev_windows, WZ)
    )
    lat_global = lax.axis_index("lat") * lat_rows + jnp.arange(lat_rows, dtype=jnp.int32)
    lat_flag = (
        (lat_global >= lax.axis_size("lat") * lat_rows - lat_half)
        .astype(jnp.int32)
        .reshape(lat_windows, WH)
    )
    region = 2 * lev_flag[:, None, :, None, None] + lat_flag[None, :, None, :, None]
    region = jnp.broadcast_to(region, (lev_windows, lat_windows, WZ, WH, WW)).reshape(
        lev_windows, lat_windows, WIN
    )
    allowed = region[:, :, :, None] == region[:, :, None, :]
    allowed = jnp.broadcast_to(
        allowed[:, :, None], (lev_windows, lat_windows, lon_windows, WIN, WIN)
    )
    allowed = allowed.reshape(window_count, WIN, WIN)
    bias_full = expand_pairs(earth_bias)
    bias_full = jnp.broadcast_to(
        bias_full[:, :, None], (lev_windows, lat_windows, lon_windows, HEADS, WIN, WIN)
    )
    bias_full = bias_full.reshape(window_count, HEADS, WIN, WIN)

    def per_sample(carry, slices):
        raw_win, up_win = slices
        grad_raw, qkv_part, out_part, grad_scores = window_backward(
            raw_win, up_win, bias_full, allowed, qkv_weight, out_weight
        )
        score_sum = jnp.sum(
            grad_scores.reshape(lev_windows, lat_windows, lon_windows, HEADS, WIN, WIN), axis=2
        )
        return ((carry[0] + qkv_part, carry[1] + out_part, carry[2] + score_sum), grad_raw)

    start = (
        jnp.zeros((channels, 3 * channels), jnp.float32),
        jnp.zeros((channels, channels), jnp.float32),
        jnp.zeros((lev_windows, lat_windows, HEADS, WIN, WIN), jnp.float32),
    )
    totals, grad_windows = lax.scan(
        per_sample, start, (to_windows(moved_fields), to_windows(moved_up))
    )
    grad_rolled = grad_windows.reshape(
        samples, lev_windows, lat_windows, lon_windows, WZ, WH, WW, channels
    )
    grad_rolled = grad_rolled.transpose(0, 1, 4, 2, 5, 3, 6, 7).reshape(
        samples, levels, lat_rows, lon_cols, channels
    )
    lev_out = from_behind(
        grad_rolled[:, levels - lev_half :].astype(jnp.bfloat16), "lev", 1
    ).astype(jnp.float32)
    grad_rolled = jnp.concatenate([lev_out, grad_rolled[:, : levels - lev_half]], axis=1)
    lat_out = from_behind(as_sent(grad_rolled[:, :, lat_rows - lat_half :]), "lat", 1)
    grad_rolled = jnp.concatenate([lat_out, grad_rolled[:, :, : lat_rows - lat_half]], axis=2)
    back_in = from_behind(as_sent(grad_rolled[:, :, :, keep_cols:]), "lon", 1)
    field_grad = jnp.concatenate([back_in, grad_rolled[:, :, :, :keep_cols]], axis=3)
    window_part = fold_pairs(totals[2])
    bias_grad = lax.psum(window_part, "lon")
    weight_totals = lax.psum((totals[0], totals[1]), ("lon", "lat", "lev"))
    token_count = (
        samples
        * levels
        * lat_rows
        * lon_cols
        * lax.axis_size("lon")
        * lax.axis_size("lat")
        * lax.axis_size("lev")
    )
    factor = 1.0 / math.sqrt(token_count)
    return (field_grad, weight_totals[0] * factor, weight_totals[1] * factor, bias_grad)


def solution(mesh):
    return jax.shard_map(
        body,
        mesh=mesh,
        in_specs=(
            P(None, "lev", "lat", "lon", None),
            P(None, "lev", "lat", "lon", None),
            P(),
            P(),
            P("lev", "lat", None, None),
        ),
        out_specs=(P(None, "lev", "lat", "lon", None), P(), P(), P("lev", "lat", None, None)),
        check_vma=False,
    )
```

profile of v0, /device:TPU:1, one launch (start us, length us, event | category | flops | bytes accessed | tf_op | source)
XLA Modules:
  0.0 762.4 jit_solution(7319803878472429782)
XLA Ops:
  8.2 3.3 collective-permute-start.3
  12.4 6.3 collective-permute-start
  18.7 1.8 reshape.218
  20.5 8.9 %convolution_bitcast_fusion = f32[1,2,6,2,6,12,2,6,12]{8,7,4,6,3,2,1,5,0:T(8,128)} fusion(f32[2,6,2,2,6,6,23]{6,5,4,3,2,0,1:T(8,128)S(1)} %reshape.218, s32[12,12]{1,0:T(8,128)S(1)} %subtract_add_fusion), kind=kOutput, calls=%fused_computation.55 | convolution fusion | flops 68680944 | bytes 1154880 | tf_op jit(solution)/shard_map/dot_general | solution.py:40
  30.3 2.6 collective-permute-start.4
  33.8 1.5 collective-permute-done.4
  35.9 2.6 collective-permute-done.1
  38.6 13.8 %collective-permute-start.2 = (bf16[2,1,12,24,192]{4,3,2,1,0:T(8,128)(2,1)S(1)}, bf16[2,1,12,24,192]{4,3,2,1,0:T(8,128)(2,1)S(1)}, u32[]{:S(2)}, u32[]{:S(2)}) collective-permute-start(bf16[2,1,12,24,192]{4,3,2,1,0:T(8,128)(2,1)S(1)} %get-tuple-element.187), channel_id=1, source_target_pairs={{0,1},{1,0},{2,3},{3,2},{4,5},{5,4},{6,7},{7,6},{8,9},{9,8},{10,11... | collective-permute-start | bytes 663560 | tf_op jit(solution)/shard_map/ppermute | solution.py:22
  53.2 20.6 %copy.113 = f32[1,2,6,2,6,12,2,6,12]{5,4,3,8,7,6,2,1,0:T(8,128)} copy(f32[1,2,6,2,6,12,2,6,12]{8,7,4,6,3,2,1,5,0:T(8,128)} %convolution_bitcast_fusion) | data formatting | bytes 1990656
  73.9 10.2 %reshape.238 = f32[2,6,144,144]{2,3,1,0:T(8,128)} reshape(f32[1,2,6,2,6,12,2,6,12]{5,4,3,8,7,6,2,1,0:T(8,128)} %copy.113) | data formatting | bytes 1990656
  87.8 125.3 %while.17 = (s32[]{:T(128)}, f32[192,576]{1,0:T(8,128)}, f32[192,192]{1,0:T(8,128)}, f32[1,2,6,144,144]{3,4,2,1,0:T(8,128)}, f32[2,4,144,192]{3,0,2,1:T(2,128)},...) while((s32[]{:T(128)}, f32[192,576]{1,0:T(8,128)}, ...), condition=%wide.region_9.10_spmd.clone, body=%wide.region_0.9_spmd.clone.sunk | while | flops 674495872 | bytes 103003152 | solution.py:195
  93.2 4.0 fusion.103
  98.9 2.0 reshape.245
  100.9 1.9 multiply_reduce_fusion.6
  106.1 1.4 fusion.106
  107.6 4.8 fusion.104
  112.4 1.5 maximum_bitcast_fusion.2
  114.0 2.5 fusion.109
  116.5 1.3 multiply_bitcast_fusion.2
  117.8 1.4 copy.153
  119.3 14.1 %dynamic_update_slice.6 = f32[2,4,144,192]{3,0,2,1:T(2,128)} dynamic-update-slice(f32[2,4,144,192]{3,0,2,1:T(2,128)} %get-tuple-element.290, f32[1,4,144,192]{3,0,2,1:T(1,128)} %copy.153, s32[]{:T(128)} %get-tuple-element.286, s32[]{:T(128)} %constant.16.clone.1..sunk, s32[]{:T(128)} %constant.16.clone.1..sunk, s32[]{:T(128)} %constant.16.clone.1..sunk) | dynamic-update-slice | bytes 884740 | tf_op jit(solution)/shard_map/while/body/jit(dynamic_update_index_in_dim)/dynamic_update_slice | solution.py:195
  133.3 4.3 bitcast_reduce_fusion.2
  137.6 3.0 bitcast_add_fusion.3
  140.7 4.2 fusion.108
  155.0 4.0 fusion.103
  160.7 2.0 reshape.245
  162.7 1.9 multiply_reduce_fusion.6
  168.0 1.4 fusion.106
  169.4 4.8 fusion.104
  174.2 1.5 maximum_bitcast_fusion.2
  175.8 2.5 fusion.109
  178.3 1.3 multiply_bitcast_fusion.2
  179.7 1.4 copy.153
  181.1 14.1 %dynamic_update_slice.6 = f32[2,4,144,192]{3,0,2,1:T(2,128)} dynamic-update-slice(f32[2,4,144,192]{3,0,2,1:T(2,128)} %get-tuple-element.290, f32[1,4,144,192]{3,0,2,1:T(1,128)} %copy.153, s32[]{:T(128)} %get-tuple-element.286, s32[]{:T(128)} %constant.16.clone.1..sunk, s32[]{:T(128)} %constant.16.clone.1..sunk, s32[]{:T(128)} %constant.16.clone.1..sunk) | dynamic-update-slice | bytes 884740 | tf_op jit(solution)/shard_map/while/body/jit(dynamic_update_index_in_dim)/dynamic_update_slice | solution.py:195
  195.2 4.3 bitcast_reduce_fusion.2
  199.5 3.6 bitcast_add_fusion.3
  203.0 4.2 fusion.108
  210.8 2.3 convolution_add_fusion.4
  213.1 2.2 copy.97
  220.1 8.6 %reshape.223 = f32[1,2,6,2,6,12,2,6,12]{8,7,6,5,4,3,2,1,0:T(8,128)} reshape(f32[1,2,6,144,144]{4,3,2,1,0:T(8,128)S(1)} %copy.100) | data formatting | bytes 1990656 | tf_op jit(solution)/shard_map/reshape | solution.py:51
  228.7 14.1 %copy.115 = f32[1,2,6,2,2,6,6,12,12]{8,7,6,5,4,3,1,2,0:T(8,128)} copy(f32[1,2,6,2,2,6,6,12,12]{8,6,4,7,5,3,2,1,0:T(8,128)} %bitcast.224) | data formatting | bytes 1990656 | tf_op jit(solution)/shard_map/reshape.12
  242.7 9.6 %reshape.240 = f32[2,6,2,2,6,6,144]{6,5,4,3,2,0,1:T(8,128)S(1)} reshape(f32[1,2,6,2,2,6,6,12,12]{8,7,6,5,4,3,1,2,0:T(8,128)} %copy.115) | data formatting | bytes 1990656 | tf_op jit(solution)/shard_map/reshape.12
  257.1 245.2 %all-reduce.6.cloned.1.call-done = (f32[192,576]{1,0:T(8,128)}, f32[192,192]{1,0:T(8,128)}) async-done(((f32[192,576]{1,0:T(8,128)}, f32[192,192]{1,0:T(8,128)}), (f32[192,576]{1,0:T(8,128)}, f32[192,192]{1,0:T(8,128)})) %all-reduce.6.cloned.1.call-update) | async-done | bytes 589840 | tf_op jit(solution)/shard_map/psum | solution.py:214
  502.3 1.9 broadcast_multiply_fusion.3
  504.3 4.4 collective-permute-start.8
  509.4 1.9 collective-permute-done.8
  512.5 241.0 %all-reduce.4.cloned.1.call-done = f32[1,2,6,3312]{3,1,2,0:T(2,128)} async-done(((f32[1,2,6,3312]{3,1,2,0:T(2,128)}), f32[1,2,6,3312]{3,1,2,0:T(2,128)}) %all-reduce.4.cloned.1.call-update) | async-done | bytes 158992 | tf_op jit(solution)/shard_map/psum | solution.py:213
  753.6 1.6 copy.173
  (208 shorter events, 49.3 us)
Async XLA Ops:
  7.2 495.1 %all-reduce.6.cloned.1.call-start = ((), (), s32[]{:S(2)}) async-start(), calls=%async_computation.1 | async-start | bytes 1376256 | tf_op jit(solution)/shard_map/psum | solution.py:214
  8.2 22.1 %collective-permute-start.3 = (bf16[2,2,12,6,192]{4,3,2,1,0:T(8,128)(2,1)S(1)}, bf16[2,2,12,6,192]{4,3,2,1,0:T(8,128)(2,1)S(1)}, u32[]{:S(2)}, u32[]{:S(2)}) collective-permute-start(bf16[2,2,12,6,192]{4,3,2,1,0:T(8,128)(2,1)S(1)} %slice.73), channel_id=1, source_target_pairs={{0,248},{8,0},{16,8},{24,16},{32,24},{40,32},{48,40},{56,48},{64,5... | collective-permute-start | bytes 331784 | tf_op jit(solution)/shard_map/ppermute | solution.py:22
  12.4 20.4 %collective-permute-start = (bf16[2,2,12,6,192]{4,3,2,1,0:T(8,128)(2,1)S(1)}, bf16[2,2,12,6,192]{4,3,2,1,0:T(8,128)(2,1)S(1)}, u32[]{:S(2)}, u32[]{:S(2)}) collective-permute-start(bf16[2,2,12,6,192]{4,3,2,1,0:T(8,128)(2,1)S(1)} %slice.67), channel_id=1, source_target_pairs={{0,248},{8,0},{16,8},{24,16},{32,24},{40,32},{48,40},{56,48},{64,5... | collective-permute-start | bytes 331784 | tf_op jit(solution)/shard_map/ppermute | solution.py:22
  20.5 9.0 %copy-start.24 = (bf16[2,2,12,24,192]{4,3,2,1,0:T(8,128)(2,1)S(1)}, bf16[2,2,12,24,192]{4,3,2,1,0:T(8,128)(2,1)}, u32[]{:S(2)}) copy-start(bf16[2,2,12,24,192]{4,3,2,1,0:T(8,128)(2,1)} %param.8) | copy-start | bytes 1327108
  20.5 9.3 %copy-start.25 = (bf16[2,2,12,24,192]{4,3,2,1,0:T(8,128)(2,1)S(1)}, bf16[2,2,12,24,192]{4,3,2,1,0:T(8,128)(2,1)}, u32[]{:S(2)}) copy-start(bf16[2,2,12,24,192]{4,3,2,1,0:T(8,128)(2,1)} %param.7) | copy-start | bytes 1327108
  30.3 5.1 collective-permute-start.4
  32.9 5.6 collective-permute-start.1
  35.5 48.6 %collective-permute-start.5 = (bf16[2,1,12,24,192]{4,3,2,1,0:T(8,128)(2,1)S(1)}, bf16[2,1,12,24,192]{4,3,2,1,0:T(8,128)(2,1)S(1)}, u32[]{:S(2)}, u32[]{:S(2)}) collective-permute-start(bf16[2,1,12,24,192]{4,3,2,1,0:T(8,128)(2,1)S(1)} %get-tuple-element.185), channel_id=1, source_target_pairs={{0,1},{1,0},{2,3},{3,2},{4,5},{5,4},{6,7},{7,6},{8,9},{9,8},{10,11... | collective-permute-start | bytes 663560 | tf_op jit(solution)/shard_map/ppermute | solution.py:22
  38.6 47.8 %collective-permute-start.2 = (bf16[2,1,12,24,192]{4,3,2,1,0:T(8,128)(2,1)S(1)}, bf16[2,1,12,24,192]{4,3,2,1,0:T(8,128)(2,1)S(1)}, u32[]{:S(2)}, u32[]{:S(2)}) collective-permute-start(bf16[2,1,12,24,192]{4,3,2,1,0:T(8,128)(2,1)S(1)} %get-tuple-element.187), channel_id=1, source_target_pairs={{0,1},{1,0},{2,3},{3,2},{4,5},{5,4},{6,7},{7,6},{8,9},{9,8},{10,11... | collective-permute-start | bytes 663560 | tf_op jit(solution)/shard_map/ppermute | solution.py:22
  87.8 2.8 copy-start.21
  90.4 1.9 copy-start.11
  93.2 4.0 copy-start
  93.2 4.0 copy-start.14
  93.2 4.7 copy-start.23
  100.9 2.0 copy-start.12
  102.8 1.8 copy-start.1
  102.8 1.8 copy-start.20
  102.8 2.2 copy-start.5
  113.9 2.6 copy-start.2
  137.6 3.0 copy-start.13
  140.7 4.8 copy-start.9
  140.7 4.8 copy-start.15
  146.1 1.8 copy-start.16
  148.2 1.5 copy-start.22
  149.7 2.8 copy-start.21
  152.3 1.9 copy-start.11
  155.0 4.0 copy-start
  155.0 4.0 copy-start.14
  155.0 4.7 copy-start.23
  162.7 2.0 copy-start.12
  164.6 1.8 copy-start.1
  164.7 1.8 copy-start.20
  164.7 2.2 copy-start.5
  175.7 2.6 copy-start.2
  199.5 3.6 copy-start.13
  203.0 4.8 copy-start.9
  203.0 4.8 copy-start.15
  208.5 1.8 copy-start.16
  210.6 2.5 copy-start.18
  210.6 2.5 copy-start.22
  215.9 3.1 copy-start.10
  217.1 38.0 %collective-permute-start.6 = (bf16[2,1,12,24,192]{4,3,2,1,0:T(8,128)(2,1)}, bf16[2,1,12,24,192]{4,3,2,1,0:T(8,128)(2,1)}, u32[]{:S(2)}, u32[]{:S(2)}) collective-permute-start(bf16[2,1,12,24,192]{4,3,2,1,0:T(8,128)(2,1)} %copy.98), channel_id=1, source_target_pairs={{0,1},{1,0},{2,3},{3,2},{4,5},{5,4},{6,7},{7,6},{8,9},{9,8},{10,11... | collective-permute-start | bytes 663560 | tf_op jit(solution)/shard_map/ppermute | solution.py:22
  242.7 9.7 %copy-start.27 = (s32[144]{0:T(256)S(1)}, s32[144]{0:T(256)}, u32[]{:S(2)}) copy-start(s32[144]{0:T(256)} %sub.92) | copy-start | bytes 1732
  252.4 501.2 %all-reduce.4.cloned.1.call-start = ((), (), s32[]{:S(2)}) async-start(), calls=%async_computation | async-start | bytes 319488 | tf_op jit(solution)/shard_map/psum | solution.py:213
  253.7 2.3 copy-start.19
  256.1 248.0 %collective-permute-start.7 = (bf16[2,2,3,24,192]{4,3,2,1,0:T(8,128)(2,1)S(1)}, bf16[2,2,3,24,192]{4,3,2,1,0:T(8,128)(2,1)S(1)}, u32[]{:S(2)}, u32[]{:S(2)}) collective-permute-start(bf16[2,2,3,24,192]{4,3,2,1,0:T(8,128)(2,1)S(1)} %fusion.33), channel_id=1, source_target_pairs={{0,2},{2,4},{4,6},{6,0},{1,3},{3,5},{5,7},{7,1},{8,10},{10,12},{12... | collective-permute-start | bytes 331784 | tf_op jit(solution)/shard_map/ppermute | solution.py:22
  504.2 4.6 copy-start.26
  504.3 7.0 collective-permute-start.8
  (12 other events, 13.8 us)
Sparse Core Ops, SparseCore 0:
  252.5 249.7 all-reduce.5
  505.7 247.8 all-reduce.3
where the time goes:
time: 773 us; the launch traced here: 762 us
  waiting for transfers between devices  492 us (64%)
  local copies, waits for them, and re-layouts  132 us (17%)
  matrix products  50.6 us (7%)
  other arithmetic  38.6 us (5%)
  starting transfers between devices  33.6 us (4%)
  between operations  14.7 us (2%)
    psum x1, waiting for transfers between devices, body(): weight_totals = lax.psum((totals[0], totals[1]), ('lon', 'lat', 'lev'))  245 us
    psum x1, waiting for transfers between devices, body(): bias_grad = lax.psum(window_part, 'lon')  241 us
    unnamed x20, local copies, waits for them, and re-layouts  34.4 us
    ppermute x9, starting transfers between devices, from_behind(): lax.ppermute(x, axis, [(i, (i + by) % devices) for i in range(devices)])  33.5 us
    dynamic_update_slice x4, local copies, waits for them, and re-layouts, body(): lax.scan(per_sample, start, (to_windows(moved_fields), to_windows(moved_u...  31 us
    another operation x3, local copies, waits for them, and re-layouts  25.5 us
  transfers between devices with their start and end apart: 11, of which 5 were waited for; matrix products, arithmetic and copies ran while one was open for 12% of the time, Pallas kernels for 0%

commit v1 on v0

v1 whole, which is shorter than its diff:
```python
import functools
import math

import jax
import jax.numpy as jnp
from jax import lax
from jax.experimental import pallas as pl
from jax.experimental.pallas import tpu as pltpu
from jax.sharding import PartitionSpec as P

HEADS = 6
WZ = 2
WH = 6
WW = 12
WIN = 144
PAIRS = 3312
C = 192
HD = 32
OFFS = 2 * WW - 1
GROUP = WH * OFFS
LANES = 384
KEYS = 256
NEG_FILL = -1e30
EPS = 1e-05
SCALE = HD**-0.5
SLAB = 1536
WROWS = 1152
BF = jnp.bfloat16
F32 = jnp.float32
CHUNK = 48
VMEM = pl.BlockSpec(memory_space=pltpu.VMEM)
HBM = pl.BlockSpec(memory_space=pl.ANY)


def params(mib):
    return pltpu.CompilerParams(vmem_limit_bytes=mib * 1024 * 1024)


def cost(flops, nbytes):
    return pl.CostEstimate(flops=flops, bytes_accessed=nbytes, transcendentals=0)


def dot(a, b, ca=1, cb=0):
    return lax.dot_general(a, b, (((ca,), (cb,)), ((), ())), preferred_element_type=F32)


def shape(dims, dtype):
    return jax.ShapeDtypeStruct(dims, dtype)


def pack_first_kernel(f, u, lev, lat, diag):
    for t, src in enumerate((f, u)):
        for b in range(2):
            for r in range(9):
                lev[t, b, r] = src[b, 0, r + 3]
            for r in range(3):
                lat[t, b, r] = src[b, 1, r]
                diag[t, b, r] = src[b, 0, r]


def pack_first(fields, upstream):
    return pl.pallas_call(
        pack_first_kernel,
        name="pack_first",
        out_shape=(
            shape((2, 2, 9, 24, C), BF),
            shape((2, 2, 3, 24, C), BF),
            shape((2, 2, 3, 24, C), BF),
        ),
        in_specs=[VMEM] * 2,
        out_specs=(VMEM,) * 3,
        compiler_params=params(32),
        cost_estimate=cost(0, 2 * 1024 * 1024),
    )(fields, upstream)


def source_line(own, lev, lat, diag, t, b, z, r):
    if z == 0:
        return own[b, 1, r + 3] if r < 9 else lat[t, b, r - 9]
    return lev[t, b, r] if r < 9 else diag[t, b, r - 9]


def pack_lon_kernel(f, u, lev, lat, diag, out, tmp):
    for t, own in enumerate((f, u)):
        for b in range(2):
            for z in range(2):
                for r in range(12):
                    line = source_line(own, lev, lat, diag, t, b, z, r)
                    row = (t * 2 + b) * WIN + (z * 12 + r) * 6
                    tmp[row : row + 6, :] = line.astype(F32)[0:6]
    out[...] = tmp[...].astype(BF)


def pack_lon(fields, upstream, lev, lat, diag):
    return pl.pallas_call(
        pack_lon_kernel,
        name="pack_lon",
        out_shape=shape((4 * WIN, C), BF),
        in_specs=[VMEM] * 5,
        out_specs=VMEM,
        scratch_shapes=[pltpu.VMEM((4 * WIN, C), F32)],
        compiler_params=params(32),
        cost_estimate=cost(0, 2 * 1024 * 1024),
    )(fields, upstream, lev, lat, diag)


def onehot_rows(target, w1):
    lane = lax.broadcasted_iota(jnp.int32, (LANES, KEYS), 0)
    return jnp.where(lane == target + w1, 1.0, 0.0).astype(BF)


def expand_kernel(eb, target, rq, rk, out_a, out_b, spread):
    spread[...] = jnp.zeros_like(spread)
    for z1 in range(2):
        for h1 in range(6):
            g = z1 * 6 + h1
            for z2 in range(2):
                off = ((z1 * 2 + z2) * 6 + h1) * GROUP
                for aw in range(2):
                    spread[g * 16 + aw * 6 : g * 16 + aw * 6 + 6, z2 * GROUP : (z2 + 1) * GROUP] = eb[
                        0, aw, :, off : off + GROUP
                    ]
    full = spread[...]
    high = full.astype(BF)
    rest = full - high.astype(F32)
    mid = rest.astype(BF)
    low = (rest - mid.astype(F32)).astype(BF)
    row = lax.broadcasted_iota(jnp.int32, (12, 1), 0)
    tgt = target[...]
    for w1 in range(WW):
        hot = onehot_rows(tgt, w1)
        block = dot(high, hot) + (dot(mid, hot) + dot(low, hot))
        for g in range(12):
            q = g * 12 + w1
            part = block[g * 16 : g * 16 + 12]
            ok0 = rq[0, q : q + 1, :] == rk[0]
            ok1 = rq[1, q : q + 1, :] == rk[1]
            ok = ((row < 6) & ok0) | ((row >= 6) & ok1)
            part = jnp.where(ok, part, NEG_FILL)
            out_a[pl.ds(q, 12, stride=WIN), :] = part[:, 0:128]
            out_b[pl.ds(q, 12, stride=WIN), :] = part[:, 128:256]


def expand(earth_bias, target, rq, rk):
    return pl.pallas_call(
        expand_kernel,
        name="expand_bias",
        out_shape=(shape((12 * WIN, 128), F32),) * 2,
        in_specs=[VMEM] * 4,
        out_specs=(VMEM, VMEM),
        scratch_shapes=[pltpu.VMEM((192, LANES), F32)],
        compiler_params=params(32),
        cost_estimate=cost(12 * 3 * 2 * 192 * LANES * WIN, 4 * 1024 * 1024),
    )(earth_bias, target, rq, rk)


def main_kernel(
    f, u, lev, lat, diag, lon, wq, wk, wv, wo, bias_a, bias_b, target,
    lines, lon_back, slab,
    x_s, u_s, g_s, gb_a, gb_b, s_s, gp_s, p_s, gs_s, w_s, lon_s, spread,
):
    for t, (own, dst) in enumerate(((f, x_s), (u, u_s))):
        for b in range(2):
            halo = lon[(t * 2 + b) * WIN : (t * 2 + b + 1) * WIN, :].astype(F32)
            for z in range(2):
                for r in range(12):
                    line = source_line(own, lev, lat, diag, t, b, z, r).astype(F32)
                    w = (r // 6) * 4 + b * 2
                    off = z * 72 + (r % 6) * 12
                    hrow = (z * 12 + r) * 6
                    dst[w, off : off + 12, :] = line[6:18]
                    dst[w + 1, off : off + 6, :] = line[18:24]
                    dst[w + 1, off + 6 : off + 12, :] = halo[hrow : hrow + 6]
    gb_a[...] = jnp.zeros_like(gb_a)
    gb_b[...] = jnp.zeros_like(gb_b)
    w_s[...] = jnp.zeros_like(w_s)
    lane = lax.broadcasted_iota(jnp.int32, (1, C), 1)
    picks = [(lane >= h * HD) & (lane < (h + 1) * HD) for h in range(HEADS)]
    picks_low = [jnp.where(m, 1.0, 0.0).astype(BF) for m in picks]
    picks_f = [jnp.where(m, 1.0, 0.0) for m in picks]

    def stack(a):
        return jnp.concatenate([a * m for m in picks_low], axis=0)

    def unstack(a):
        total = a[0:WIN] * picks_f[0]
        for h in range(1, HEADS):
            total = total + a[h * WIN : (h + 1) * WIN] * picks_f[h]
        return total

    def window(w, carry):
        start = pl.multiple_of((w // 4) * (HEADS * WIN), HEADS * WIN)
        raw = x_s[w]
        centred = raw - jnp.mean(raw, axis=-1, keepdims=True)
        inv_std = lax.rsqrt(jnp.mean(centred * centred, axis=-1, keepdims=True) + EPS)
        normed = centred * inv_std
        low = normed.astype(BF)
        q = dot(low, wq[...]).astype(BF)
        k = dot(low, wk[...]).astype(BF)
        v = dot(low, wv[...]).astype(BF)
        up = u_s[w].astype(BF)
        ga = dot(up, wo[...], 1, 1).astype(BF)
        qs = stack(q)
        gas = stack(ga)
        s_s[...] = dot(qs, k, 1, 1)
        gp_s[...] = dot(gas, v, 1, 1)
        for i in range(HEADS * WIN // CHUNK):
            rows = slice(i * CHUNK, (i + 1) * CHUNK)
            brows = pl.ds(pl.multiple_of(start + i * CHUNK, CHUNK), CHUNK)
            both = jnp.concatenate([bias_a[brows, :], bias_b[brows, 0:16]], axis=1)
            s = s_s[rows, :] * SCALE + both
            e = jnp.exp(s - jnp.max(s, axis=-1, keepdims=True))
            p = e * (1.0 / jnp.sum(e, axis=-1, keepdims=True))
            gp = gp_s[rows, :]
            gs = p * (gp - jnp.sum(p * gp, axis=-1, keepdims=True))
            p_s[rows, :] = p.astype(BF)
            gs_s[rows, :] = gs.astype(BF)
            gb_a[brows, :] += gs[:, 0:128]
            gb_b[brows, 0:16] += gs[:, 128:144]
        p = p_s[...]
        gs = gs_s[...]
        att = unstack(dot(p, v)).astype(BF)
        gv = dot(p, gas, 0, 0).astype(BF)
        gq = (unstack(dot(gs, k)) * SCALE).astype(BF)
        gk = (dot(gs, qs, 0, 0) * SCALE).astype(BF)
        w_s[0:C, :] += dot(low, gq, 0, 0)
        w_s[C : 2 * C, :] += dot(low, gk, 0, 0)
        w_s[2 * C : 3 * C, :] += dot(low, gv, 0, 0)
        w_s[3 * C : 4 * C, :] += dot(att, up, 0, 0)
        gu = dot(gq, wq[...], 1, 1) + dot(gk, wk[...], 1, 1) + dot(gv, wv[...], 1, 1)
        centre = jnp.mean(gu, axis=-1, keepdims=True)
        along = jnp.mean(gu * normed, axis=-1, keepdims=True)
        g_s[w] = inv_std * (gu - centre - normed * along)
        return carry

    lax.fori_loop(0, 8, window, 0)

    for b in range(2):
        for z in range(2):
            for r in range(12):
                w = (r // 6) * 4 + b * 2
                off = z * 72 + (r % 6) * 12
                row = b * WIN + (z * 12 + r) * 6
                second = g_s[w + 1, off : off + 12, :]
                line = jnp.concatenate(
                    [jnp.zeros((6, C), F32), g_s[w, off : off + 12, :], second[0:6]], axis=0
                )
                lines[b, z, r] = line.astype(BF)
                lon_s[row : row + 6, :] = second[6:12]
    lon_back[...] = lon_s[...].astype(BF)

    slab[0:768, :] = w_s[:, 0:128].astype(BF)
    slab[768:1152, :] = jnp.concatenate([w_s[0:384, 128:192], w_s[384:768, 128:192]], axis=1).astype(BF)
    folded = jnp.zeros((192, LANES), F32)
    tgt = target[...]
    for w1 in range(WW):
        for g in range(12):
            picked = pl.ds(g * 12 + w1, 12, stride=WIN)
            spread[g * 16 : g * 16 + 12, 0:128] = gb_a[picked, :]
            spread[g * 16 : g * 16 + 12, 128:256] = gb_b[picked, :]
        full = spread[...]
        high = full.astype(BF)
        mid = (full - high.astype(F32)).astype(BF)
        hot = onehot_rows(tgt, w1)
        folded = folded + (dot(high, hot, 1, 1) + dot(mid, hot, 1, 1))
    tight = jnp.concatenate([folded[g * 16 : g * 16 + 12] for g in range(12)], axis=0)
    slab[1152:1296, :] = tight[:, 0:128].astype(BF)
    slab[1296:1440, :] = tight[:, 128:256].astype(BF)
    rest = [tight[24 * i : 24 * i + 24, 256:276] for i in range(6)]
    rest = jnp.concatenate(rest + [jnp.zeros((24, 8), F32)], axis=1)
    slab[1440:1536, :] = jnp.concatenate([rest, jnp.zeros((72, 128), F32)], axis=0).astype(BF)


def windows(fields, upstream, lev, lat, diag, lon, wq, wk, wv, wo, bias_a, bias_b, target):
    return pl.pallas_call(
        main_kernel,
        name="windows",
        out_shape=(
            shape((2, 2, 12, 24, C), BF),
            shape((2 * WIN, C), BF),
            shape((SLAB, 128), BF),
        ),
        in_specs=[VMEM] * 13,
        out_specs=(VMEM, VMEM, VMEM),
        scratch_shapes=[
            pltpu.VMEM((8, WIN, C), F32),
            pltpu.VMEM((8, WIN, C), F32),
            pltpu.VMEM((8, WIN, C), F32),
            pltpu.VMEM((12 * WIN, 128), F32),
            pltpu.VMEM((12 * WIN, 128), F32),
            pltpu.VMEM((HEADS * WIN, WIN), F32),
            pltpu.VMEM((HEADS * WIN, WIN), F32),
            pltpu.VMEM((HEADS * WIN, WIN), BF),
            pltpu.VMEM((HEADS * WIN, WIN), BF),
            pltpu.VMEM((4 * C, C), F32),
            pltpu.VMEM((2 * WIN, C), F32),
            pltpu.VMEM((192, KEYS), F32),
        ],
        compiler_params=params(48),
        cost_estimate=cost(2 * 10**9, 8 * 1024 * 1024),
    )(fields, upstream, lev, lat, diag, lon, wq, wk, wv, wo, bias_a, bias_b, target)


def merge_kernel(lines, lon_in, own, lev, lat, diag):
    for b in range(2):
        halo = lon_in[b * WIN : (b + 1) * WIN, :].astype(F32)
        for z in range(2):
            for r in range(12):
                row = (z * 12 + r) * 6
                line = jnp.concatenate(
                    [halo[row : row + 6], lines[b, z, r].astype(F32)[6:24]], axis=0
                ).astype(BF)
                if z == 0:
                    if r < 9:
                        own[b, r] = line
                    else:
                        lat[b, r - 9] = line
                elif r < 9:
                    lev[b, r] = line
                else:
                    diag[b, r - 9] = line


def merge(lines, lon_in):
    return pl.pallas_call(
        merge_kernel,
        name="merge_lon",
        out_shape=(
            shape((2, 9, 24, C), BF),
            shape((2, 9, 24, C), BF),
            shape((2, 3, 24, C), BF),
            shape((2, 3, 24, C), BF),
        ),
        in_specs=[VMEM] * 2,
        out_specs=(VMEM,) * 4,
        compiler_params=params(32),
        cost_estimate=cost(2 * 10**10, 2 * 1024 * 1024),
    )(lines, lon_in)


def place_kernel(own, lev, lat, diag, out):
    for b in range(2):
        out[b, 1, 3:12] = own[b].astype(F32)
        out[b, 1, 0:3] = lat[b].astype(F32)
        out[b, 0, 3:12] = lev[b].astype(F32)
        out[b, 0, 0:3] = diag[b].astype(F32)


def place(own, lev, lat, diag):
    return pl.pallas_call(
        place_kernel,
        name="place_grad",
        out_shape=shape((2, 2, 12, 24, C), F32),
        in_specs=[VMEM] * 4,
        out_specs=VMEM,
        compiler_params=params(32),
        cost_estimate=cost(2 * 10**10, 2 * 1024 * 1024),
    )(own, lev, lat, diag)


def finish_kernel(factor, slab, qkv, out, bias):
    full = slab[...].astype(F32)
    right = full[768:1152]
    rest = jnp.concatenate([right[:, 0:64], right[:, 64:128]], axis=0)
    whole = jnp.concatenate([full[0:768], rest], axis=1) * factor
    for j in range(3):
        qkv[:, j * C : (j + 1) * C] = whole[j * C : (j + 1) * C]
    out[...] = whole[3 * C : 4 * C]
    tail = full[1440:1464]
    tail = jnp.concatenate([tail[:, 20 * i : 20 * i + 20] for i in range(6)], axis=0)
    pairs = jnp.concatenate([full[1152:1296], full[1296:1440], tail], axis=1)
    for z1 in range(2):
        for h1 in range(6):
            g = z1 * 6 + h1
            for z2 in range(2):
                off = ((z1 * 2 + z2) * 6 + h1) * GROUP
                for aw in range(2):
                    bias[0, aw, :, off : off + GROUP] = pairs[
                        g * 12 + aw * 6 : g * 12 + aw * 6 + 6, z2 * GROUP : (z2 + 1) * GROUP
                    ]


def finish(slab, factor):
    return pl.pallas_call(
        functools.partial(finish_kernel, factor),
        name="finish_params",
        out_shape=(
            shape((C, 3 * C), F32),
            shape((C, C), F32),
            shape((1, 2, HEADS, PAIRS), F32),
        ),
        in_specs=[VMEM],
        out_specs=(VMEM,) * 3,
        compiler_params=params(32),
        cost_estimate=cost(0, 2 * 1024 * 1024),
    )(slab)


def from_behind(x, axis, by):
    devices = lax.axis_size(axis)
    return lax.ppermute(x, axis, [(i, (i + by) % devices) for i in range(devices)])


def from_corner(x, by):
    lats, levs = lax.axis_size("lat"), lax.axis_size("lev")
    pairs = [
        (a * levs + v, ((a + by) % lats) * levs + (v + by) % levs)
        for a in range(lats)
        for v in range(levs)
    ]
    return lax.ppermute(x, ("lat", "lev"), pairs)


def reduce_slab(slab):
    lons = lax.axis_size("lon")
    others = lax.axis_size("lat") * lax.axis_size("lev")
    rows = SLAB // lons
    pieces = lax.all_to_all(slab.reshape(lons, rows, 128), "lon", 0, 0, tiled=True)
    mine = jnp.sum(pieces.astype(F32), axis=0).astype(BF)
    every = lax.all_to_all(
        jnp.broadcast_to(mine[None], (others, rows, 128)), ("lat", "lev"), 0, 0, tiled=True
    )
    total = jnp.sum(every.astype(F32), axis=0).astype(BF)
    mine = jnp.where(lax.axis_index("lon") * rows < WROWS, total, mine)
    full = lax.all_to_all(jnp.broadcast_to(mine[None], (lons, rows, 128)), "lon", 0, 0, tiled=True)
    return full.reshape(SLAB, 128)


def body(fields, upstream, qkv_weight, out_weight, earth_bias):
    lev_msg, lat_msg, diag_msg = pack_first(fields, upstream)
    lev = from_behind(lev_msg, "lev", -1)
    lat = from_behind(lat_msg, "lat", -1)
    diag = from_corner(diag_msg, -1)

    key = jnp.arange(WIN, dtype=jnp.int32)
    target = (key // WW) * OFFS - key % WW + WW - 1
    target = jnp.concatenate([target, jnp.full((KEYS - WIN,), -1000, jnp.int32)])[None, :]
    last_lev = lax.axis_index("lev") == lax.axis_size("lev") - 1
    last_lat = lax.axis_index("lat") == lax.axis_size("lat") - 1
    lev_flag = ((key // 72) == 1) & last_lev
    lat_flag = ((key // WW) % WH >= WH // 2) & last_lat
    region = jnp.stack(
        [2 * lev_flag.astype(F32), 2 * lev_flag.astype(F32) + lat_flag.astype(F32)]
    )
    keys = jnp.concatenate([region, jnp.zeros((2, KEYS - WIN), F32)], axis=1)
    bias_a, bias_b = expand(earth_bias, target, region[:, :, None], keys[:, None, :])

    lon = from_behind(pack_lon(fields, upstream, lev, lat, diag), "lon", -1)
    lines, lon_back, slab = windows(
        fields, upstream, lev, lat, diag, lon,
        qkv_weight[:, 0:C], qkv_weight[:, C : 2 * C], qkv_weight[:, 2 * C :], out_weight,
        bias_a, bias_b, target,
    )
    lon_in = from_behind(lon_back, "lon", 1)
    own, lev_out, lat_out, diag_out = merge(lines, lon_in)
    lev_in = from_behind(lev_out, "lev", 1)
    lat_in = from_behind(lat_out, "lat", 1)
    diag_in = from_corner(diag_out, 1)
    field_grad = place(own, lev_in, lat_in, diag_in)

    samples, levels, rows, cols, _ = fields.shape
    tokens = samples * levels * rows * cols
    for axis in ("lon", "lat", "lev"):
        tokens = tokens * lax.axis_size(axis)
    qkv_grad, out_grad, bias_grad = finish(reduce_slab(slab), 1.0 / math.sqrt(tokens))
    return (field_grad, qkv_grad, out_grad, bias_grad)


def solution(mesh):
    return jax.shard_map(
        body,
        mesh=mesh,
        in_specs=(
            P(None, "lev", "lat", "lon", None),
            P(None, "lev", "lat", "lon", None),
            P(),
            P(),
            P("lev", "lat", None, None),
        ),
        out_specs=(P(None, "lev", "lat", "lon", None), P(), P(), P("lev", "lat", None, None)),
        check_vma=False,
    )
```

time: 773 us -> 110 us (0.14); the launches traced: 762 us -> 110 us
  waiting for transfers between devices: 492 us -> 43.9 us
  local copies, waits for them, and re-layouts: 132 us -> 4.63 us
  matrix products: 50.6 us -> 0 us
  other arithmetic: 38.6 us -> 0.15 us
  Pallas kernels: 0 us -> 24.8 us
  between operations: 14.7 us -> 0.84 us
    psum x2 -> x0, waiting for transfers between devices: 486 us -> none  [the longest x1 245 us: body(): weight_totals = lax.psum((totals[0], totals[1]), ('lon', 'lat', 'lev'))]
    dot_general x24 -> x0, matrix products: 50.6 us -> none  [the longest x2 9.65 us: window_backward(): jnp.einsum('nhqk,nhqd->nhkd', probs_low, grad_att, preferred_element_type...]
    unnamed x20 -> x16, local copies, waits for them, and re-layouts: 34.4 us -> 2.93 us
    dynamic_update_slice x4 -> x0, local copies, waits for them, and re-layouts: 31 us -> none  [body(): lax.scan(per_sample, start, (to_windows(moved_fields), to_windows(moved_u...]
    all_to_all x0 -> x3, waiting for transfers between devices: none -> 25.9 us  [the longest x1 13.3 us: reduce_slab(): lax.all_to_all(jnp.broadcast_to(mine[None], (lons, rows, 128)), 'lon', 0,...]
    another operation x3 -> x0, local copies, waits for them, and re-layouts: 25.5 us -> none
    pallas_call x0 -> x7, Pallas kernels: none -> 24.8 us  [the longest x1 19.6 us: windows(): pl.pallas_call(main_kernel, name='windows', out_shape=(shape((2, 2, 12, 2...]
    ppermute x9 -> x6, starting transfers between devices: 33.5 us -> 9.56 us  [from_behind(): lax.ppermute(x, axis, [(i, (i + by) % devices) for i in range(devices)])]
  transfers between devices with their start and end apart: 11 -> 11, of which waited for: 5 -> 6; matrix products, arithmetic and copies ran while one was open for 12% -> 2% of each run, Pallas kernels for 0% -> 4%
where the time goes in v1:
time: 110 us
  waiting for transfers between devices  43.9 us (40%)
  starting transfers between devices  35.3 us (32%)
  Pallas kernels  24.8 us (23%)
  local copies, waits for them, and re-layouts  4.63 us (4%)
    pallas_call x1, Pallas kernels, windows(): pl.pallas_call(main_kernel, name='windows', out_shape=(shape((2, 2, 12, 2...  19.6 us
    ppermute x6, waiting for transfers between devices, from_behind(): lax.ppermute(x, axis, [(i, (i + by) % devices) for i in range(devices)])  16.1 us
    all_to_all x1, waiting for transfers between devices, reduce_slab(): lax.all_to_all(jnp.broadcast_to(mine[None], (lons, rows, 128)), 'lon', 0,...  13.3 us
    all_to_all x1, starting transfers between devices, reduce_slab(): lax.all_to_all(slab.reshape(lons, rows, 128), 'lon', 0, 0, tiled=True)  11.9 us
    all_to_all x1, waiting for transfers between devices, reduce_slab(): lax.all_to_all(slab.reshape(lons, rows, 128), 'lon', 0, 0, tiled=True)  11.3 us
    ppermute x6, starting transfers between devices, from_behind(): lax.ppermute(x, axis, [(i, (i + by) % devices) for i in range(devices)])  9.56 us
    all_to_all x1, starting transfers between devices, reduce_slab(): lax.all_to_all(jnp.broadcast_to(mine[None], (lons, rows, 128)), 'lon', 0,...  6.8 us
    ppermute x2, starting transfers between devices, from_corner(): return lax.ppermute(x, ('lat', 'lev'), pairs)  3.66 us
  transfers between devices with their start and end apart: 11, of which 6 were waited for; matrix products, arithmetic and copies ran while one was open for 2% of the time, Pallas kernels for 4%

profile of v1, /device:TPU:1, one launch (start us, length us, event | category | flops | bytes accessed | tf_op | source)
XLA Modules:
  0.0 109.6 jit_solution(3728851536269773951)
XLA Ops:
  0.6 0.0 copy-start
  0.6 1.1 copy-done
  1.7 0.0 copy-start.2
  1.7 1.1 copy-done.2
  2.8 0.0 copy-start.6
  2.8 3.4 %collective-permute-start.1 = (bf16[2,2,3,24,192]{4,3,2,1,0:T(8,128)(2,1)S(1)}, bf16[2,2,3,24,192]{4,3,2,1,0:T(8,128)(2,1)S(1)}, u32[]{:S(2)}, u32[]{:S(2)}) collective-permute-start(bf16[2,2,3,24,192]{4,3,2,1,0:T(8,128)(2,1)S(1)} %get-tuple-element.20), channel_id=1, source_target_pairs={{0,6},{2,0},{4,2},{6,4},{1,7},{3,1},{5,3},{7,5},{8,14},{10,8},{12,... | collective-permute-start | bytes 331784 | tf_op jit(solution)/shard_map/ppermute | solution.py:401
  6.2 1.6 %collective-permute-start.2 = (bf16[2,2,3,24,192]{4,3,2,1,0:T(8,128)(2,1)S(1)}, bf16[2,2,3,24,192]{4,3,2,1,0:T(8,128)(2,1)S(1)}, u32[]{:S(2)}, u32[]{:S(2)}) collective-permute-start(bf16[2,2,3,24,192]{4,3,2,1,0:T(8,128)(2,1)S(1)} %get-tuple-element.21), channel_id=1, source_target_pairs={{0,7},{1,6},{2,1},{3,0},{4,3},{5,2},{6,5},{7,4},{8,15},{9,14},{10,... | collective-permute-start | bytes 331784 | tf_op jit(solution)/shard_map/ppermute | solution.py:411
  7.8 0.2 collective-permute-start
  8.0 0.1 copy.13.rq
  8.2 0.0 copy-done.6
  8.2 0.0 copy-start.1
  8.2 0.0 copy-start.3
  8.2 2.9 %expand_bias.1 = (f32[1728,128]{1,0:T(8,128)S(1)}, f32[1728,128]{1,0:T(8,128)S(1)}) custom-call(f32[1,2,6,3312]{3,2,1,0:T(8,128)S(1)} %copy.12.eb, s32[1,256]{1,0:T(1,128)S(1)} %bitcast.6, f32[2,144,1]{2,1,0:T(8,128)S(1)} %copy.13.rq, f32[2,1,256]{2,1,0:T(1,128)S(1)} %broadcast_in_dim.12.rk), custom_call_target="tpu_custom_call" | custom-call | flops 764411904 | bytes 4194304 | tf_op jit(solution)/shard_map/expand_bias/pallas_call | solution.py:145
  11.2 0.0 copy-start.5
  11.2 0.0 copy-start.4
  11.2 0.0 collective-permute-done.1.lat
  11.2 1.8 %collective-permute-done.2.diag = bf16[2,2,3,24,192]{4,3,2,1,0:T(8,128)(2,1)S(1)} collective-permute-done((bf16[2,2,3,24,192]{4,3,2,1,0:T(8,128)(2,1)S(1)}, bf16[2,2,3,24,192]{4,3,2,1,0:T(8,128)(2,1)S(1)}, u32[]{:S(2)}, u32[]{:S(2)}) %collective-permute-start.2) | collective-permute-done | bytes 110624 | tf_op jit(solution)/shard_map/ppermute | solution.py:411
  13.0 9.1 %collective-permute-done.lev = bf16[2,2,9,24,192]{4,3,2,1,0:T(8,128)(2,1)S(1)} collective-permute-done((bf16[2,2,9,24,192]{4,3,2,1,0:T(8,128)(2,1)S(1)}, bf16[2,2,9,24,192]{4,3,2,1,0:T(8,128)(2,1)S(1)}, u32[]{:S(2)}, u32[]{:S(2)}) %collective-permute-start) | collective-permute-done | bytes 331808 | tf_op jit(solution)/shard_map/ppermute | solution.py:401
  22.2 0.0 copy-done.1
  22.2 0.0 copy-done.3
  22.2 0.1 pack_lon.1
  22.3 1.1 collective-permute-start.3
  23.4 0.0 copy-done.5
  23.4 0.1 fusion.8
  23.5 7.0 %collective-permute-done.3.lon = bf16[576,192]{1,0:T(8,128)(2,1)S(1)} collective-permute-done((bf16[576,192]{1,0:T(8,128)(2,1)S(1)}, bf16[576,192]{1,0:T(8,128)(2,1)S(1)}, u32[]{:S(2)}, u32[]{:S(2)}) %collective-permute-start.3) | collective-permute-done | bytes 221216 | tf_op jit(solution)/shard_map/ppermute | solution.py:401
  30.5 0.0 copy-done.4
  30.5 19.6 %windows.1 = (bf16[2,2,12,24,192]{4,3,2,1,0:T(8,128)(2,1)S(1)}, bf16[288,192]{1,0:T(8,128)(2,1)S(1)}, bf16[1536,128]{1,0:T(8,128)(2,1)}) custom-call(bf16[2,2,12,24,192]{4,3,2,1,0:T(8,128)(2,1)S(1)} %copy-done.1, bf16[2,2,12,24,192]{4,3,2,1,0:T(8,128)(2,1)S(1)} %copy-done.3, bf16[2,2,9,24,192]{4,3,2,1,0:T(8,128)(2,1)S(1)} %collective-permute-done.lev, ...), custom_call_target="tpu_custom_call" | custom-call | flops 2000000000 | bytes 8388608 | tf_op jit(solution)/shard_map/windows/pallas_call | solution.py:275
  50.0 11.9 %all-to-all-start = ((bf16[32,48,128]{2,1,0:T(8,128)(2,1)}), bf16[32,48,128]{2,1,0:T(8,128)(2,1)S(1)}, u32[]{:S(2)}, u32[]{:S(2)}) async-start(bf16[32,48,128]{2,1,0:T(8,128)(2,1)} %bitcast.2), calls=%async_computation | async-start | bytes 786432 | tf_op jit(solution)/shard_map/all_to_all | solution.py:418
  61.9 3.2 %collective-permute-start.4 = (bf16[288,192]{1,0:T(8,128)(2,1)S(1)}, bf16[288,192]{1,0:T(8,128)(2,1)S(1)}, u32[]{:S(2)}, u32[]{:S(2)}) collective-permute-start(bf16[288,192]{1,0:T(8,128)(2,1)S(1)} %get-tuple-element.25), channel_id=1, source_target_pairs={{0,8},{8,16},{16,24},{24,32},{32,40},{40,48},{48,56},{56,64},{64,7... | collective-permute-start | bytes 331784 | tf_op jit(solution)/shard_map/ppermute | solution.py:401
  65.1 11.3 %all-to-all-done = bf16[32,48,128]{2,1,0:T(8,128)(2,1)S(1)} async-done(((bf16[32,48,128]{2,1,0:T(8,128)(2,1)}), bf16[32,48,128]{2,1,0:T(8,128)(2,1)S(1)}, u32[]{:S(2)}, u32[]{:S(2)}) %all-to-all-start) | async-done | bytes 393248 | tf_op jit(solution)/shard_map/all_to_all | solution.py:418
  76.5 0.1 reduce_sum.24
  76.5 0.7 broadcast_in_dim.26
  77.2 3.4 %all-to-all-start.1 = ((bf16[8,48,128]{2,1,0:T(8,128)(2,1)}), bf16[8,48,128]{2,1,0:T(8,128)(2,1)S(1)}, u32[]{:S(2)}, u32[]{:S(2)}) async-start(bf16[8,48,128]{2,1,0:T(8,128)(2,1)} %broadcast_in_dim.26), calls=%async_computation.1 | async-start | bytes 196608 | tf_op jit(solution)/shard_map/all_to_all | solution.py:420
  80.6 0.0 collective-permute-done.4.lon_in
  80.6 0.1 merge_lon.1
  80.6 1.4 %collective-permute-start.6 = (bf16[2,3,24,192]{3,2,1,0:T(8,128)(2,1)S(1)}, bf16[2,3,24,192]{3,2,1,0:T(8,128)(2,1)S(1)}, u32[]{:S(2)}, u32[]{:S(2)}) collective-permute-start(bf16[2,3,24,192]{3,2,1,0:T(8,128)(2,1)S(1)} %get-tuple-element.28), channel_id=1, source_target_pairs={{0,2},{2,4},{4,6},{6,0},{1,3},{3,5},{5,7},{7,1},{8,10},{10,12},{12... | collective-permute-start | bytes 165896 | tf_op jit(solution)/shard_map/ppermute | solution.py:401
  82.1 2.1 %collective-permute-start.7 = (bf16[2,3,24,192]{3,2,1,0:T(8,128)(2,1)S(1)}, bf16[2,3,24,192]{3,2,1,0:T(8,128)(2,1)S(1)}, u32[]{:S(2)}, u32[]{:S(2)}) collective-permute-start(bf16[2,3,24,192]{3,2,1,0:T(8,128)(2,1)S(1)} %get-tuple-element.29), channel_id=1, source_target_pairs={{0,3},{1,2},{2,5},{3,4},{4,7},{5,6},{6,1},{7,0},{8,11},{9,10},{10,... | collective-permute-start | bytes 165896 | tf_op jit(solution)/shard_map/ppermute | solution.py:411
  84.2 0.3 collective-permute-start.5
  84.5 1.3 %all-to-all-done.1 = bf16[8,48,128]{2,1,0:T(8,128)(2,1)S(1)} async-done(((bf16[8,48,128]{2,1,0:T(8,128)(2,1)}), bf16[8,48,128]{2,1,0:T(8,128)(2,1)S(1)}, u32[]{:S(2)}, u32[]{:S(2)}) %all-to-all-start.1) | async-done | bytes 98336 | tf_op jit(solution)/shard_map/all_to_all | solution.py:420
  85.8 0.8 broadcast_in_dim.27
  86.6 6.8 %all-to-all-start.2 = ((bf16[32,48,128]{2,1,0:T(8,128)(2,1)}), bf16[32,48,128]{2,1,0:T(8,128)(2,1)S(1)}, u32[]{:S(2)}, u32[]{:S(2)}) async-start(bf16[32,48,128]{2,1,0:T(8,128)(2,1)} %broadcast_in_dim.27), calls=%async_computation.2 | async-start | bytes 786432 | tf_op jit(solution)/shard_map/all_to_all | solution.py:425
  93.4 0.0 collective-permute-done.6.lat
  93.4 0.0 collective-permute-done.7.diag
  93.4 0.0 collective-permute-done.5.lev
  93.4 1.1 place_grad.1
  94.5 13.3 %all-to-all-done.2 = bf16[32,48,128]{2,1,0:T(8,128)(2,1)S(1)} async-done(((bf16[32,48,128]{2,1,0:T(8,128)(2,1)}), bf16[32,48,128]{2,1,0:T(8,128)(2,1)S(1)}, u32[]{:S(2)}, u32[]{:S(2)}) %all-to-all-start.2) | async-done | bytes 393248 | tf_op jit(solution)/shard_map/all_to_all | solution.py:425
  107.8 1.0 finish_params.1
  108.8 0.7 copy.14
  (10 shorter events, 0.2 us)
Async XLA Ops:
  0.6 1.1 copy-start
  1.7 1.1 copy-start.2
  2.8 5.4 %copy-start.6 = (f32[1,2,6,3312]{3,1,2,0:T(2,128)S(1)}, f32[1,2,6,3312]{3,1,2,0:T(2,128)}, u32[]{:S(2)}) copy-start(f32[1,2,6,3312]{3,1,2,0:T(2,128)} %param.9) | copy-start | bytes 476932
  2.8 8.4 %collective-permute-start.1 = (bf16[2,2,3,24,192]{4,3,2,1,0:T(8,128)(2,1)S(1)}, bf16[2,2,3,24,192]{4,3,2,1,0:T(8,128)(2,1)S(1)}, u32[]{:S(2)}, u32[]{:S(2)}) collective-permute-start(bf16[2,2,3,24,192]{4,3,2,1,0:T(8,128)(2,1)S(1)} %get-tuple-element.20), channel_id=1, source_target_pairs={{0,6},{2,0},{4,2},{6,4},{1,7},{3,1},{5,3},{7,5},{8,14},{10,8},{12,... | collective-permute-start | bytes 331784 | tf_op jit(solution)/shard_map/ppermute | solution.py:401
  6.2 6.8 %collective-permute-start.2 = (bf16[2,2,3,24,192]{4,3,2,1,0:T(8,128)(2,1)S(1)}, bf16[2,2,3,24,192]{4,3,2,1,0:T(8,128)(2,1)S(1)}, u32[]{:S(2)}, u32[]{:S(2)}) collective-permute-start(bf16[2,2,3,24,192]{4,3,2,1,0:T(8,128)(2,1)S(1)} %get-tuple-element.21), channel_id=1, source_target_pairs={{0,7},{1,6},{2,1},{3,0},{4,3},{5,2},{6,5},{7,4},{8,15},{9,14},{10,... | collective-permute-start | bytes 331784 | tf_op jit(solution)/shard_map/ppermute | solution.py:411
  7.8 14.4 %collective-permute-start = (bf16[2,2,9,24,192]{4,3,2,1,0:T(8,128)(2,1)S(1)}, bf16[2,2,9,24,192]{4,3,2,1,0:T(8,128)(2,1)S(1)}, u32[]{:S(2)}, u32[]{:S(2)}) collective-permute-start(bf16[2,2,9,24,192]{4,3,2,1,0:T(8,128)(2,1)S(1)} %get-tuple-element.19), channel_id=1, source_target_pairs={{0,1},{1,0},{2,3},{3,2},{4,5},{5,4},{6,7},{7,6},{8,9},{9,8},{10,11... | collective-permute-start | bytes 995336 | tf_op jit(solution)/shard_map/ppermute | solution.py:401
  8.2 14.0 %copy-start.1 = (bf16[2,2,12,24,192]{4,3,2,1,0:T(8,128)(2,1)S(1)}, bf16[2,2,12,24,192]{4,3,2,1,0:T(8,128)(2,1)}, u32[]{:S(2)}) copy-start(bf16[2,2,12,24,192]{4,3,2,1,0:T(8,128)(2,1)} %f.5) | copy-start | bytes 1327108
  8.2 13.9 %copy-start.3 = (bf16[2,2,12,24,192]{4,3,2,1,0:T(8,128)(2,1)S(1)}, bf16[2,2,12,24,192]{4,3,2,1,0:T(8,128)(2,1)}, u32[]{:S(2)}) copy-start(bf16[2,2,12,24,192]{4,3,2,1,0:T(8,128)(2,1)} %u.5) | copy-start | bytes 1327108
  11.2 12.2 %copy-start.5 = (bf16[192,576]{1,0:T(8,128)(2,1)S(1)}, bf16[192,576]{1,0:T(8,128)(2,1)}, u32[]{:S(2)}) copy-start(bf16[192,576]{1,0:T(8,128)(2,1)} %param.7) | copy-start | bytes 663556
  11.2 19.3 %copy-start.4 = (bf16[192,192]{1,0:T(8,128)(2,1)S(1)}, bf16[192,192]{1,0:T(8,128)(2,1)}, u32[]{:S(2)}) copy-start(bf16[192,192]{1,0:T(8,128)(2,1)} %wo.1) | copy-start | bytes 221188
  22.3 8.2 %collective-permute-start.3 = (bf16[576,192]{1,0:T(8,128)(2,1)S(1)}, bf16[576,192]{1,0:T(8,128)(2,1)S(1)}, u32[]{:S(2)}, u32[]{:S(2)}) collective-permute-start(bf16[576,192]{1,0:T(8,128)(2,1)S(1)} %pack_lon.1), channel_id=1, source_target_pairs={{0,248},{8,0},{16,8},{24,16},{32,24},{40,32},{48,40},{56,48},{64,5... | collective-permute-start | bytes 663560 | tf_op jit(solution)/shard_map/ppermute | solution.py:401
  50.0 26.4 %all-to-all-start = ((bf16[32,48,128]{2,1,0:T(8,128)(2,1)}), bf16[32,48,128]{2,1,0:T(8,128)(2,1)S(1)}, u32[]{:S(2)}, u32[]{:S(2)}) async-start(bf16[32,48,128]{2,1,0:T(8,128)(2,1)} %bitcast.2), calls=%async_computation | async-start | bytes 786432 | tf_op jit(solution)/shard_map/all_to_all | solution.py:418
  61.9 18.7 %collective-permute-start.4 = (bf16[288,192]{1,0:T(8,128)(2,1)S(1)}, bf16[288,192]{1,0:T(8,128)(2,1)S(1)}, u32[]{:S(2)}, u32[]{:S(2)}) collective-permute-start(bf16[288,192]{1,0:T(8,128)(2,1)S(1)} %get-tuple-element.25), channel_id=1, source_target_pairs={{0,8},{8,16},{16,24},{24,32},{32,40},{40,48},{48,56},{56,64},{64,7... | collective-permute-start | bytes 331784 | tf_op jit(solution)/shard_map/ppermute | solution.py:401
  77.2 8.6 %all-to-all-start.1 = ((bf16[8,48,128]{2,1,0:T(8,128)(2,1)}), bf16[8,48,128]{2,1,0:T(8,128)(2,1)S(1)}, u32[]{:S(2)}, u32[]{:S(2)}) async-start(bf16[8,48,128]{2,1,0:T(8,128)(2,1)} %broadcast_in_dim.26), calls=%async_computation.1 | async-start | bytes 196608 | tf_op jit(solution)/shard_map/all_to_all | solution.py:420
  80.6 12.7 %collective-permute-start.6 = (bf16[2,3,24,192]{3,2,1,0:T(8,128)(2,1)S(1)}, bf16[2,3,24,192]{3,2,1,0:T(8,128)(2,1)S(1)}, u32[]{:S(2)}, u32[]{:S(2)}) collective-permute-start(bf16[2,3,24,192]{3,2,1,0:T(8,128)(2,1)S(1)} %get-tuple-element.28), channel_id=1, source_target_pairs={{0,2},{2,4},{4,6},{6,0},{1,3},{3,5},{5,7},{7,1},{8,10},{10,12},{12... | collective-permute-start | bytes 165896 | tf_op jit(solution)/shard_map/ppermute | solution.py:401
  82.1 11.3 %collective-permute-start.7 = (bf16[2,3,24,192]{3,2,1,0:T(8,128)(2,1)S(1)}, bf16[2,3,24,192]{3,2,1,0:T(8,128)(2,1)S(1)}, u32[]{:S(2)}, u32[]{:S(2)}) collective-permute-start(bf16[2,3,24,192]{3,2,1,0:T(8,128)(2,1)S(1)} %get-tuple-element.29), channel_id=1, source_target_pairs={{0,3},{1,2},{2,5},{3,4},{4,7},{5,6},{6,1},{7,0},{8,11},{9,10},{10,... | collective-permute-start | bytes 165896 | tf_op jit(solution)/shard_map/ppermute | solution.py:411
  84.2 9.2 %collective-permute-start.5 = (bf16[2,9,24,192]{3,2,1,0:T(8,128)(2,1)S(1)}, bf16[2,9,24,192]{3,2,1,0:T(8,128)(2,1)S(1)}, u32[]{:S(2)}, u32[]{:S(2)}) collective-permute-start(bf16[2,9,24,192]{3,2,1,0:T(8,128)(2,1)S(1)} %get-tuple-element.27), channel_id=1, source_target_pairs={{0,1},{1,0},{2,3},{3,2},{4,5},{5,4},{6,7},{7,6},{8,9},{9,8},{10,11... | collective-permute-start | bytes 497672 | tf_op jit(solution)/shard_map/ppermute | solution.py:401
  86.6 21.2 %all-to-all-start.2 = ((bf16[32,48,128]{2,1,0:T(8,128)(2,1)}), bf16[32,48,128]{2,1,0:T(8,128)(2,1)S(1)}, u32[]{:S(2)}, u32[]{:S(2)}) async-start(bf16[32,48,128]{2,1,0:T(8,128)(2,1)} %broadcast_in_dim.27), calls=%async_computation.2 | async-start | bytes 786432 | tf_op jit(solution)/shard_map/all_to_all | solution.py:425

commit v2 on v1

v2 whole, which is shorter than its diff:
```python
import functools
import math

import jax
import jax.numpy as jnp
from jax import lax
from jax.experimental import pallas as pl
from jax.experimental.pallas import tpu as pltpu
from jax.sharding import PartitionSpec as P

HEADS = 6
WZ = 2
WH = 6
WW = 12
WIN = 144
PAIRS = 3312
C = 192
HD = 32
OFFS = 2 * WW - 1
GROUP = WH * OFFS
LANES = 384
KEYS = 256
NEG_FILL = -1e30
EPS = 1e-05
SCALE = HD**-0.5
SLAB = 1536
SIDE = SLAB // 2
WROWS = 1152
BF = jnp.bfloat16
F32 = jnp.float32
SPREAD = 896
PAIR = 2 * WIN
BOTH = 2 * C
VMEM = pl.BlockSpec(memory_space=pltpu.VMEM)
HBM = pl.BlockSpec(memory_space=pl.ANY)
SMEM = pl.BlockSpec(memory_space=pltpu.SMEM)


def params(mib):
    return pltpu.CompilerParams(vmem_limit_bytes=mib * 1024 * 1024)


def cost(flops, nbytes):
    return pl.CostEstimate(flops=flops, bytes_accessed=nbytes, transcendentals=0)


def dot(a, b, ca=1, cb=0):
    return lax.dot_general(a, b, (((ca,), (cb,)), ((), ())), preferred_element_type=F32)


def shape(dims, dtype):
    return jax.ShapeDtypeStruct(dims, dtype)


def join(a, b):
    return jnp.concatenate([a[:, 0:128], b[:, 0:128], a[:, 128:C], b[:, 128:C]], axis=1)


def split(m):
    return (
        jnp.concatenate([m[:, 0:128], m[:, 256:320]], axis=1),
        jnp.concatenate([m[:, 128:256], m[:, 320:384]], axis=1),
    )


def pack_near_kernel(f, u, near):
    for b in range(2):
        for h in range(6):
            near[b, h] = join(f[b, 0, h + 3], u[b, 0, h + 3])


def pack_near(fields, upstream):
    return pl.pallas_call(
        pack_near_kernel,
        name="pack_near",
        out_shape=shape((2, 6, 24, BOTH), BF),
        in_specs=[VMEM] * 2,
        out_specs=VMEM,
        compiler_params=params(16),
        cost_estimate=cost(0, 2 * 1024 * 1024),
    )(fields, upstream)


def pack_rest_kernel(f, u, far, lat, diag):
    for b in range(2):
        for r in range(3):
            far[b, r] = join(f[b, 0, r + 9], u[b, 0, r + 9])
            lat[b, r] = join(f[b, 1, r], u[b, 1, r])
            diag[b, r] = join(f[b, 0, r], u[b, 0, r])


def pack_rest(fields, upstream):
    return pl.pallas_call(
        pack_rest_kernel,
        name="pack_rest",
        out_shape=(shape((2, 3, 24, BOTH), BF),) * 3,
        in_specs=[VMEM] * 2,
        out_specs=(VMEM,) * 3,
        compiler_params=params(16),
        cost_estimate=cost(0, 2 * 1024 * 1024),
    )(fields, upstream)


def source_lines(own, halos, aw, b, z, h):
    if z == 0 and (aw == 0 or h < 3):
        return [a[b, 1, 6 * aw + h + 3].astype(F32) for a in own]
    if aw == 0:
        line = halos[0][b, h]
    elif z == 0:
        line = halos[2][b, h - 3]
    else:
        line = halos[1][b, h] if h < 3 else halos[3][b, h - 3]
    return split(line.astype(F32))


def pack_lon_kernel(f, u, near, far, lat, diag, out, tmp):
    for b in range(2):
        for z in range(2):
            for r in range(12):
                lines = source_lines((f, u), (near, far, lat, diag), r // 6, b, z, r % 6)
                row = b * WIN + (z * 12 + r) * 6
                tmp[row : row + 6, :] = join(lines[0][0:6], lines[1][0:6])
    out[...] = tmp[...].astype(BF)


def pack_lon(fields, upstream, halos):
    return pl.pallas_call(
        pack_lon_kernel,
        name="pack_lon",
        out_shape=shape((2 * WIN, BOTH), BF),
        in_specs=[VMEM] * 6,
        out_specs=VMEM,
        scratch_shapes=[pltpu.VMEM((2 * WIN, BOTH), F32)],
        compiler_params=params(16),
        cost_estimate=cost(0, 2 * 1024 * 1024),
    )(fields, upstream, *halos)


def onehot_rows(target, w1):
    lane = lax.broadcasted_iota(jnp.int32, (LANES, KEYS), 0)
    return jnp.where(lane == target + w1, 1.0, 0.0).astype(BF)


def expand_kernel(eb, target, rq, rk, out0, out1, spread, out_a, out_b):
    spread[...] = jnp.zeros_like(spread)
    for z1 in range(2):
        for h1 in range(6):
            g = z1 * 6 + h1
            for z2 in range(2):
                off = ((z1 * 2 + z2) * 6 + h1) * GROUP
                for aw in range(2):
                    spread[g * 16 + aw * 6 : g * 16 + aw * 6 + 6, z2 * GROUP : (z2 + 1) * GROUP] = eb[
                        0, aw, :, off : off + GROUP
                    ]
    full = spread[...]
    high = full.astype(BF)
    rest = full - high.astype(F32)
    mid = rest.astype(BF)
    low = (rest - mid.astype(F32)).astype(BF)
    row = lax.broadcasted_iota(jnp.int32, (12, 1), 0)
    tgt = target[...]
    for w1 in range(WW):
        hot = onehot_rows(tgt, w1)
        block = dot(high, hot) + (dot(mid, hot) + dot(low, hot))
        for g in range(12):
            q = g * 12 + w1
            part = block[g * 16 : g * 16 + 12]
            ok0 = rq[0, q : q + 1, :] == rk[0]
            ok1 = rq[1, q : q + 1, :] == rk[1]
            ok = ((row < 6) & ok0) | ((row >= 6) & ok1)
            part = jnp.where(ok, part, NEG_FILL)
            out_a[pl.ds(q, 12, stride=WIN), :] = part[:, 0:128]
            out_b[pl.ds(q, 12, stride=WIN), :] = part[:, 128:256]
    for aw, out in enumerate((out0, out1)):
        heads = []
        for h in range(HEADS):
            rows = slice((aw * HEADS + h) * WIN, (aw * HEADS + h + 1) * WIN)
            heads.append(jnp.concatenate([out_a[rows, :], out_b[rows, 0:16]], axis=1).T)
        heads.append(jnp.zeros((WIN, SPREAD - HEADS * WIN), F32))
        out[...] = jnp.concatenate(heads, axis=1)


def expand(earth_bias, target, rq, rk):
    return pl.pallas_call(
        expand_kernel,
        name="expand_bias",
        out_shape=(shape((WIN, SPREAD), F32),) * 2,
        in_specs=[VMEM] * 4,
        out_specs=(VMEM,) * 2,
        scratch_shapes=[
            pltpu.VMEM((192, LANES), F32),
            pltpu.VMEM((12 * WIN, 128), F32),
            pltpu.VMEM((12 * WIN, 128), F32),
        ],
        compiler_params=params(16),
        cost_estimate=cost(4 * 10**9, 4 * 1024 * 1024),
    )(earth_bias, target, rq, rk)


def windows_kernel(aws, second, *refs):
    refs = list(refs)
    take = lambda n: [refs.pop(0) for _ in range(n)]
    f, u, wq, wk, wv, wo = take(6)
    biases = dict(zip(aws, take(len(aws))))
    near = take(1) if 0 in aws else [None]
    halos = near + (take(3) if 1 in aws else [])
    if second:
        (lon,) = take(1)
    started = second or 1 in aws
    if started:
        (w_in,) = take(1)
    if second:
        gb_in = take(len(aws))
    grads, w_s = take(2)
    gbs = dict(zip(aws, take(len(aws))))
    if second:
        (lon_back,) = take(1)
    x_s, u_s, i_s, low_s, q_s, k_s, v_s, ga_s, gq_s = take(9)
    if second:
        g_s, lon_s = take(2)
    w_s[...] = w_in[...] if started else jnp.zeros_like(w_s)
    for n, aw in enumerate(aws):
        gbs[aw][...] = gb_in[n][...] if second else jnp.zeros_like(gbs[aw])

    for n, aw in enumerate(aws):
        for b in range(2):
            if second:
                halo = split(lon[b * WIN : (b + 1) * WIN, :].astype(F32))
            for z in range(2):
                for h in range(6):
                    lines = source_lines((f, u), halos, aw, b, z, h)
                    row = (n * 2 + b) * WIN + z * 72 + h * 12
                    hrow = (z * 12 + aw * 6 + h) * 6
                    for t, dst in enumerate((x_s, u_s)):
                        if second:
                            dst[row : row + 6, :] = lines[t][18:24]
                            dst[row + 6 : row + 12, :] = halo[t][hrow : hrow + 6]
                        else:
                            dst[row : row + 12, :] = lines[t][6:18]

    raw = x_s[...]
    centred = raw - jnp.mean(raw, axis=-1, keepdims=True)
    inv_std = lax.rsqrt(jnp.mean(centred * centred, axis=-1, keepdims=True) + EPS)
    normed = centred * inv_std
    low = normed.astype(BF)
    x_s[...] = normed
    i_s[...] = inv_std
    low_s[...] = low
    q_s[...] = dot(low, wq[...]).astype(BF)
    k_s[...] = dot(low, wk[...]).astype(BF)
    v_s[...] = dot(low, wv[...]).astype(BF)
    ga_s[...] = dot(u_s[...].astype(BF), wo[...], 1, 1).astype(BF)

    lane = lax.broadcasted_iota(jnp.int32, (1, C), 1)
    picks = [
        jnp.where((lane >= h * HD) & (lane < (h + 1) * HD), 1.0, 0.0).astype(BF)
        for h in range(HEADS)
    ]

    def stack(a):
        pad = jnp.zeros((SPREAD - HEADS * WIN, C), BF)
        return jnp.concatenate([a * m for m in picks] + [pad], axis=0)

    def unstack(a):
        return jnp.concatenate(
            [a[h * HD : (h + 1) * HD, h * WIN : (h + 1) * WIN] for h in range(HEADS)], axis=0
        )

    for w in range(2 * len(aws)):
        rows = slice(w * WIN, (w + 1) * WIN)
        bias, gb_s = biases[aws[w // 2]], gbs[aws[w // 2]]
        low, q, k, v, ga = low_s[rows, :], q_s[rows, :], k_s[rows, :], v_s[rows, :], ga_s[rows, :]
        up = u_s[rows, :].astype(BF)
        qs = stack(q)
        gas = stack(ga)
        scores = dot(k, qs, 1, 1)
        grad_probs = dot(v, gas, 1, 1)
        probs, grads_low = [], []
        for i in range(SPREAD // 128):
            cols = slice(i * 128, (i + 1) * 128)
            s = scores[:, cols] * SCALE + bias[:, cols]
            e = jnp.exp(s - jnp.max(s, axis=0, keepdims=True))
            p = e * (1.0 / jnp.sum(e, axis=0, keepdims=True))
            gp = grad_probs[:, cols]
            gs = p * (gp - jnp.sum(p * gp, axis=0, keepdims=True))
            gb_s[:, cols] += gs
            probs.append(p.astype(BF))
            grads_low.append(gs.astype(BF))
        p = jnp.concatenate(probs, axis=1)
        gs = jnp.concatenate(grads_low, axis=1)
        gv = dot(p, gas).astype(BF)
        gk = (dot(gs, qs) * SCALE).astype(BF)
        att_t = unstack(dot(v, p, 0, 0)).astype(BF)
        gq_t = (unstack(dot(k, gs, 0, 0)) * SCALE).astype(BF)
        w_s[0:C, :] += dot(gq_t, low)
        w_s[C : 2 * C, :] += dot(low, gk, 0, 0)
        w_s[2 * C : 3 * C, :] += dot(low, gv, 0, 0)
        w_s[3 * C : 4 * C, :] += dot(att_t, up)
        gq_s[rows, :] = (
            dot(gq_t, wq[...], 0, 1) + dot(gk, wk[...], 1, 1) + dot(gv, wv[...], 1, 1)
        )

    gu = gq_s[...]
    normed = x_s[...]
    centre = jnp.mean(gu, axis=-1, keepdims=True)
    along = jnp.mean(gu * normed, axis=-1, keepdims=True)
    grad = i_s[...] * (gu - centre - normed * along)
    grads[...] = grad.astype(BF)
    if not second:
        return

    g_s[...] = grad
    for b in range(2):
        for z in range(2):
            for r in range(12):
                row = ((r // 6) * 2 + b) * WIN + z * 72 + (r % 6) * 12
                to = b * WIN + (z * 12 + r) * 6
                lon_s[to : to + 6, :] = g_s[row + 6 : row + 12, :]
    lon_back[...] = lon_s[...].astype(BF)


def fold_kernel(w, gb0, gb1, target, core, keep, send, w_s, turned, slab):
    w_s[C:, :] = w[C:, :]
    w_s[0:C, :] = w[0:C, :].T
    slab[0:768, :] = w_s[:, 0:128].astype(BF)
    slab[768:1152, :] = jnp.concatenate([w_s[0:384, 128:192], w_s[384:768, 128:192]], axis=1).astype(BF)
    for z2 in range(2):
        for aw, gb in enumerate((gb0, gb1)):
            for h in range(HEADS):
                at = ((z2 * 2 + aw) * HEADS + h) * WIN
                rows = slice(z2 * 72, z2 * 72 + 72)
                turned[at : at + WIN, 0:72] = gb[rows, h * WIN : (h + 1) * WIN].T
    folded = jnp.zeros((288, KEYS), F32)
    tgt = target[...]
    lane = lax.broadcasted_iota(jnp.int32, (KEYS, 72), 0)
    for w1 in range(WW):
        rows = [turned[pl.ds(g * 12 + w1, 24, stride=WIN), :] for g in range(12)]
        full = jnp.concatenate(rows, axis=0)[:, 0:72].astype(BF)
        hot = jnp.where(lane == tgt[:, 0:72] + w1, 1.0, 0.0).astype(BF)
        folded = folded + dot(full, hot, 1, 1)
    slab[1152:1440, :] = folded[:, 0:128].astype(BF)
    rest = [folded[24 * i : 24 * i + 24, 128:138] for i in range(12)]
    rest = jnp.concatenate(rest + [jnp.zeros((24, 8), F32)], axis=1)
    slab[1440:1536, :] = jnp.concatenate([rest, jnp.zeros((72, 128), F32)], axis=0).astype(BF)
    top = pl.multiple_of(core[0, 0] * SIDE, SIDE)
    keep[...] = slab[pl.ds(top, SIDE), :]
    send[...] = slab[pl.ds(SIDE - top, SIDE), :]


def fold(w, gb0, gb1, target, core):
    return pl.pallas_call(
        fold_kernel,
        name="fold",
        out_shape=(shape((SIDE, 128), BF),) * 2,
        in_specs=[VMEM] * 4 + [SMEM],
        out_specs=(VMEM,) * 2,
        scratch_shapes=[
            pltpu.VMEM((4 * C, C), F32),
            pltpu.VMEM((24 * WIN, 128), F32),
            pltpu.VMEM((SLAB, 128), BF),
        ],
        compiler_params=params(24),
        cost_estimate=cost(2 * 10**9, 4 * 1024 * 1024),
    )(w, gb0, gb1, target, core)


def windows(aws, second, *args):
    tokens = len(aws) * PAIR
    rows = [pltpu.VMEM((tokens, C), F32)] * 2 + [pltpu.VMEM((tokens, 1), F32)]
    rows += [pltpu.VMEM((tokens, C), BF)] * 5 + [pltpu.VMEM((tokens, C), F32)]
    outs = (shape((tokens, C), BF), shape((4 * C, C), F32))
    outs += (shape((WIN, SPREAD), F32),) * len(aws)
    if second:
        outs += (shape((2 * WIN, C), BF),)
        rows += [pltpu.VMEM((tokens, C), F32), pltpu.VMEM((2 * WIN, C), F32)]
    return pl.pallas_call(
        functools.partial(windows_kernel, aws, second),
        name="windows_second" if second else "windows_upper" if 1 in aws else "windows_lower",
        out_shape=outs,
        in_specs=[VMEM] * len(args),
        out_specs=(VMEM,) * len(outs),
        scratch_shapes=rows,
        compiler_params=params(28),
        cost_estimate=cost(3 * 10**9 * len(aws), 4 * 1024 * 1024),
    )(*args)


def merge_kernel(g_lower, g_upper, g_second, lon_in, own, lev, lat, diag):
    for b in range(2):
        halo = lon_in[b * WIN : (b + 1) * WIN, :].astype(F32)
        for aw, g_first in enumerate((g_lower, g_upper)):
            first = g_first[b * WIN : (b + 1) * WIN, :].astype(F32)
            second = g_second[(aw * 2 + b) * WIN : (aw * 2 + b + 1) * WIN, :].astype(F32)
            for z in range(2):
                for h in range(6):
                    r = aw * 6 + h
                    off = z * 72 + h * 12
                    hrow = (z * 12 + r) * 6
                    line = jnp.concatenate(
                        [halo[hrow : hrow + 6], first[off : off + 12], second[off : off + 6]], axis=0
                    ).astype(BF)
                    if z == 0:
                        if r < 9:
                            own[b, r] = line
                        else:
                            lat[b, r - 9] = line
                    elif r < 9:
                        lev[b, r] = line
                    else:
                        diag[b, r - 9] = line


def merge(*args):
    return pl.pallas_call(
        merge_kernel,
        name="merge_lon",
        out_shape=(
            shape((2, 9, 24, C), BF),
            shape((2, 9, 24, C), BF),
            shape((2, 3, 24, C), BF),
            shape((2, 3, 24, C), BF),
        ),
        in_specs=[VMEM] * 4,
        out_specs=(VMEM,) * 4,
        compiler_params=params(16),
        cost_estimate=cost(2 * 10**10, 2 * 1024 * 1024),
    )(*args)


def place_kernel(own, lev, lat, diag, out):
    for b in range(2):
        out[b, 1, 3:12] = own[b].astype(F32)
        out[b, 1, 0:3] = lat[b].astype(F32)
        out[b, 0, 3:12] = lev[b].astype(F32)
        out[b, 0, 0:3] = diag[b].astype(F32)


def place(own, lev, lat, diag):
    return pl.pallas_call(
        place_kernel,
        name="place_grad",
        out_shape=shape((2, 2, 12, 24, C), F32),
        in_specs=[VMEM] * 4,
        out_specs=VMEM,
        compiler_params=params(16),
        cost_estimate=cost(2 * 10**10, 2 * 1024 * 1024),
    )(own, lev, lat, diag)


def finish_kernel(factor, half, other, core, qkv, out, bias, slab):
    top = pl.multiple_of(core[0, 0] * SIDE, SIDE)
    slab[pl.ds(top, SIDE), :] = half[...].astype(F32)
    slab[pl.ds(SIDE - top, SIDE), :] = other[...].astype(F32)
    full = slab[...]
    right = full[768:1152]
    rest = jnp.concatenate([right[:, 0:64], right[:, 64:128]], axis=0)
    whole = jnp.concatenate([full[0:768], rest], axis=1) * factor
    for j in range(3):
        qkv[:, j * C : (j + 1) * C] = whole[j * C : (j + 1) * C]
    out[...] = whole[3 * C : 4 * C]
    tail = full[1440:1464]
    tail = jnp.concatenate([tail[:, 10 * i : 10 * i + 10] for i in range(12)], axis=0)
    pairs = jnp.concatenate([full[1152:1440], tail], axis=1)
    for z1 in range(2):
        for h1 in range(6):
            for z2 in range(2):
                off = ((z1 * 2 + z2) * 6 + h1) * GROUP
                for aw in range(2):
                    at = (z1 * 6 + h1) * 24 + z2 * 12 + aw * 6
                    bias[0, aw, :, off : off + GROUP] = pairs[at : at + 6]


def finish(half, other, core, factor):
    return pl.pallas_call(
        functools.partial(finish_kernel, factor),
        name="finish_params",
        out_shape=(
            shape((C, 3 * C), F32),
            shape((C, C), F32),
            shape((1, 2, HEADS, PAIRS), F32),
        ),
        in_specs=[VMEM, VMEM, SMEM],
        out_specs=(VMEM,) * 3,
        scratch_shapes=[pltpu.VMEM((SLAB, 128), F32)],
        compiler_params=params(16),
        cost_estimate=cost(0, 2 * 1024 * 1024),
    )(half, other, core)


def from_behind(x, axis, by):
    devices = lax.axis_size(axis)
    return lax.ppermute(x, axis, [(i, (i + by) % devices) for i in range(devices)])


def from_corner(x, by):
    lats, levs = lax.axis_size("lat"), lax.axis_size("lev")
    pairs = [
        (a * levs + v, ((a + by) % lats) * levs + (v + by) % levs)
        for a in range(lats)
        for v in range(levs)
    ]
    return lax.ppermute(x, ("lat", "lev"), pairs)


def other_core(x):
    return lax.ppermute(x, "lon", [(i, i ^ 1) for i in range(lax.axis_size("lon"))])


def reduce_slab(keep, send):
    lons, lats, levs = (lax.axis_size(a) for a in ("lon", "lat", "lev"))
    depth = lons // 4
    rows = SIDE // depth
    along = [[4 * z + low for z in range(depth)] for low in range(4)]
    plane = [
        [((4 * z + 2 * y + c) * lats + a) * levs + v for y in range(2) for a in range(lats) for v in range(levs)]
        for z in range(depth)
        for c in range(2)
    ]
    half = (keep.astype(F32) + other_core(send).astype(F32)).astype(BF)
    pieces = lax.all_to_all(
        half.reshape(depth, rows, 128), "lon", 0, 0, axis_index_groups=along, tiled=True
    )
    mine = jnp.sum(pieces.astype(F32), axis=0).astype(BF)
    count = 2 * lats * levs
    every = lax.all_to_all(
        jnp.broadcast_to(mine[None], (count, rows, 128)),
        ("lon", "lat", "lev"), 0, 0, axis_index_groups=plane, tiled=True,
    )
    lon = lax.axis_index("lon")
    first = (lon % 2) * SIDE + (lon // 4) * rows
    spot = jnp.arange(count, dtype=jnp.int32) % (lats * levs)
    same = spot == lax.axis_index("lat") * levs + lax.axis_index("lev")
    picked = jnp.where(same | (first < WROWS), 1.0, 0.0).astype(F32)
    mine = jnp.sum(every.astype(F32) * picked[:, None, None], axis=0).astype(BF)
    half = lax.all_to_all(
        jnp.broadcast_to(mine[None], (depth, rows, 128)), "lon", 0, 0, axis_index_groups=along, tiled=True
    ).reshape(SIDE, 128)
    return half, other_core(half)


def body(fields, upstream, qkv_weight, out_weight, earth_bias):
    near = from_behind(pack_near(fields, upstream), "lev", -1)
    far_msg, lat_msg, diag_msg = pack_rest(fields, upstream)
    far = from_behind(far_msg, "lev", -1)
    lat = from_behind(lat_msg, "lat", -1)
    diag = from_corner(diag_msg, -1)

    key = jnp.arange(WIN, dtype=jnp.int32)
    target = (key // WW) * OFFS - key % WW + WW - 1
    target = jnp.concatenate([target, jnp.full((KEYS - WIN,), -1000, jnp.int32)])[None, :]
    last_lev = lax.axis_index("lev") == lax.axis_size("lev") - 1
    last_lat = lax.axis_index("lat") == lax.axis_size("lat") - 1
    lev_flag = ((key // 72) == 1) & last_lev
    lat_flag = ((key // WW) % WH >= WH // 2) & last_lat
    region = jnp.stack(
        [2 * lev_flag.astype(F32), 2 * lev_flag.astype(F32) + lat_flag.astype(F32)]
    )
    keys = jnp.concatenate([region, jnp.zeros((2, KEYS - WIN), F32)], axis=1)
    bias0, bias1 = expand(earth_bias, target, region[:, :, None], keys[:, None, :])
    core = (lax.axis_index("lon") % 2).astype(jnp.int32).reshape(1, 1)

    shared = (
        fields, upstream,
        qkv_weight[:, 0:C], qkv_weight[:, C : 2 * C], qkv_weight[:, 2 * C :], out_weight,
    )
    g_lower, w, gb0 = windows((0,), False, *shared, bias0, near)
    rest = (far, lat, diag)
    lon = from_behind(pack_lon(fields, upstream, (near,) + rest), "lon", -1)
    g_upper, w, gb1 = windows((1,), False, *shared, bias1, *rest, w)
    g_second, w, gb0, gb1, lon_back = windows(
        (0, 1), True, *shared, bias0, bias1, near, *rest, lon, w, gb0, gb1
    )
    keep, send = fold(w, gb0, gb1, target, core)
    half, other = reduce_slab(keep, send)
    lon_in = from_behind(lon_back, "lon", 1)
    own, lev_out, lat_out, diag_out = merge(g_lower, g_upper, g_second, lon_in)
    lev_in = from_behind(lev_out, "lev", 1)
    lat_in = from_behind(lat_out, "lat", 1)
    diag_in = from_corner(diag_out, 1)
    field_grad = place(own, lev_in, lat_in, diag_in)

    samples, levels, rows, cols, _ = fields.shape
    tokens = samples * levels * rows * cols
    for axis in ("lon", "lat", "lev"):
        tokens = tokens * lax.axis_size(axis)
    qkv_grad, out_grad, bias_grad = finish(half, other, core, 1.0 / math.sqrt(tokens))
    return (field_grad, qkv_grad, out_grad, bias_grad)


def solution(mesh):
    return jax.shard_map(
        body,
        mesh=mesh,
        in_specs=(
            P(None, "lev", "lat", "lon", None),
            P(None, "lev", "lat", "lon", None),
            P(),
            P(),
            P("lev", "lat", None, None),
        ),
        out_specs=(P(None, "lev", "lat", "lon", None), P(), P(), P("lev", "lat", None, None)),
        check_vma=False,
    )
```

time: 110 us -> 86.9 us (0.79)
  waiting for transfers between devices: 43.9 us -> 12.8 us
  blocking collectives: 0 us -> 12.3 us
  Pallas kernels: 24.8 us -> 20.2 us
    ppermute x6 -> x7, waiting for transfers between devices: 16.1 us -> 0.28 us  [from_behind(): lax.ppermute(x, axis, [(i, (i + by) % devices) for i in range(devices)])]
    all_to_all x3 -> x2, waiting for transfers between devices: 25.9 us -> 11.4 us  [the longest x1 8.03 us: reduce_slab(): lax.all_to_all(jnp.broadcast_to(mine[None], (depth, rows, 128)), 'lon', 0...]
    all_to_all x0 -> x1, blocking collectives: none -> 12.3 us  [reduce_slab(): lax.all_to_all(half.reshape(depth, rows, 128), 'lon', 0, 0, axis_index_gr...]
    all_to_all x3 -> x2, starting transfers between devices: 22 us -> 10.5 us  [the longest x1 6.12 us: reduce_slab(): lax.all_to_all(jnp.broadcast_to(mine[None], (count, rows, 128)), ('lon',...]
    ppermute x0 -> x2, starting transfers between devices: none -> 10 us  [other_core(): lax.ppermute(x, 'lon', [(i, i ^ 1) for i in range(lax.axis_size('lon'))])]
    pallas_call x4 -> x8, Pallas kernels: 22.6 us -> 17.8 us  [the longest x3 11.4 us: windows(): pl.pallas_call(functools.partial(windows_kernel, aws, second), name='wind...]
    ppermute x6 -> x7, starting transfers between devices: 9.56 us -> 12.1 us  [from_behind(): lax.ppermute(x, axis, [(i, (i + by) % devices) for i in range(devices)])]
    ppermute x2, waiting for transfers between devices: 1.82 us -> 0.01 us  [from_corner(): return lax.ppermute(x, ('lat', 'lev'), pairs)]
  transfers between devices with their start and end apart: 11 -> 13, of which waited for: 6 -> 4; matrix products, arithmetic and copies ran while one was open for 2% -> 1% of each run, Pallas kernels for 4% -> 13%
where the time goes in v2:
time: 86.9 us; the launch traced here: 86.5 us
  starting transfers between devices  34.4 us (40%)
  Pallas kernels  20.2 us (23%)
  waiting for transfers between devices  12.8 us (15%)
  blocking collectives  12.3 us (14%)
  local copies, waits for them, and re-layouts  5.47 us (6%)
  between operations  0.99 us (1%)
    all_to_all x1, blocking collectives, reduce_slab(): lax.all_to_all(half.reshape(depth, rows, 128), 'lon', 0, 0, axis_index_gr...  12.3 us
    ppermute x7, starting transfers between devices, from_behind(): lax.ppermute(x, axis, [(i, (i + by) % devices) for i in range(devices)])  12.1 us
    pallas_call x3, Pallas kernels, windows(): pl.pallas_call(functools.partial(windows_kernel, aws, second), name='wind...  11.4 us
    ppermute x2, starting transfers between devices, other_core(): lax.ppermute(x, 'lon', [(i, i ^ 1) for i in range(lax.axis_size('lon'))])  10 us
    all_to_all x1, waiting for transfers between devices, reduce_slab(): lax.all_to_all(jnp.broadcast_to(mine[None], (depth, rows, 128)), 'lon', 0...  8.03 us
    all_to_all x1, starting transfers between devices, reduce_slab(): lax.all_to_all(jnp.broadcast_to(mine[None], (count, rows, 128)), ('lon',...  6.12 us
    all_to_all x1, starting transfers between devices, reduce_slab(): lax.all_to_all(jnp.broadcast_to(mine[None], (depth, rows, 128)), 'lon', 0...  4.33 us
    pallas_call x1, Pallas kernels, expand(): pl.pallas_call(expand_kernel, name='expand_bias', out_shape=(shape((WIN,...  4 us
  transfers between devices with their start and end apart: 13, of which 4 were waited for; matrix products, arithmetic and copies ran while one was open for 1% of the time, Pallas kernels for 13%

profile of v2, /device:TPU:1, one launch (start us, length us, event | category | flops | bytes accessed | tf_op | source)
XLA Modules:
  0.0 86.5 jit_solution(18302502229015118262)
XLA Ops:
  0.6 0.0 copy-start
  0.6 1.1 %copy-done = bf16[2,2,12,24,192]{4,3,2,1,0:T(8,128)(2,1)S(1)} copy-done((bf16[2,2,12,24,192]{4,3,2,1,0:T(8,128)(2,1)S(1)}, bf16[2,2,12,24,192]{4,3,2,1,0:T(8,128)(2,1)}, u32[]{:S(2)}) %copy-start) | copy-done | bytes 442392
  1.7 1.1 %copy-done.2 = bf16[2,2,12,24,192]{4,3,2,1,0:T(8,128)(2,1)S(1)} copy-done((bf16[2,2,12,24,192]{4,3,2,1,0:T(8,128)(2,1)S(1)}, bf16[2,2,12,24,192]{4,3,2,1,0:T(8,128)(2,1)}, u32[]{:S(2)}) %copy-start.2) | copy-done | bytes 442392
  2.8 0.1 pack_near.1
  2.9 2.2 %collective-permute-start = (bf16[2,6,24,384]{3,2,1,0:T(8,128)(2,1)S(1)}, bf16[2,6,24,384]{3,2,1,0:T(8,128)(2,1)S(1)}, u32[]{:S(2)}, u32[]{:S(2)}) collective-permute-start(bf16[2,6,24,384]{3,2,1,0:T(8,128)(2,1)S(1)} %pack_near.1), channel_id=1, source_target_pairs={{0,1},{1,0},{2,3},{3,2},{4,5},{5,4},{6,7},{7,6},{8,9},{9,8},{10,11... | collective-permute-start | bytes 663560 | tf_op jit(solution)/shard_map/ppermute | solution.py:492
  5.1 0.1 pack_rest.1
  5.2 0.1 collective-permute-start.1
  5.3 2.6 %collective-permute-start.2 = (bf16[2,3,24,384]{3,2,1,0:T(8,128)(2,1)S(1)}, bf16[2,3,24,384]{3,2,1,0:T(8,128)(2,1)S(1)}, u32[]{:S(2)}, u32[]{:S(2)}) collective-permute-start(bf16[2,3,24,384]{3,2,1,0:T(8,128)(2,1)S(1)} %get-tuple-element.33), channel_id=1, source_target_pairs={{0,6},{2,0},{4,2},{6,4},{1,7},{3,1},{5,3},{7,5},{8,14},{10,8},{12,... | collective-permute-start | bytes 331784 | tf_op jit(solution)/shard_map/ppermute | solution.py:492
  7.9 1.6 %collective-permute-start.3 = (bf16[2,3,24,384]{3,2,1,0:T(8,128)(2,1)S(1)}, bf16[2,3,24,384]{3,2,1,0:T(8,128)(2,1)S(1)}, u32[]{:S(2)}, u32[]{:S(2)}) collective-permute-start(bf16[2,3,24,384]{3,2,1,0:T(8,128)(2,1)S(1)} %get-tuple-element.34), channel_id=1, source_target_pairs={{0,7},{1,6},{2,1},{3,0},{4,3},{5,2},{6,5},{7,4},{8,15},{9,14},{10,... | collective-permute-start | bytes 331784 | tf_op jit(solution)/shard_map/ppermute | solution.py:502
  9.6 0.1 copy.13.rq
  9.8 0.0 copy-start.9
  9.8 0.0 copy-start.1
  9.8 0.0 copy-start.3
  9.8 4.0 %expand_bias.1 = (f32[144,896]{1,0:T(8,128)S(1)}, f32[144,896]{1,0:T(8,128)S(1)}) custom-call(f32[1,2,6,3312]{3,2,1,0:T(8,128)S(1)} %copy.12.eb, s32[1,256]{1,0:T(1,128)S(1)} %bitcast.8, f32[2,144,1]{2,1,0:T(8,128)S(1)} %copy.13.rq, f32[2,1,256]{2,1,0:T(1,128)S(1)} %broadcast_in_dim.34.rk), custom_call_target="tpu_custom_call" | custom-call | flops 4000000000 | bytes 4194304 | tf_op jit(solution)/shard_map/expand_bias/pallas_call | solution.py:184
  13.8 0.0 copy-start.5
  13.9 0.8 copy-done.5
  14.6 0.1 fusion.8
  14.7 0.0 copy-start.6
  14.8 0.0 collective-permute-done.2.refs_8_.lat.refs_10_
  14.8 0.2 pack_lon.1
  15.0 2.1 %collective-permute-start.4 = (bf16[288,384]{1,0:T(8,128)(2,1)S(1)}, bf16[288,384]{1,0:T(8,128)(2,1)S(1)}, u32[]{:S(2)}, u32[]{:S(2)}) collective-permute-start(bf16[288,384]{1,0:T(8,128)(2,1)S(1)} %pack_lon.1), channel_id=1, source_target_pairs={{0,248},{8,0},{16,8},{24,16},{32,24},{40,32},{48,40},{56,48},{64,5... | collective-permute-start | bytes 663560 | tf_op jit(solution)/shard_map/ppermute | solution.py:492
  17.1 2.9 %windows_lower.1 = (bf16[288,192]{1,0:T(8,128)(2,1)S(1)}, f32[768,192]{1,0:T(8,128)S(1)}, f32[144,896]{1,0:T(8,128)S(1)}) custom-call(bf16[2,2,12,24,192]{4,3,2,1,0:T(8,128)(2,1)S(1)} %copy-done.1, bf16[2,2,12,24,192]{4,3,2,1,0:T(8,128)(2,1)S(1)} %copy-done.3, bf16[192,192]{1,0:T(8,128)(2,1)S(1)} %get-tuple-element.63.refs_2_, ...), custom_call_target="tpu_custom_call" | custom-call | flops 3000000000 | bytes 4194304 | tf_op jit(solution)/shard_map/windows_lower/pallas_call | solution.py:376
  20.0 3.0 %windows_upper.1 = (bf16[288,192]{1,0:T(8,128)(2,1)S(1)}, f32[768,192]{1,0:T(8,128)S(1)}, f32[144,896]{1,0:T(8,128)S(1)}) custom-call(bf16[2,2,12,24,192]{4,3,2,1,0:T(8,128)(2,1)S(1)} %copy-done.1, bf16[2,2,12,24,192]{4,3,2,1,0:T(8,128)(2,1)S(1)} %copy-done.3, bf16[192,192]{1,0:T(8,128)(2,1)S(1)} %get-tuple-element.63.refs_2_, ...), custom_call_target="tpu_custom_call" | custom-call | flops 3000000000 | bytes 4194304 | tf_op jit(solution)/shard_map/windows_upper/pallas_call | solution.py:376
  23.0 0.3 collective-permute-done.4.refs_12_
  23.3 5.5 %windows_second.1 = (bf16[576,192]{1,0:T(8,128)(2,1)S(1)}, f32[768,192]{1,0:T(8,128)S(1)}, f32[144,896]{1,0:T(8,128)S(1)}, f32[144,896]{1,0:T(8,128)S(1)}, bf16[288,192]{1,0:T(8,128)(2,1)S(1)}) custom-call(bf16[2,2,12,24,192]{4,3,2,1,0:T(8,128)(2,1)S(1)} %copy-done.1, bf16[2,2,12,24,192]{4,3,2,1,0:T(8,128)(2,1)S(1)} %copy-done.3, ...), custom_call_target="tpu_custom_call" | custom-call | flops 6000000000 | bytes 4194304 | tf_op jit(solution)/shard_map/windows_second/pallas_call | solution.py:376
  28.8 0.0 copy-start.7
  28.8 1.9 %fold.1 = (bf16[768,128]{1,0:T(8,128)(2,1)S(1)}, bf16[768,128]{1,0:T(8,128)(2,1)S(1)}) custom-call(f32[768,192]{1,0:T(8,128)S(1)} %get-tuple-element.46.w, f32[144,896]{1,0:T(8,128)S(1)} %get-tuple-element.47.gb0, f32[144,896]{1,0:T(8,128)S(1)} %get-tuple-element.48.gb1, s32[1,256]{1,0:T(1,128)S(1)} %bitcast.9, s32[1,1]{1,0:T(1,128)} %bitcast.2.core), custom_call_target="tpu_custom_call" | custom-call | flops 2000000000 | bytes 4194304 | tf_op jit(solution)/shard_map/fold/pallas_call | solution.py:351
  30.8 6.7 %collective-permute-start.9 = (bf16[768,128]{1,0:T(8,128)(2,1)S(1)}, bf16[768,128]{1,0:T(8,128)(2,1)S(1)}, u32[]{:S(2)}, u32[]{:S(2)}) collective-permute-start(bf16[768,128]{1,0:T(8,128)(2,1)S(1)} %get-tuple-element.50), channel_id=1, source_target_pairs={{0,8},{8,0},{16,24},{24,16},{32,40},{40,32},{48,56},{56,48},{64,72... | collective-permute-start | bytes 589832 | tf_op jit(solution)/shard_map/ppermute | solution.py:506
  37.4 1.1 %collective-permute-done.9 = bf16[768,128]{1,0:T(8,128)(2,1)S(1)} collective-permute-done((bf16[768,128]{1,0:T(8,128)(2,1)S(1)}, bf16[768,128]{1,0:T(8,128)(2,1)S(1)}, u32[]{:S(2)}, u32[]{:S(2)}) %collective-permute-start.9) | collective-permute-done | bytes 196640 | tf_op jit(solution)/shard_map/ppermute | solution.py:506
  38.5 0.1 add_convert_fusion
  38.6 12.3 %all_to_all.15 = bf16[8,96,128]{2,1,0:T(8,128)(2,1)S(1)} all-to-all(bf16[8,96,128]{2,1,0:T(8,128)(2,1)S(1)} %bitcast.10), channel_id=1, replica_groups={{0,32,64,96,128,160,192,224},{8,40,72,104,136,168,200,232},{16,48,80,11..., dimensions={0} | all-to-all | bytes 393216 | tf_op jit(solution)/shard_map/all_to_all | solution.py:520
  50.9 0.0 copy-start.8
  50.9 0.8 broadcast_in_dim.35
  51.7 6.1 %all-to-all-start.1 = ((bf16[16,96,128]{2,1,0:T(8,128)(2,1)}), bf16[16,96,128]{2,1,0:T(8,128)(2,1)S(1)}, u32[]{:S(2)}, u32[]{:S(2)}) async-start(bf16[16,96,128]{2,1,0:T(8,128)(2,1)} %broadcast_in_dim.35), calls=%async_computation.1 | async-start | bytes 786432 | tf_op jit(solution)/shard_map/all_to_all | solution.py:525
  57.9 4.9 %collective-permute-start.5 = (bf16[288,192]{1,0:T(8,128)(2,1)S(1)}, bf16[288,192]{1,0:T(8,128)(2,1)S(1)}, u32[]{:S(2)}, u32[]{:S(2)}) collective-permute-start(bf16[288,192]{1,0:T(8,128)(2,1)S(1)} %get-tuple-element.41), channel_id=1, source_target_pairs={{0,8},{8,16},{16,24},{24,32},{32,40},{40,48},{48,56},{56,64},{64,7... | collective-permute-start | bytes 331784 | tf_op jit(solution)/shard_map/ppermute | solution.py:492
  62.8 3.4 %all-to-all-done.1 = bf16[16,96,128]{2,1,0:T(8,128)(2,1)S(1)} async-done(((bf16[16,96,128]{2,1,0:T(8,128)(2,1)}), bf16[16,96,128]{2,1,0:T(8,128)(2,1)S(1)}, u32[]{:S(2)}, u32[]{:S(2)}) %all-to-all-start.1) | async-done | bytes 393248 | tf_op jit(solution)/shard_map/all_to_all | solution.py:525
  66.2 0.1 multiply_reduce_fusion
  66.3 0.7 broadcast_in_dim.38
  67.0 4.3 %all-to-all-start.2 = ((bf16[8,96,128]{2,1,0:T(8,128)(2,1)}), bf16[8,96,128]{2,1,0:T(8,128)(2,1)S(1)}, u32[]{:S(2)}, u32[]{:S(2)}) async-start(bf16[8,96,128]{2,1,0:T(8,128)(2,1)} %broadcast_in_dim.38), calls=%async_computation.2 | async-start | bytes 393216 | tf_op jit(solution)/shard_map/all_to_all | solution.py:535
  71.4 0.2 merge_lon.1
  71.5 0.1 collective-permute-start.6
  71.6 0.1 collective-permute-start.7
  71.7 0.3 collective-permute-start.8
  72.1 8.0 %all-to-all-done.2 = bf16[8,96,128]{2,1,0:T(8,128)(2,1)S(1)} async-done(((bf16[8,96,128]{2,1,0:T(8,128)(2,1)}), bf16[8,96,128]{2,1,0:T(8,128)(2,1)S(1)}, u32[]{:S(2)}, u32[]{:S(2)}) %all-to-all-start.2) | async-done | bytes 196640 | tf_op jit(solution)/shard_map/all_to_all | solution.py:535
  80.1 3.4 %collective-permute-start.10 = (bf16[768,128]{1,0:T(8,128)(2,1)S(1)}, bf16[768,128]{1,0:T(8,128)(2,1)S(1)}, u32[]{:S(2)}, u32[]{:S(2)}) collective-permute-start(bf16[768,128]{1,0:T(8,128)(2,1)S(1)} %bitcast.6), channel_id=1, source_target_pairs={{0,8},{8,0},{16,24},{24,16},{32,40},{40,32},{48,56},{56,48},{64,72... | collective-permute-start | bytes 589832 | tf_op jit(solution)/shard_map/ppermute | solution.py:506
  83.5 1.1 %place_grad.1 = f32[2,2,12,24,192]{4,3,2,1,0:T(8,128)} custom-call(bf16[2,9,24,192]{3,2,1,0:T(8,128)(2,1)S(1)} %get-tuple-element.42.own, bf16[2,9,24,192]{3,2,1,0:T(8,128)(2,1)S(1)} %collective-permute-done.6.lev, bf16[2,3,24,192]{3,2,1,0:T(8,128)(2,1)S(1)} %collective-permute-done.7.lat, bf16[2,3,24,192]{3,2,1,0:T(8,128)(2,1)S(1)} %collective-permute-done.8.diag), custom_call_target="tpu_custom_call" | custom-call | flops 20000000000 | bytes 2097152 | tf_op jit(solution)/shard_map/place_grad/pallas_call | solution.py:439
  84.6 1.2 %finish_params.1 = (f32[192,576]{1,0:T(8,128)}, f32[192,192]{1,0:T(8,128)}, f32[1,2,6,3312]{3,2,1,0:T(8,128)S(1)}) custom-call(bf16[768,128]{1,0:T(8,128)(2,1)S(1)} %bitcast.7, bf16[768,128]{1,0:T(8,128)(2,1)S(1)} %collective-permute-done.10.other, s32[1,1]{1,0:T(1,128)} %bitcast.2.core), custom_call_target="tpu_custom_call" | custom-call | bytes 2097152 | tf_op jit(solution)/shard_map/finish_params/pallas_call | solution.py:474
  85.7 0.7 copy.14
  (28 shorter events, 0.2 us)
Async XLA Ops:
  0.6 1.1 %copy-start = (bf16[2,2,12,24,192]{4,3,2,1,0:T(8,128)(2,1)S(1)}, bf16[2,2,12,24,192]{4,3,2,1,0:T(8,128)(2,1)}, u32[]{:S(2)}) copy-start(bf16[2,2,12,24,192]{4,3,2,1,0:T(8,128)(2,1)} %refs_0_.5) | copy-start | bytes 1327108
  1.7 1.1 %copy-start.2 = (bf16[2,2,12,24,192]{4,3,2,1,0:T(8,128)(2,1)S(1)}, bf16[2,2,12,24,192]{4,3,2,1,0:T(8,128)(2,1)}, u32[]{:S(2)}) copy-start(bf16[2,2,12,24,192]{4,3,2,1,0:T(8,128)(2,1)} %refs_1_.5) | copy-start | bytes 1327108
  2.8 7.0 %copy-start.10 = (f32[1,2,6,3312]{3,1,2,0:T(2,128)S(1)}, f32[1,2,6,3312]{3,1,2,0:T(2,128)}, u32[]{:S(2)}) copy-start(f32[1,2,6,3312]{3,1,2,0:T(2,128)} %param.9) | copy-start | bytes 476932
  2.9 11.9 %collective-permute-start = (bf16[2,6,24,384]{3,2,1,0:T(8,128)(2,1)S(1)}, bf16[2,6,24,384]{3,2,1,0:T(8,128)(2,1)S(1)}, u32[]{:S(2)}, u32[]{:S(2)}) collective-permute-start(bf16[2,6,24,384]{3,2,1,0:T(8,128)(2,1)S(1)} %pack_near.1), channel_id=1, source_target_pairs={{0,1},{1,0},{2,3},{3,2},{4,5},{5,4},{6,7},{7,6},{8,9},{9,8},{10,11... | collective-permute-start | bytes 663560 | tf_op jit(solution)/shard_map/ppermute | solution.py:492
  5.2 9.6 %collective-permute-start.1 = (bf16[2,3,24,384]{3,2,1,0:T(8,128)(2,1)S(1)}, bf16[2,3,24,384]{3,2,1,0:T(8,128)(2,1)S(1)}, u32[]{:S(2)}, u32[]{:S(2)}) collective-permute-start(bf16[2,3,24,384]{3,2,1,0:T(8,128)(2,1)S(1)} %get-tuple-element.32), channel_id=1, source_target_pairs={{0,1},{1,0},{2,3},{3,2},{4,5},{5,4},{6,7},{7,6},{8,9},{9,8},{10,11... | collective-permute-start | bytes 331784 | tf_op jit(solution)/shard_map/ppermute | solution.py:492
  5.3 9.5 %collective-permute-start.2 = (bf16[2,3,24,384]{3,2,1,0:T(8,128)(2,1)S(1)}, bf16[2,3,24,384]{3,2,1,0:T(8,128)(2,1)S(1)}, u32[]{:S(2)}, u32[]{:S(2)}) collective-permute-start(bf16[2,3,24,384]{3,2,1,0:T(8,128)(2,1)S(1)} %get-tuple-element.33), channel_id=1, source_target_pairs={{0,6},{2,0},{4,2},{6,4},{1,7},{3,1},{5,3},{7,5},{8,14},{10,8},{12,... | collective-permute-start | bytes 331784 | tf_op jit(solution)/shard_map/ppermute | solution.py:492
  7.9 6.8 %collective-permute-start.3 = (bf16[2,3,24,384]{3,2,1,0:T(8,128)(2,1)S(1)}, bf16[2,3,24,384]{3,2,1,0:T(8,128)(2,1)S(1)}, u32[]{:S(2)}, u32[]{:S(2)}) collective-permute-start(bf16[2,3,24,384]{3,2,1,0:T(8,128)(2,1)S(1)} %get-tuple-element.34), channel_id=1, source_target_pairs={{0,7},{1,6},{2,1},{3,0},{4,3},{5,2},{6,5},{7,4},{8,15},{9,14},{10,... | collective-permute-start | bytes 331784 | tf_op jit(solution)/shard_map/ppermute | solution.py:502
  9.8 4.8 %copy-start.9 = (bf16[192,576]{1,0:T(8,128)(2,1)S(1)}, bf16[192,576]{1,0:T(8,128)(2,1)}, u32[]{:S(2)}) copy-start(bf16[192,576]{1,0:T(8,128)(2,1)} %param.7) | copy-start | bytes 663556
  9.8 5.0 %copy-start.1 = (bf16[2,2,12,24,192]{4,3,2,1,0:T(8,128)(2,1)S(1)}, bf16[2,2,12,24,192]{4,3,2,1,0:T(8,128)(2,1)}, u32[]{:S(2)}) copy-start(bf16[2,2,12,24,192]{4,3,2,1,0:T(8,128)(2,1)} %refs_0_.5) | copy-start | bytes 1327108
  9.8 5.0 %copy-start.3 = (bf16[2,2,12,24,192]{4,3,2,1,0:T(8,128)(2,1)S(1)}, bf16[2,2,12,24,192]{4,3,2,1,0:T(8,128)(2,1)}, u32[]{:S(2)}) copy-start(bf16[2,2,12,24,192]{4,3,2,1,0:T(8,128)(2,1)} %refs_1_.5) | copy-start | bytes 1327108
  13.8 0.8 copy-start.5
  14.6 2.4 %copy-start.4 = (bf16[192,192]{1,0:T(8,128)(2,1)S(1)}, bf16[192,192]{1,0:T(8,128)(2,1)}, u32[]{:S(2)}) copy-start(bf16[192,192]{1,0:T(8,128)(2,1)} %refs_5_.5) | copy-start | bytes 221188
  14.7 2.3 %copy-start.6 = (f32[144,896]{1,0:T(8,128)S(1)}, f32[144,896]{1,0:T(8,128)}, u32[]{:S(2)}) copy-start(f32[144,896]{1,0:T(8,128)} %copy-done.5) | copy-start | bytes 1548292
  15.0 8.3 %collective-permute-start.4 = (bf16[288,384]{1,0:T(8,128)(2,1)S(1)}, bf16[288,384]{1,0:T(8,128)(2,1)S(1)}, u32[]{:S(2)}, u32[]{:S(2)}) collective-permute-start(bf16[288,384]{1,0:T(8,128)(2,1)S(1)} %pack_lon.1), channel_id=1, source_target_pairs={{0,248},{8,0},{16,8},{24,16},{32,24},{40,32},{48,40},{56,48},{64,5... | collective-permute-start | bytes 663560 | tf_op jit(solution)/shard_map/ppermute | solution.py:492
  28.8 1.9 %copy-start.7 = (bf16[576,192]{1,0:T(8,128)(2,1)}, bf16[576,192]{1,0:T(8,128)(2,1)S(1)}, u32[]{:S(2)}) copy-start(bf16[576,192]{1,0:T(8,128)(2,1)S(1)} %get-tuple-element.40.g_second) | copy-start | bytes 663556
  30.8 7.7 %collective-permute-start.9 = (bf16[768,128]{1,0:T(8,128)(2,1)S(1)}, bf16[768,128]{1,0:T(8,128)(2,1)S(1)}, u32[]{:S(2)}, u32[]{:S(2)}) collective-permute-start(bf16[768,128]{1,0:T(8,128)(2,1)S(1)} %get-tuple-element.50), channel_id=1, source_target_pairs={{0,8},{8,0},{16,24},{24,16},{32,40},{40,32},{48,56},{56,48},{64,72... | collective-permute-start | bytes 589832 | tf_op jit(solution)/shard_map/ppermute | solution.py:506
  50.9 20.4 %copy-start.8 = (bf16[576,192]{1,0:T(8,128)(2,1)S(1)}, bf16[576,192]{1,0:T(8,128)(2,1)}, u32[]{:S(2)}) copy-start(bf16[576,192]{1,0:T(8,128)(2,1)} %copy-done.7) | copy-start | bytes 663556
  51.7 14.4 %all-to-all-start.1 = ((bf16[16,96,128]{2,1,0:T(8,128)(2,1)}), bf16[16,96,128]{2,1,0:T(8,128)(2,1)S(1)}, u32[]{:S(2)}, u32[]{:S(2)}) async-start(bf16[16,96,128]{2,1,0:T(8,128)(2,1)} %broadcast_in_dim.35), calls=%async_computation.1 | async-start | bytes 786432 | tf_op jit(solution)/shard_map/all_to_all | solution.py:525
  57.9 13.4 %collective-permute-start.5 = (bf16[288,192]{1,0:T(8,128)(2,1)S(1)}, bf16[288,192]{1,0:T(8,128)(2,1)S(1)}, u32[]{:S(2)}, u32[]{:S(2)}) collective-permute-start(bf16[288,192]{1,0:T(8,128)(2,1)S(1)} %get-tuple-element.41), channel_id=1, source_target_pairs={{0,8},{8,16},{16,24},{24,32},{32,40},{40,48},{48,56},{56,64},{64,7... | collective-permute-start | bytes 331784 | tf_op jit(solution)/shard_map/ppermute | solution.py:492
  67.0 13.1 %all-to-all-start.2 = ((bf16[8,96,128]{2,1,0:T(8,128)(2,1)}), bf16[8,96,128]{2,1,0:T(8,128)(2,1)S(1)}, u32[]{:S(2)}, u32[]{:S(2)}) async-start(bf16[8,96,128]{2,1,0:T(8,128)(2,1)} %broadcast_in_dim.38), calls=%async_computation.2 | async-start | bytes 393216 | tf_op jit(solution)/shard_map/all_to_all | solution.py:535
  71.5 11.9 %collective-permute-start.6 = (bf16[2,9,24,192]{3,2,1,0:T(8,128)(2,1)S(1)}, bf16[2,9,24,192]{3,2,1,0:T(8,128)(2,1)S(1)}, u32[]{:S(2)}, u32[]{:S(2)}) collective-permute-start(bf16[2,9,24,192]{3,2,1,0:T(8,128)(2,1)S(1)} %get-tuple-element.43), channel_id=1, source_target_pairs={{0,1},{1,0},{2,3},{3,2},{4,5},{5,4},{6,7},{7,6},{8,9},{9,8},{10,11... | collective-permute-start | bytes 497672 | tf_op jit(solution)/shard_map/ppermute | solution.py:492
  71.6 11.8 %collective-permute-start.7 = (bf16[2,3,24,192]{3,2,1,0:T(8,128)(2,1)S(1)}, bf16[2,3,24,192]{3,2,1,0:T(8,128)(2,1)S(1)}, u32[]{:S(2)}, u32[]{:S(2)}) collective-permute-start(bf16[2,3,24,192]{3,2,1,0:T(8,128)(2,1)S(1)} %get-tuple-element.44), channel_id=1, source_target_pairs={{0,2},{2,4},{4,6},{6,0},{1,3},{3,5},{5,7},{7,1},{8,10},{10,12},{12... | collective-permute-start | bytes 165896 | tf_op jit(solution)/shard_map/ppermute | solution.py:492
  71.7 11.7 %collective-permute-start.8 = (bf16[2,3,24,192]{3,2,1,0:T(8,128)(2,1)S(1)}, bf16[2,3,24,192]{3,2,1,0:T(8,128)(2,1)S(1)}, u32[]{:S(2)}, u32[]{:S(2)}) collective-permute-start(bf16[2,3,24,192]{3,2,1,0:T(8,128)(2,1)S(1)} %get-tuple-element.45), channel_id=1, source_target_pairs={{0,3},{1,2},{2,5},{3,4},{4,7},{5,6},{6,1},{7,0},{8,11},{9,10},{10,... | collective-permute-start | bytes 165896 | tf_op jit(solution)/shard_map/ppermute | solution.py:502
  80.1 4.5 %collective-permute-start.10 = (bf16[768,128]{1,0:T(8,128)(2,1)S(1)}, bf16[768,128]{1,0:T(8,128)(2,1)S(1)}, u32[]{:S(2)}, u32[]{:S(2)}) collective-permute-start(bf16[768,128]{1,0:T(8,128)(2,1)S(1)} %bitcast.6), channel_id=1, source_target_pairs={{0,8},{8,0},{16,24},{24,16},{32,40},{40,32},{48,56},{56,48},{64,72... | collective-permute-start | bytes 589832 | tf_op jit(solution)/shard_map/ppermute | solution.py:506

commit v3 on v2

--- a/solution.py
+++ b/solution.py
@@ -29,6 +29,9 @@
 BF = jnp.bfloat16
 F32 = jnp.float32
 SPREAD = 896
+MAIN = 128
+TAIL = WIN - MAIN
+TAILS = HEADS * MAIN
 PAIR = 2 * WIN
 BOTH = 2 * C
 VMEM = pl.BlockSpec(memory_space=pltpu.VMEM)
@@ -113,7 +116,7 @@
     return split(line.astype(F32))
 
 
-def pack_lon_kernel(f, u, near, far, lat, diag, out, tmp):
+def pack_lon_kernel(f, u, near, far, lat, diag, after, out, tmp):
     for b in range(2):
         for z in range(2):
             for r in range(12):
@@ -123,17 +126,17 @@
     out[...] = tmp[...].astype(BF)
 
 
-def pack_lon(fields, upstream, halos):
+def pack_lon(fields, upstream, halos, after):
     return pl.pallas_call(
         pack_lon_kernel,
         name="pack_lon",
         out_shape=shape((2 * WIN, BOTH), BF),
-        in_specs=[VMEM] * 6,
+        in_specs=[VMEM] * 6 + [HBM],
         out_specs=VMEM,
         scratch_shapes=[pltpu.VMEM((2 * WIN, BOTH), F32)],
         compiler_params=params(16),
         cost_estimate=cost(0, 2 * 1024 * 1024),
-    )(fields, upstream, *halos)
+    )(fields, upstream, *halos, after)
 
 
 def onehot_rows(target, w1):
@@ -172,12 +175,14 @@
             out_a[pl.ds(q, 12, stride=WIN), :] = part[:, 0:128]
             out_b[pl.ds(q, 12, stride=WIN), :] = part[:, 128:256]
     for aw, out in enumerate((out0, out1)):
-        heads = []
+        tails = []
         for h in range(HEADS):
             rows = slice((aw * HEADS + h) * WIN, (aw * HEADS + h + 1) * WIN)
-            heads.append(jnp.concatenate([out_a[rows, :], out_b[rows, 0:16]], axis=1).T)
-        heads.append(jnp.zeros((WIN, SPREAD - HEADS * WIN), F32))
-        out[...] = jnp.concatenate(heads, axis=1)
+            turned = jnp.concatenate([out_a[rows, :], out_b[rows, 0:16]], axis=1).T
+            out[:, h * MAIN : (h + 1) * MAIN] = turned[:, 0:MAIN]
+            tails.append(turned[:, MAIN:WIN])
+        tails.append(jnp.zeros((WIN, SPREAD - HEADS * WIN), F32))
+        out[:, TAILS:SPREAD] = jnp.concatenate(tails, axis=1)
 
 
 def expand(earth_bias, target, rq, rk):
@@ -215,7 +220,7 @@
     gbs = dict(zip(aws, take(len(aws))))
     if second:
         (lon_back,) = take(1)
-    x_s, u_s, i_s, low_s, q_s, k_s, v_s, ga_s, gq_s = take(9)
+    x_s, u_s, i_s, low_s, q_s, k_s, v_s, ga_s, gq_s, gk_s, gv_s, att_s, up_s = take(13)
     if second:
         g_s, lon_s = take(2)
     w_s[...] = w_in[...] if started else jnp.zeros_like(w_s)
@@ -249,7 +254,12 @@
     q_s[...] = dot(low, wq[...]).astype(BF)
     k_s[...] = dot(low, wk[...]).astype(BF)
     v_s[...] = dot(low, wv[...]).astype(BF)
-    ga_s[...] = dot(u_s[...].astype(BF), wo[...], 1, 1).astype(BF)
+    up = u_s[...].astype(BF)
+    ga_s[...] = dot(up, wo[...], 1, 1).astype(BF)
+    att_s[...] = jnp.zeros_like(att_s)
+    up_s[...] = jnp.zeros_like(up_s)
+    for w in range(2 * len(aws)):
+        up_s[w * KEYS : w * KEYS + WIN, :] = up[w * WIN : (w + 1) * WIN]
 
     lane = lax.broadcasted_iota(jnp.int32, (1, C), 1)
     picks = [
@@ -259,18 +269,25 @@
 
     def stack(a):
         pad = jnp.zeros((SPREAD - HEADS * WIN, C), BF)
-        return jnp.concatenate([a * m for m in picks] + [pad], axis=0)
-
-    def unstack(a):
-        return jnp.concatenate(
-            [a[h * HD : (h + 1) * HD, h * WIN : (h + 1) * WIN] for h in range(HEADS)], axis=0
-        )
+        mains = [a[0:MAIN] * m for m in picks]
+        return jnp.concatenate(mains + [a[MAIN:WIN] * m for m in picks] + [pad], axis=0)
+
+    def per_head(a, probs):
+        tails = dot(a, probs[:, TAILS:SPREAD])
+        heads = []
+        for i in range(HEADS // 2):
+            pair = dot(a[2 * i * HD : 2 * (i + 1) * HD], probs[:, 2 * i * MAIN : 2 * (i + 1) * MAIN])
+            for n in range(2):
+                h = 2 * i + n
+                main = pair[n * HD : (n + 1) * HD, n * MAIN : (n + 1) * MAIN]
+                tail = tails[h * HD : (h + 1) * HD, h * TAIL : (h + 1) * TAIL]
+                heads.append(jnp.concatenate([main, tail], axis=1))
+        return jnp.concatenate(heads, axis=0)
 
     for w in range(2 * len(aws)):
         rows = slice(w * WIN, (w + 1) * WIN)
         bias, gb_s = biases[aws[w // 2]], gbs[aws[w // 2]]
         low, q, k, v, ga = low_s[rows, :], q_s[rows, :], k_s[rows, :], v_s[rows, :], ga_s[rows, :]
-        up = u_s[rows, :].astype(BF)
         qs = stack(q)
         gas = stack(ga)
         scores = dot(k, qs, 1, 1)
@@ -288,19 +305,18 @@
             grads_low.append(gs.astype(BF))
         p = jnp.concatenate(probs, axis=1)
         gs = jnp.concatenate(grads_low, axis=1)
-        gv = dot(p, gas).astype(BF)
-        gk = (dot(gs, qs) * SCALE).astype(BF)
-        att_t = unstack(dot(v, p, 0, 0)).astype(BF)
-        gq_t = (unstack(dot(k, gs, 0, 0)) * SCALE).astype(BF)
-        w_s[0:C, :] += dot(gq_t, low)
-        w_s[C : 2 * C, :] += dot(low, gk, 0, 0)
-        w_s[2 * C : 3 * C, :] += dot(low, gv, 0, 0)
-        w_s[3 * C : 4 * C, :] += dot(att_t, up)
-        gq_s[rows, :] = (
-            dot(gq_t, wq[...], 0, 1) + dot(gk, wk[...], 1, 1) + dot(gv, wv[...], 1, 1)
-        )
-
-    gu = gq_s[...]
+        gv_s[rows, :] = dot(p, gas).astype(BF)
+        gk_s[rows, :] = (dot(gs, qs) * SCALE).astype(BF)
+        gq_s[rows, :] = (per_head(k.T, gs) * SCALE).T.astype(BF)
+        att_s[:, w * KEYS : w * KEYS + WIN] = per_head(v.T, p).astype(BF)
+
+    w_s[3 * C : 4 * C, :] += dot(att_s[...], up_s[...])
+    gq, gk, gv = gq_s[...], gk_s[...], gv_s[...]
+    low_t = low_s[...].T
+    w_s[0:C, :] += dot(low_t, gq)
+    w_s[C : 2 * C, :] += dot(low_t, gk)
+    w_s[2 * C : 3 * C, :] += dot(low_t, gv)
+    gu = dot(gq, wq[...], 1, 1) + dot(gk, wk[...], 1, 1) + dot(gv, wv[...], 1, 1)
     normed = x_s[...]
     centre = jnp.mean(gu, axis=-1, keepdims=True)
     along = jnp.mean(gu * normed, axis=-1, keepdims=True)
@@ -319,17 +335,17 @@
     lon_back[...] = lon_s[...].astype(BF)
 
 
-def fold_kernel(w, gb0, gb1, target, core, keep, send, w_s, turned, slab):
-    w_s[C:, :] = w[C:, :]
-    w_s[0:C, :] = w[0:C, :].T
+def fold_kernel(w_s, gb0, gb1, target, core, keep, send, turned, slab):
     slab[0:768, :] = w_s[:, 0:128].astype(BF)
     slab[768:1152, :] = jnp.concatenate([w_s[0:384, 128:192], w_s[384:768, 128:192]], axis=1).astype(BF)
     for z2 in range(2):
         for aw, gb in enumerate((gb0, gb1)):
+            rows = slice(z2 * 72, z2 * 72 + 72)
+            tails = gb[rows, TAILS:SPREAD].T
             for h in range(HEADS):
-                at = ((z2 * 2 + aw) * HEADS + h) * WIN
-                rows = slice(z2 * 72, z2 * 72 + 72)
-                turned[at : at + WIN, 0:72] = gb[rows, h * WIN : (h + 1) * WIN].T
+                at = ((z2 * HEADS + h) * 2 + aw) * WIN
+                turned[at : at + MAIN, 0:72] = gb[rows, h * MAIN : (h + 1) * MAIN].T
+                turned[at + MAIN : at + WIN, 0:72] = tails[h * TAIL : (h + 1) * TAIL]
     folded = jnp.zeros((288, KEYS), F32)
     tgt = target[...]
     lane = lax.broadcasted_iota(jnp.int32, (KEYS, 72), 0)
@@ -355,7 +371,6 @@
         in_specs=[VMEM] * 4 + [SMEM],
         out_specs=(VMEM,) * 2,
         scratch_shapes=[
-            pltpu.VMEM((4 * C, C), F32),
             pltpu.VMEM((24 * WIN, 128), F32),
             pltpu.VMEM((SLAB, 128), BF),
         ],
@@ -367,7 +382,9 @@
 def windows(aws, second, *args):
     tokens = len(aws) * PAIR
     rows = [pltpu.VMEM((tokens, C), F32)] * 2 + [pltpu.VMEM((tokens, 1), F32)]
-    rows += [pltpu.VMEM((tokens, C), BF)] * 5 + [pltpu.VMEM((tokens, C), F32)]
+    rows += [pltpu.VMEM((tokens, C), BF)] * 8
+    padded = 2 * len(aws) * KEYS
+    rows += [pltpu.VMEM((C, padded), BF), pltpu.VMEM((padded, C), BF)]
     outs = (shape((tokens, C), BF), shape((4 * C, C), F32))
     outs += (shape((WIN, SPREAD), F32),) * len(aws)
     if second:
@@ -465,9 +482,8 @@
         for h1 in range(6):
             for z2 in range(2):
                 off = ((z1 * 2 + z2) * 6 + h1) * GROUP
-                for aw in range(2):
-                    at = (z1 * 6 + h1) * 24 + z2 * 12 + aw * 6
-                    bias[0, aw, :, off : off + GROUP] = pairs[at : at + 6]
+                at = (z1 * 6 + h1) * 24 + z2 * 12
+                bias[0, :, :, off : off + GROUP] = pairs[at : at + 12].reshape(HEADS, 2, GROUP)
 
 
 def finish(half, other, core, factor):
@@ -477,7 +493,7 @@
         out_shape=(
             shape((C, 3 * C), F32),
             shape((C, C), F32),
-            shape((1, 2, HEADS, PAIRS), F32),
+            shape((1, HEADS, 2, PAIRS), F32),
         ),
         in_specs=[VMEM, VMEM, SMEM],
         out_specs=(VMEM,) * 3,
@@ -565,7 +581,7 @@
     )
     g_lower, w, gb0 = windows((0,), False, *shared, bias0, near)
     rest = (far, lat, diag)
-    lon = from_behind(pack_lon(fields, upstream, (near,) + rest), "lon", -1)
+    lon = from_behind(pack_lon(fields, upstream, (near,) + rest, g_lower), "lon", -1)
     g_upper, w, gb1 = windows((1,), False, *shared, bias1, *rest, w)
     g_second, w, gb0, gb1, lon_back = windows(
         (0, 1), True, *shared, bias0, bias1, near, *rest, lon, w, gb0, gb1
@@ -584,7 +600,7 @@
     for axis in ("lon", "lat", "lev"):
         tokens = tokens * lax.axis_size(axis)
     qkv_grad, out_grad, bias_grad = finish(half, other, core, 1.0 / math.sqrt(tokens))
-    return (field_grad, qkv_grad, out_grad, bias_grad)
+    return (field_grad, qkv_grad, out_grad, bias_grad.transpose(0, 2, 1, 3))
 
 
 def solution(mesh):

time: 86.9 us -> 84.6 us (0.974)
  starting transfers between devices: 34.4 us -> 30.6 us
  waiting for transfers between devices: 12.8 us -> 16 us
  Pallas kernels: 20.2 us -> 18 us
  blocking collectives: 12.3 us -> 14.4 us
  local copies, waits for them, and re-layouts: 5.47 us -> 3.93 us
    ppermute x7, waiting for transfers between devices: 0.28 us -> 3.54 us  [from_behind(): lax.ppermute(x, axis, [(i, (i + by) % devices) for i in range(devices)])]
    ppermute x2, starting transfers between devices: 10 us -> 7.3 us  [other_core(): lax.ppermute(x, 'lon', [(i, i ^ 1) for i in range(lax.axis_size('lon'))])]
    all_to_all x1, blocking collectives: 12.3 us -> 14.4 us  [reduce_slab(): lax.all_to_all(half.reshape(depth, rows, 128), 'lon', 0, 0, axis_index_gr...]
    unnamed x24 -> x15, local copies, waits for them, and re-layouts: 3.73 us -> 2.18 us
    pallas_call x3, Pallas kernels: 11.4 us -> 9.97 us  [windows(): pl.pallas_call(functools.partial(windows_kernel, aws, second), name='wind...]
    all_to_all x1, starting transfers between devices: 6.12 us -> 5 us  [reduce_slab(): lax.all_to_all(jnp.broadcast_to(mine[None], (count, rows, 128)), ('lon',...]
  transfers between devices with their start and end apart: 13 -> 13, of which waited for: 4 -> 4; matrix products, arithmetic and copies ran while one was open for 1% -> 1% of each run, Pallas kernels for 13% -> 12%
where the time goes in v3:
time: 84.6 us; the launch traced here: 84.2 us
  starting transfers between devices  30.6 us (36%)
  Pallas kernels  18 us (21%)
  waiting for transfers between devices  16 us (19%)
  blocking collectives  14.4 us (17%)
  local copies, waits for them, and re-layouts  3.93 us (5%)
  between operations  0.95 us (1%)
    all_to_all x1, blocking collectives, reduce_slab(): lax.all_to_all(half.reshape(depth, rows, 128), 'lon', 0, 0, axis_index_gr...  14.4 us
    ppermute x7, starting transfers between devices, from_behind(): lax.ppermute(x, axis, [(i, (i + by) % devices) for i in range(devices)])  12 us
    pallas_call x3, Pallas kernels, windows(): pl.pallas_call(functools.partial(windows_kernel, aws, second), name='wind...  9.97 us
    all_to_all x1, waiting for transfers between devices, reduce_slab(): lax.all_to_all(jnp.broadcast_to(mine[None], (depth, rows, 128)), 'lon', 0...  8.04 us
    ppermute x2, starting transfers between devices, other_core(): lax.ppermute(x, 'lon', [(i, i ^ 1) for i in range(lax.axis_size('lon'))])  7.3 us
    all_to_all x1, starting transfers between devices, reduce_slab(): lax.all_to_all(jnp.broadcast_to(mine[None], (count, rows, 128)), ('lon',...  5 us
    all_to_all x1, starting transfers between devices, reduce_slab(): lax.all_to_all(jnp.broadcast_to(mine[None], (depth, rows, 128)), 'lon', 0...  4.33 us
    pallas_call x1, Pallas kernels, expand(): pl.pallas_call(expand_kernel, name='expand_bias', out_shape=(shape((WIN,...  3.83 us
  transfers between devices with their start and end apart: 13, of which 4 were waited for; matrix products, arithmetic and copies ran while one was open for 1% of the time, Pallas kernels for 12%

profile of v3, /device:TPU:1, one launch (start us, length us, event | category | flops | bytes accessed | tf_op | source)
XLA Modules:
  0.0 84.2 jit_solution(851263261665026446)
XLA Ops:
  0.6 0.0 copy-start
  0.6 1.1 %copy-done = bf16[2,2,12,24,192]{4,3,2,1,0:T(8,128)(2,1)S(1)} copy-done((bf16[2,2,12,24,192]{4,3,2,1,0:T(8,128)(2,1)S(1)}, bf16[2,2,12,24,192]{4,3,2,1,0:T(8,128)(2,1)}, u32[]{:S(2)}) %copy-start) | copy-done | bytes 442392
  1.7 1.1 %copy-done.2 = bf16[2,2,12,24,192]{4,3,2,1,0:T(8,128)(2,1)S(1)} copy-done((bf16[2,2,12,24,192]{4,3,2,1,0:T(8,128)(2,1)S(1)}, bf16[2,2,12,24,192]{4,3,2,1,0:T(8,128)(2,1)}, u32[]{:S(2)}) %copy-start.2) | copy-done | bytes 442392
  2.8 0.1 pack_near.1
  2.9 2.2 %collective-permute-start = (bf16[2,6,24,384]{3,2,1,0:T(8,128)(2,1)S(1)}, bf16[2,6,24,384]{3,2,1,0:T(8,128)(2,1)S(1)}, u32[]{:S(2)}, u32[]{:S(2)}) collective-permute-start(bf16[2,6,24,384]{3,2,1,0:T(8,128)(2,1)S(1)} %pack_near.1), channel_id=1, source_target_pairs={{0,1},{1,0},{2,3},{3,2},{4,5},{5,4},{6,7},{7,6},{8,9},{9,8},{10,11... | collective-permute-start | bytes 663560 | tf_op jit(solution)/shard_map/ppermute | solution.py:508
  5.1 0.1 pack_rest.1
  5.2 0.1 collective-permute-start.1
  5.3 2.6 %collective-permute-start.2 = (bf16[2,3,24,384]{3,2,1,0:T(8,128)(2,1)S(1)}, bf16[2,3,24,384]{3,2,1,0:T(8,128)(2,1)S(1)}, u32[]{:S(2)}, u32[]{:S(2)}) collective-permute-start(bf16[2,3,24,384]{3,2,1,0:T(8,128)(2,1)S(1)} %get-tuple-element.33), channel_id=1, source_target_pairs={{0,6},{2,0},{4,2},{6,4},{1,7},{3,1},{5,3},{7,5},{8,14},{10,8},{12,... | collective-permute-start | bytes 331784 | tf_op jit(solution)/shard_map/ppermute | solution.py:508
  7.9 1.6 %collective-permute-start.3 = (bf16[2,3,24,384]{3,2,1,0:T(8,128)(2,1)S(1)}, bf16[2,3,24,384]{3,2,1,0:T(8,128)(2,1)S(1)}, u32[]{:S(2)}, u32[]{:S(2)}) collective-permute-start(bf16[2,3,24,384]{3,2,1,0:T(8,128)(2,1)S(1)} %get-tuple-element.34), channel_id=1, source_target_pairs={{0,7},{1,6},{2,1},{3,0},{4,3},{5,2},{6,5},{7,4},{8,15},{9,14},{10,... | collective-permute-start | bytes 331784 | tf_op jit(solution)/shard_map/ppermute | solution.py:518
  9.6 0.1 copy.12.rq
  9.8 0.0 copy-start.5
  9.8 0.0 copy-start.1
  9.8 0.0 copy-start.3
  9.8 0.0 copy-start.4
  9.8 3.8 %expand_bias.1 = (f32[144,896]{1,0:T(8,128)S(1)}, f32[144,896]{1,0:T(8,128)S(1)}) custom-call(f32[1,2,6,3312]{3,2,1,0:T(8,128)S(1)} %copy.11.eb, s32[1,256]{1,0:T(1,128)S(1)} %bitcast.9, f32[2,144,1]{2,1,0:T(8,128)S(1)} %copy.12.rq, f32[2,1,256]{2,1,0:T(1,128)S(1)} %broadcast_in_dim.34.rk), custom_call_target="tpu_custom_call" | custom-call | flops 4000000000 | bytes 4194304 | tf_op jit(solution)/shard_map/expand_bias/pallas_call | solution.py:189
  13.7 0.1 fusion.8
  13.8 0.0 collective-permute-done.refs_7_.near.refs_8_
  13.8 2.6 %windows_lower.1 = (bf16[288,192]{1,0:T(8,128)(2,1)S(1)}, f32[768,192]{1,0:T(8,128)S(1)}, f32[144,896]{1,0:T(8,128)S(1)}) custom-call(bf16[2,2,12,24,192]{4,3,2,1,0:T(8,128)(2,1)S(1)} %copy-done.1, bf16[2,2,12,24,192]{4,3,2,1,0:T(8,128)(2,1)S(1)} %copy-done.3, bf16[192,192]{1,0:T(8,128)(2,1)S(1)} %get-tuple-element.55.refs_2_, ...), custom_call_target="tpu_custom_call" | custom-call | flops 3000000000 | bytes 4194304 | tf_op jit(solution)/shard_map/windows_lower/pallas_call | solution.py:393
  16.4 0.0 collective-permute-done.1.refs_7_.far.refs_9_
  16.4 0.0 collective-permute-done.2.refs_8_.lat.refs_10_
  16.4 0.0 collective-permute-done.3.refs_9_.diag.refs_11_
  16.4 0.2 pack_lon.1
  16.6 2.0 %collective-permute-start.4 = (bf16[288,384]{1,0:T(8,128)(2,1)S(1)}, bf16[288,384]{1,0:T(8,128)(2,1)S(1)}, u32[]{:S(2)}, u32[]{:S(2)}) collective-permute-start(bf16[288,384]{1,0:T(8,128)(2,1)S(1)} %pack_lon.1), channel_id=1, source_target_pairs={{0,248},{8,0},{16,8},{24,16},{32,24},{40,32},{48,40},{56,48},{64,5... | collective-permute-start | bytes 663560 | tf_op jit(solution)/shard_map/ppermute | solution.py:508
  18.7 2.6 %windows_upper.1 = (bf16[288,192]{1,0:T(8,128)(2,1)S(1)}, f32[768,192]{1,0:T(8,128)S(1)}, f32[144,896]{1,0:T(8,128)S(1)}) custom-call(bf16[2,2,12,24,192]{4,3,2,1,0:T(8,128)(2,1)S(1)} %copy-done.1, bf16[2,2,12,24,192]{4,3,2,1,0:T(8,128)(2,1)S(1)} %copy-done.3, bf16[192,192]{1,0:T(8,128)(2,1)S(1)} %get-tuple-element.55.refs_2_, ...), custom_call_target="tpu_custom_call" | custom-call | flops 3000000000 | bytes 4194304 | tf_op jit(solution)/shard_map/windows_upper/pallas_call | solution.py:393
  21.3 3.5 %collective-permute-done.4.refs_12_ = bf16[288,384]{1,0:T(8,128)(2,1)S(1)} collective-permute-done((bf16[288,384]{1,0:T(8,128)(2,1)S(1)}, bf16[288,384]{1,0:T(8,128)(2,1)S(1)}, u32[]{:S(2)}, u32[]{:S(2)}) %collective-permute-start.4) | collective-permute-done | bytes 221216 | tf_op jit(solution)/shard_map/ppermute | solution.py:508
  24.8 4.8 %windows_second.1 = (bf16[576,192]{1,0:T(8,128)(2,1)S(1)}, f32[768,192]{1,0:T(8,128)S(1)}, f32[144,896]{1,0:T(8,128)S(1)}, f32[144,896]{1,0:T(8,128)S(1)}, bf16[288,192]{1,0:T(8,128)(2,1)S(1)}) custom-call(bf16[2,2,12,24,192]{4,3,2,1,0:T(8,128)(2,1)S(1)} %copy-done.1, bf16[2,2,12,24,192]{4,3,2,1,0:T(8,128)(2,1)S(1)} %copy-done.3, ...), custom_call_target="tpu_custom_call" | custom-call | flops 6000000000 | bytes 4194304 | tf_op jit(solution)/shard_map/windows_second/pallas_call | solution.py:393
  29.6 1.3 %fold.1 = (bf16[768,128]{1,0:T(8,128)(2,1)S(1)}, bf16[768,128]{1,0:T(8,128)(2,1)S(1)}) custom-call(f32[768,192]{1,0:T(8,128)S(1)} %get-tuple-element.46.w_s, f32[144,896]{1,0:T(8,128)S(1)} %get-tuple-element.47.gb0, f32[144,896]{1,0:T(8,128)S(1)} %get-tuple-element.48.gb1, s32[1,256]{1,0:T(1,128)S(1)} %bitcast.10, s32[1,1]{1,0:T(1,128)} %bitcast.2.core), custom_call_target="tpu_custom_call" | custom-call | flops 2000000000 | bytes 4194304 | tf_op jit(solution)/shard_map/fold/pallas_call | solution.py:367
  30.9 3.9 %collective-permute-start.9 = (bf16[768,128]{1,0:T(8,128)(2,1)S(1)}, bf16[768,128]{1,0:T(8,128)(2,1)S(1)}, u32[]{:S(2)}, u32[]{:S(2)}) collective-permute-start(bf16[768,128]{1,0:T(8,128)(2,1)S(1)} %get-tuple-element.50), channel_id=1, source_target_pairs={{0,8},{8,0},{16,24},{24,16},{32,40},{40,32},{48,56},{56,48},{64,72... | collective-permute-start | bytes 589832 | tf_op jit(solution)/shard_map/ppermute | solution.py:522
  34.9 1.1 %collective-permute-done.9 = bf16[768,128]{1,0:T(8,128)(2,1)S(1)} collective-permute-done((bf16[768,128]{1,0:T(8,128)(2,1)S(1)}, bf16[768,128]{1,0:T(8,128)(2,1)S(1)}, u32[]{:S(2)}, u32[]{:S(2)}) %collective-permute-start.9) | collective-permute-done | bytes 196640 | tf_op jit(solution)/shard_map/ppermute | solution.py:522
  35.9 0.1 add_convert_fusion
  36.0 14.4 %all_to_all.15 = bf16[8,96,128]{2,1,0:T(8,128)(2,1)S(1)} all-to-all(bf16[8,96,128]{2,1,0:T(8,128)(2,1)S(1)} %bitcast.11), channel_id=1, replica_groups={{0,32,64,96,128,160,192,224},{8,40,72,104,136,168,200,232},{16,48,80,11..., dimensions={0} | all-to-all | bytes 393216 | tf_op jit(solution)/shard_map/all_to_all | solution.py:536
  50.5 0.8 broadcast_in_dim.35
  51.3 5.0 %all-to-all-start.1 = ((bf16[16,96,128]{2,1,0:T(8,128)(2,1)}), bf16[16,96,128]{2,1,0:T(8,128)(2,1)S(1)}, u32[]{:S(2)}, u32[]{:S(2)}) async-start(bf16[16,96,128]{2,1,0:T(8,128)(2,1)} %broadcast_in_dim.35), calls=%async_computation.1 | async-start | bytes 786432 | tf_op jit(solution)/shard_map/all_to_all | solution.py:541
  56.3 4.9 %collective-permute-start.5 = (bf16[288,192]{1,0:T(8,128)(2,1)S(1)}, bf16[288,192]{1,0:T(8,128)(2,1)S(1)}, u32[]{:S(2)}, u32[]{:S(2)}) collective-permute-start(bf16[288,192]{1,0:T(8,128)(2,1)S(1)} %get-tuple-element.41), channel_id=1, source_target_pairs={{0,8},{8,16},{16,24},{24,32},{32,40},{40,48},{48,56},{56,64},{64,7... | collective-permute-start | bytes 331784 | tf_op jit(solution)/shard_map/ppermute | solution.py:508
  61.2 3.4 %all-to-all-done.1 = bf16[16,96,128]{2,1,0:T(8,128)(2,1)S(1)} async-done(((bf16[16,96,128]{2,1,0:T(8,128)(2,1)}), bf16[16,96,128]{2,1,0:T(8,128)(2,1)S(1)}, u32[]{:S(2)}, u32[]{:S(2)}) %all-to-all-start.1) | async-done | bytes 393248 | tf_op jit(solution)/shard_map/all_to_all | solution.py:541
  64.6 0.1 multiply_reduce_fusion
  64.7 0.7 broadcast_in_dim.38
  65.4 4.3 %all-to-all-start.2 = ((bf16[8,96,128]{2,1,0:T(8,128)(2,1)}), bf16[8,96,128]{2,1,0:T(8,128)(2,1)S(1)}, u32[]{:S(2)}, u32[]{:S(2)}) async-start(bf16[8,96,128]{2,1,0:T(8,128)(2,1)} %broadcast_in_dim.38), calls=%async_computation.2 | async-start | bytes 393216 | tf_op jit(solution)/shard_map/all_to_all | solution.py:551
  69.7 0.0 collective-permute-done.5.lon_in
  69.7 0.2 merge_lon.1
  69.9 0.1 collective-permute-start.6
  70.0 0.1 collective-permute-start.7
  70.1 0.3 collective-permute-start.8
  70.4 8.0 %all-to-all-done.2 = bf16[8,96,128]{2,1,0:T(8,128)(2,1)S(1)} async-done(((bf16[8,96,128]{2,1,0:T(8,128)(2,1)}), bf16[8,96,128]{2,1,0:T(8,128)(2,1)S(1)}, u32[]{:S(2)}, u32[]{:S(2)}) %all-to-all-start.2) | async-done | bytes 196640 | tf_op jit(solution)/shard_map/all_to_all | solution.py:551
  78.5 3.4 %collective-permute-start.10 = (bf16[768,128]{1,0:T(8,128)(2,1)S(1)}, bf16[768,128]{1,0:T(8,128)(2,1)S(1)}, u32[]{:S(2)}, u32[]{:S(2)}) collective-permute-start(bf16[768,128]{1,0:T(8,128)(2,1)S(1)} %bitcast.7), channel_id=1, source_target_pairs={{0,8},{8,0},{16,24},{24,16},{32,40},{40,32},{48,56},{56,48},{64,72... | collective-permute-start | bytes 589832 | tf_op jit(solution)/shard_map/ppermute | solution.py:522
  81.9 0.0 collective-permute-done.6.lev
  81.9 1.1 %place_grad.1 = f32[2,2,12,24,192]{4,3,2,1,0:T(8,128)} custom-call(bf16[2,9,24,192]{3,2,1,0:T(8,128)(2,1)S(1)} %get-tuple-element.42.own, bf16[2,9,24,192]{3,2,1,0:T(8,128)(2,1)S(1)} %collective-permute-done.6.lev, bf16[2,3,24,192]{3,2,1,0:T(8,128)(2,1)S(1)} %collective-permute-done.7.lat, bf16[2,3,24,192]{3,2,1,0:T(8,128)(2,1)S(1)} %collective-permute-done.8.diag), custom_call_target="tpu_custom_call" | custom-call | flops 20000000000 | bytes 2097152 | tf_op jit(solution)/shard_map/place_grad/pallas_call | solution.py:456
  83.0 1.3 %finish_params.1 = (f32[192,576]{1,0:T(8,128)}, f32[192,192]{1,0:T(8,128)}, f32[1,6,2,3312]{3,2,1,0:T(2,128)}) custom-call(bf16[768,128]{1,0:T(8,128)(2,1)S(1)} %bitcast.8, bf16[768,128]{1,0:T(8,128)(2,1)S(1)} %collective-permute-done.10.other, s32[1,1]{1,0:T(1,128)} %bitcast.2.core), custom_call_target="tpu_custom_call" | custom-call | bytes 2097152 | tf_op jit(solution)/shard_map/finish_params/pallas_call | solution.py:490
  (19 shorter events, 0.2 us)
Async XLA Ops:
  0.6 1.1 %copy-start = (bf16[2,2,12,24,192]{4,3,2,1,0:T(8,128)(2,1)S(1)}, bf16[2,2,12,24,192]{4,3,2,1,0:T(8,128)(2,1)}, u32[]{:S(2)}) copy-start(bf16[2,2,12,24,192]{4,3,2,1,0:T(8,128)(2,1)} %refs_0_.5) | copy-start | bytes 1327108
  1.7 1.1 %copy-start.2 = (bf16[2,2,12,24,192]{4,3,2,1,0:T(8,128)(2,1)S(1)}, bf16[2,2,12,24,192]{4,3,2,1,0:T(8,128)(2,1)}, u32[]{:S(2)}) copy-start(bf16[2,2,12,24,192]{4,3,2,1,0:T(8,128)(2,1)} %refs_1_.5) | copy-start | bytes 1327108
  2.8 7.0 %copy-start.6 = (f32[1,2,6,3312]{3,1,2,0:T(2,128)S(1)}, f32[1,2,6,3312]{3,1,2,0:T(2,128)}, u32[]{:S(2)}) copy-start(f32[1,2,6,3312]{3,1,2,0:T(2,128)} %param.9) | copy-start | bytes 476932
  2.9 10.9 %collective-permute-start = (bf16[2,6,24,384]{3,2,1,0:T(8,128)(2,1)S(1)}, bf16[2,6,24,384]{3,2,1,0:T(8,128)(2,1)S(1)}, u32[]{:S(2)}, u32[]{:S(2)}) collective-permute-start(bf16[2,6,24,384]{3,2,1,0:T(8,128)(2,1)S(1)} %pack_near.1), channel_id=1, source_target_pairs={{0,1},{1,0},{2,3},{3,2},{4,5},{5,4},{6,7},{7,6},{8,9},{9,8},{10,11... | collective-permute-start | bytes 663560 | tf_op jit(solution)/shard_map/ppermute | solution.py:508
  5.2 11.2 %collective-permute-start.1 = (bf16[2,3,24,384]{3,2,1,0:T(8,128)(2,1)S(1)}, bf16[2,3,24,384]{3,2,1,0:T(8,128)(2,1)S(1)}, u32[]{:S(2)}, u32[]{:S(2)}) collective-permute-start(bf16[2,3,24,384]{3,2,1,0:T(8,128)(2,1)S(1)} %get-tuple-element.32), channel_id=1, source_target_pairs={{0,1},{1,0},{2,3},{3,2},{4,5},{5,4},{6,7},{7,6},{8,9},{9,8},{10,11... | collective-permute-start | bytes 331784 | tf_op jit(solution)/shard_map/ppermute | solution.py:508
  5.3 11.1 %collective-permute-start.2 = (bf16[2,3,24,384]{3,2,1,0:T(8,128)(2,1)S(1)}, bf16[2,3,24,384]{3,2,1,0:T(8,128)(2,1)S(1)}, u32[]{:S(2)}, u32[]{:S(2)}) collective-permute-start(bf16[2,3,24,384]{3,2,1,0:T(8,128)(2,1)S(1)} %get-tuple-element.33), channel_id=1, source_target_pairs={{0,6},{2,0},{4,2},{6,4},{1,7},{3,1},{5,3},{7,5},{8,14},{10,8},{12,... | collective-permute-start | bytes 331784 | tf_op jit(solution)/shard_map/ppermute | solution.py:508
  7.9 8.5 %collective-permute-start.3 = (bf16[2,3,24,384]{3,2,1,0:T(8,128)(2,1)S(1)}, bf16[2,3,24,384]{3,2,1,0:T(8,128)(2,1)S(1)}, u32[]{:S(2)}, u32[]{:S(2)}) collective-permute-start(bf16[2,3,24,384]{3,2,1,0:T(8,128)(2,1)S(1)} %get-tuple-element.34), channel_id=1, source_target_pairs={{0,7},{1,6},{2,1},{3,0},{4,3},{5,2},{6,5},{7,4},{8,15},{9,14},{10,... | collective-permute-start | bytes 331784 | tf_op jit(solution)/shard_map/ppermute | solution.py:518
  9.8 3.9 %copy-start.5 = (bf16[192,576]{1,0:T(8,128)(2,1)S(1)}, bf16[192,576]{1,0:T(8,128)(2,1)}, u32[]{:S(2)}) copy-start(bf16[192,576]{1,0:T(8,128)(2,1)} %param.7) | copy-start | bytes 663556
  9.8 4.0 %copy-start.1 = (bf16[2,2,12,24,192]{4,3,2,1,0:T(8,128)(2,1)S(1)}, bf16[2,2,12,24,192]{4,3,2,1,0:T(8,128)(2,1)}, u32[]{:S(2)}) copy-start(bf16[2,2,12,24,192]{4,3,2,1,0:T(8,128)(2,1)} %refs_0_.5) | copy-start | bytes 1327108
  9.8 4.0 %copy-start.3 = (bf16[2,2,12,24,192]{4,3,2,1,0:T(8,128)(2,1)S(1)}, bf16[2,2,12,24,192]{4,3,2,1,0:T(8,128)(2,1)}, u32[]{:S(2)}) copy-start(bf16[2,2,12,24,192]{4,3,2,1,0:T(8,128)(2,1)} %refs_1_.5) | copy-start | bytes 1327108
  9.8 4.0 %copy-start.4 = (bf16[192,192]{1,0:T(8,128)(2,1)S(1)}, bf16[192,192]{1,0:T(8,128)(2,1)}, u32[]{:S(2)}) copy-start(bf16[192,192]{1,0:T(8,128)(2,1)} %refs_5_.5) | copy-start | bytes 221188
  16.6 8.2 %collective-permute-start.4 = (bf16[288,384]{1,0:T(8,128)(2,1)S(1)}, bf16[288,384]{1,0:T(8,128)(2,1)S(1)}, u32[]{:S(2)}, u32[]{:S(2)}) collective-permute-start(bf16[288,384]{1,0:T(8,128)(2,1)S(1)} %pack_lon.1), channel_id=1, source_target_pairs={{0,248},{8,0},{16,8},{24,16},{32,24},{40,32},{48,40},{56,48},{64,5... | collective-permute-start | bytes 663560 | tf_op jit(solution)/shard_map/ppermute | solution.py:508
  30.9 5.0 %collective-permute-start.9 = (bf16[768,128]{1,0:T(8,128)(2,1)S(1)}, bf16[768,128]{1,0:T(8,128)(2,1)S(1)}, u32[]{:S(2)}, u32[]{:S(2)}) collective-permute-start(bf16[768,128]{1,0:T(8,128)(2,1)S(1)} %get-tuple-element.50), channel_id=1, source_target_pairs={{0,8},{8,0},{16,24},{24,16},{32,40},{40,32},{48,56},{56,48},{64,72... | collective-permute-start | bytes 589832 | tf_op jit(solution)/shard_map/ppermute | solution.py:522
  51.3 13.3 %all-to-all-start.1 = ((bf16[16,96,128]{2,1,0:T(8,128)(2,1)}), bf16[16,96,128]{2,1,0:T(8,128)(2,1)S(1)}, u32[]{:S(2)}, u32[]{:S(2)}) async-start(bf16[16,96,128]{2,1,0:T(8,128)(2,1)} %broadcast_in_dim.35), calls=%async_computation.1 | async-start | bytes 786432 | tf_op jit(solution)/shard_map/all_to_all | solution.py:541
  56.3 13.4 %collective-permute-start.5 = (bf16[288,192]{1,0:T(8,128)(2,1)S(1)}, bf16[288,192]{1,0:T(8,128)(2,1)S(1)}, u32[]{:S(2)}, u32[]{:S(2)}) collective-permute-start(bf16[288,192]{1,0:T(8,128)(2,1)S(1)} %get-tuple-element.41), channel_id=1, source_target_pairs={{0,8},{8,16},{16,24},{24,32},{32,40},{40,48},{48,56},{56,64},{64,7... | collective-permute-start | bytes 331784 | tf_op jit(solution)/shard_map/ppermute | solution.py:508
  65.4 13.1 %all-to-all-start.2 = ((bf16[8,96,128]{2,1,0:T(8,128)(2,1)}), bf16[8,96,128]{2,1,0:T(8,128)(2,1)S(1)}, u32[]{:S(2)}, u32[]{:S(2)}) async-start(bf16[8,96,128]{2,1,0:T(8,128)(2,1)} %broadcast_in_dim.38), calls=%async_computation.2 | async-start | bytes 393216 | tf_op jit(solution)/shard_map/all_to_all | solution.py:551
  69.9 11.9 %collective-permute-start.6 = (bf16[2,9,24,192]{3,2,1,0:T(8,128)(2,1)S(1)}, bf16[2,9,24,192]{3,2,1,0:T(8,128)(2,1)S(1)}, u32[]{:S(2)}, u32[]{:S(2)}) collective-permute-start(bf16[2,9,24,192]{3,2,1,0:T(8,128)(2,1)S(1)} %get-tuple-element.43), channel_id=1, source_target_pairs={{0,1},{1,0},{2,3},{3,2},{4,5},{5,4},{6,7},{7,6},{8,9},{9,8},{10,11... | collective-permute-start | bytes 497672 | tf_op jit(solution)/shard_map/ppermute | solution.py:508
  70.0 11.8 %collective-permute-start.7 = (bf16[2,3,24,192]{3,2,1,0:T(8,128)(2,1)S(1)}, bf16[2,3,24,192]{3,2,1,0:T(8,128)(2,1)S(1)}, u32[]{:S(2)}, u32[]{:S(2)}) collective-permute-start(bf16[2,3,24,192]{3,2,1,0:T(8,128)(2,1)S(1)} %get-tuple-element.44), channel_id=1, source_target_pairs={{0,2},{2,4},{4,6},{6,0},{1,3},{3,5},{5,7},{7,1},{8,10},{10,12},{12... | collective-permute-start | bytes 165896 | tf_op jit(solution)/shard_map/ppermute | solution.py:508
  70.1 11.7 %collective-permute-start.8 = (bf16[2,3,24,192]{3,2,1,0:T(8,128)(2,1)S(1)}, bf16[2,3,24,192]{3,2,1,0:T(8,128)(2,1)S(1)}, u32[]{:S(2)}, u32[]{:S(2)}) collective-permute-start(bf16[2,3,24,192]{3,2,1,0:T(8,128)(2,1)S(1)} %get-tuple-element.45), channel_id=1, source_target_pairs={{0,3},{1,2},{2,5},{3,4},{4,7},{5,6},{6,1},{7,0},{8,11},{9,10},{10,... | collective-permute-start | bytes 165896 | tf_op jit(solution)/shard_map/ppermute | solution.py:518
  78.5 4.5 %collective-permute-start.10 = (bf16[768,128]{1,0:T(8,128)(2,1)S(1)}, bf16[768,128]{1,0:T(8,128)(2,1)S(1)}, u32[]{:S(2)}, u32[]{:S(2)}) collective-permute-start(bf16[768,128]{1,0:T(8,128)(2,1)S(1)} %bitcast.7), channel_id=1, source_target_pairs={{0,8},{8,0},{16,24},{24,16},{32,40},{40,32},{48,56},{56,48},{64,72... | collective-permute-start | bytes 589832 | tf_op jit(solution)/shard_map/ppermute | solution.py:522

commit v4 on v3

--- a/solution.py
+++ b/solution.py
@@ -66,183 +66,182 @@
     )
 
 
-def pack_near_kernel(f, u, near):
+def both_lines(f, u, b, level, row):
+    return join(f[b, level, row].astype(F32), u[b, level, row].astype(F32))
+
+
+def pack_lev_kernel(f, u, out, tmp):
     for b in range(2):
-        for h in range(6):
-            near[b, h] = join(f[b, 0, h + 3], u[b, 0, h + 3])
-
-
-def pack_near(fields, upstream):
-    return pl.pallas_call(
-        pack_near_kernel,
-        name="pack_near",
-        out_shape=shape((2, 6, 24, BOTH), BF),
+        for r in range(9):
+            tmp[b, r * 18 : r * 18 + 18, :] = both_lines(f, u, b, 0, r + 3)[6:24]
+    out[...] = tmp[...].astype(BF)
+
+
+def pack_lev(fields, upstream):
+    return pl.pallas_call(
+        pack_lev_kernel,
+        name="pack_lev",
+        out_shape=shape((2, 162, BOTH), BF),
         in_specs=[VMEM] * 2,
         out_specs=VMEM,
+        scratch_shapes=[pltpu.VMEM((2, 162, BOTH), F32)],
         compiler_params=params(16),
         cost_estimate=cost(0, 2 * 1024 * 1024),
     )(fields, upstream)
 
 
-def pack_rest_kernel(f, u, far, lat, diag):
+def pack_lon_kernel(f, u, out, tmp):
     for b in range(2):
-        for r in range(3):
-            far[b, r] = join(f[b, 0, r + 9], u[b, 0, r + 9])
-            lat[b, r] = join(f[b, 1, r], u[b, 1, r])
-            diag[b, r] = join(f[b, 0, r], u[b, 0, r])
-
-
-def pack_rest(fields, upstream):
+        for level in range(2):
+            for row in range(12):
+                at = (level * 12 + row) * 6
+                tmp[b, at : at + 6, :] = both_lines(f, u, b, level, row)[0:6]
+    out[...] = tmp[...].astype(BF)
+
+
+def pack_lon(fields, upstream):
+    return pl.pallas_call(
+        pack_lon_kernel,
+        name="pack_lon",
+        out_shape=shape((2, WIN, BOTH), BF),
+        in_specs=[VMEM] * 2,
+        out_specs=VMEM,
+        scratch_shapes=[pltpu.VMEM((2, WIN, BOTH), F32)],
+        compiler_params=params(16),
+        cost_estimate=cost(0, 2 * 1024 * 1024),
+    )(fields, upstream)
+
+
+def pack_rest_kernel(f, u, lon, diag, edge, lat):
+    for b in range(2):
+        halo = lon[b].astype(F32)
+        for level, out in ((0, diag), (1, lat)):
+            for row in range(3):
+                at = (level * 12 + row) * 6
+                line = both_lines(f, u, b, level, row)
+                out[b, row] = jnp.concatenate([line[6:24], halo[at : at + 6]], axis=0).astype(BF)
+        edge[b] = halo[18:72].astype(BF)
+
+
+def pack_rest(fields, upstream, lon):
     return pl.pallas_call(
         pack_rest_kernel,
         name="pack_rest",
-        out_shape=(shape((2, 3, 24, BOTH), BF),) * 3,
-        in_specs=[VMEM] * 2,
+        out_shape=(
+            shape((2, 3, 24, BOTH), BF), shape((2, 54, BOTH), BF), shape((2, 3, 24, BOTH), BF)
+        ),
+        in_specs=[VMEM] * 3,
         out_specs=(VMEM,) * 3,
         compiler_params=params(16),
         cost_estimate=cost(0, 2 * 1024 * 1024),
-    )(fields, upstream)
-
-
-def source_lines(own, halos, aw, b, z, h):
-    if z == 0 and (aw == 0 or h < 3):
-        return [a[b, 1, 6 * aw + h + 3].astype(F32) for a in own]
-    if aw == 0:
-        line = halos[0][b, h]
-    elif z == 0:
-        line = halos[2][b, h - 3]
-    else:
-        line = halos[1][b, h] if h < 3 else halos[3][b, h - 3]
-    return split(line.astype(F32))
-
-
-def pack_lon_kernel(f, u, near, far, lat, diag, after, out, tmp):
-    for b in range(2):
-        for z in range(2):
-            for r in range(12):
-                lines = source_lines((f, u), (near, far, lat, diag), r // 6, b, z, r % 6)
-                row = b * WIN + (z * 12 + r) * 6
-                tmp[row : row + 6, :] = join(lines[0][0:6], lines[1][0:6])
-    out[...] = tmp[...].astype(BF)
-
-
-def pack_lon(fields, upstream, halos, after):
-    return pl.pallas_call(
-        pack_lon_kernel,
-        name="pack_lon",
-        out_shape=shape((2 * WIN, BOTH), BF),
-        in_specs=[VMEM] * 6 + [HBM],
-        out_specs=VMEM,
-        scratch_shapes=[pltpu.VMEM((2 * WIN, BOTH), F32)],
-        compiler_params=params(16),
-        cost_estimate=cost(0, 2 * 1024 * 1024),
-    )(fields, upstream, *halos, after)
+    )(fields, upstream, lon)
 
 
 def onehot_rows(target, w1):
-    lane = lax.broadcasted_iota(jnp.int32, (LANES, KEYS), 0)
-    return jnp.where(lane == target + w1, 1.0, 0.0).astype(BF)
-
-
-def expand_kernel(eb, target, rq, rk, out0, out1, spread, out_a, out_b):
+    row = lax.broadcasted_iota(jnp.int32, (KEYS, target.shape[1]), 0)
+    return jnp.where(row == target + w1, 1.0, 0.0).astype(BF)
+
+
+def expand_kernel(eb, target, region_k, region_q, out0, out1, spread, wide):
     spread[...] = jnp.zeros_like(spread)
     for z1 in range(2):
         for h1 in range(6):
-            g = z1 * 6 + h1
             for z2 in range(2):
                 off = ((z1 * 2 + z2) * 6 + h1) * GROUP
                 for aw in range(2):
-                    spread[g * 16 + aw * 6 : g * 16 + aw * 6 + 6, z2 * GROUP : (z2 + 1) * GROUP] = eb[
-                        0, aw, :, off : off + GROUP
-                    ]
+                    at = (z1 * 6 + h1) * 24 + (z2 * 2 + aw) * 6
+                    spread[at : at + 6, 0:GROUP] = eb[0, aw, :, off : off + GROUP]
     full = spread[...]
     high = full.astype(BF)
     rest = full - high.astype(F32)
     mid = rest.astype(BF)
     low = (rest - mid.astype(F32)).astype(BF)
-    row = lax.broadcasted_iota(jnp.int32, (12, 1), 0)
     tgt = target[...]
     for w1 in range(WW):
         hot = onehot_rows(tgt, w1)
         block = dot(high, hot) + (dot(mid, hot) + dot(low, hot))
         for g in range(12):
-            q = g * 12 + w1
-            part = block[g * 16 : g * 16 + 12]
-            ok0 = rq[0, q : q + 1, :] == rk[0]
-            ok1 = rq[1, q : q + 1, :] == rk[1]
-            ok = ((row < 6) & ok0) | ((row >= 6) & ok1)
-            part = jnp.where(ok, part, NEG_FILL)
-            out_a[pl.ds(q, 12, stride=WIN), :] = part[:, 0:128]
-            out_b[pl.ds(q, 12, stride=WIN), :] = part[:, 128:256]
+            wide[pl.ds(g * 12 + w1, 24, stride=WIN), :] = block[g * 24 : g * 24 + 24]
     for aw, out in enumerate((out0, out1)):
-        tails = []
-        for h in range(HEADS):
-            rows = slice((aw * HEADS + h) * WIN, (aw * HEADS + h + 1) * WIN)
-            turned = jnp.concatenate([out_a[rows, :], out_b[rows, 0:16]], axis=1).T
-            out[:, h * MAIN : (h + 1) * MAIN] = turned[:, 0:MAIN]
-            tails.append(turned[:, MAIN:WIN])
-        tails.append(jnp.zeros((WIN, SPREAD - HEADS * WIN), F32))
-        out[:, TAILS:SPREAD] = jnp.concatenate(tails, axis=1)
-
-
-def expand(earth_bias, target, rq, rk):
+        for z2 in range(2):
+            keys = slice(z2 * 72, z2 * 72 + 72)
+            ok = region_k[aw, keys, :] == region_q[aw]
+            tails = []
+            for h in range(HEADS):
+                at = ((z2 * 2 + aw) * HEADS + h) * WIN
+                turned = wide[at : at + WIN, 0:72].T
+                out[keys, h * MAIN : (h + 1) * MAIN] = jnp.where(
+                    ok[:, 0:MAIN], turned[:, 0:MAIN], NEG_FILL
+                )
+                tails.append(turned[:, MAIN:WIN])
+            tails.append(jnp.zeros((72, SPREAD - HEADS * WIN), F32))
+            out[keys, TAILS:SPREAD] = jnp.where(
+                ok[:, MAIN:], jnp.concatenate(tails, axis=1), NEG_FILL
+            )
+
+
+def expand(earth_bias, target, region_k, region_q):
     return pl.pallas_call(
         expand_kernel,
         name="expand_bias",
         out_shape=(shape((WIN, SPREAD), F32),) * 2,
         in_specs=[VMEM] * 4,
         out_specs=(VMEM,) * 2,
-        scratch_shapes=[
-            pltpu.VMEM((192, LANES), F32),
-            pltpu.VMEM((12 * WIN, 128), F32),
-            pltpu.VMEM((12 * WIN, 128), F32),
-        ],
+        scratch_shapes=[pltpu.VMEM((288, KEYS), F32), pltpu.VMEM((24 * WIN, 128), F32)],
         compiler_params=params(16),
         cost_estimate=cost(4 * 10**9, 4 * 1024 * 1024),
-    )(earth_bias, target, rq, rk)
-
-
-def windows_kernel(aws, second, *refs):
+    )(earth_bias, target, region_k, region_q)
+
+
+def windows_kernel(aw, seconds, *refs):
     refs = list(refs)
     take = lambda n: [refs.pop(0) for _ in range(n)]
-    f, u, wq, wk, wv, wo = take(6)
-    biases = dict(zip(aws, take(len(aws))))
-    near = take(1) if 0 in aws else [None]
-    halos = near + (take(3) if 1 in aws else [])
-    if second:
-        (lon,) = take(1)
-    started = second or 1 in aws
-    if started:
+    f, u, wqkv, wo, bias, inner = take(6)
+    if aw == 1:
+        lat, diag = take(2)
+    if True in seconds:
+        lon, edge = take(2)
         (w_in,) = take(1)
-    if second:
-        gb_in = take(len(aws))
-    grads, w_s = take(2)
-    gbs = dict(zip(aws, take(len(aws))))
-    if second:
+    (other,) = take(1) if True in seconds else (None,)
+    grads, w_s, gb_s = take(3)
+    if aw == 1:
         (lon_back,) = take(1)
     x_s, u_s, i_s, low_s, q_s, k_s, v_s, ga_s, gq_s, gk_s, gv_s, att_s, up_s = take(13)
-    if second:
+    if aw == 1:
         g_s, lon_s = take(2)
-    w_s[...] = w_in[...] if started else jnp.zeros_like(w_s)
-    for n, aw in enumerate(aws):
-        gbs[aw][...] = gb_in[n][...] if second else jnp.zeros_like(gbs[aw])
-
-    for n, aw in enumerate(aws):
-        for b in range(2):
-            if second:
-                halo = split(lon[b * WIN : (b + 1) * WIN, :].astype(F32))
+    w_s[...] = w_in[...] if True in seconds else jnp.zeros_like(w_s)
+    gb_s[...] = other[...] if aw == 0 and True in seconds else jnp.zeros_like(gb_s)
+
+    def put(row, pair):
+        for value, dst in zip(pair, (x_s, u_s)):
+            dst[row : row + value.shape[0], :] = value
+
+    for b in range(2):
+        lines = inner[b].astype(F32)
+        if True in seconds:
+            at_lon, at_edge = lon[b].astype(F32), edge[b].astype(F32)
+        for n, second in enumerate(seconds):
             for z in range(2):
                 for h in range(6):
-                    lines = source_lines((f, u), halos, aw, b, z, h)
+                    r = aw * 6 + h
                     row = (n * 2 + b) * WIN + z * 72 + h * 12
-                    hrow = (z * 12 + aw * 6 + h) * 6
-                    for t, dst in enumerate((x_s, u_s)):
-                        if second:
-                            dst[row : row + 6, :] = lines[t][18:24]
-                            dst[row + 6 : row + 12, :] = halo[t][hrow : hrow + 6]
-                        else:
-                            dst[row : row + 12, :] = lines[t][6:18]
-
+                    if r >= 9:
+                        line = (diag if z else lat)[b, r - 9].astype(F32)
+                        put(row, split(line[12:24] if second else line[0:12]))
+                        continue
+                    if z:
+                        line = split(lines[r * 18 : r * 18 + 18])
+                    else:
+                        line = [a[b, 1, r + 3].astype(F32)[6:24] for a in (f, u)]
+                    if second:
+                        put(row, [a[12:18] for a in line])
+                        halo = at_edge[r * 6 : r * 6 + 6] if z else at_lon[(r + 15) * 6 : (r + 16) * 6]
+                        put(row + 6, split(halo))
+                    else:
+                        put(row, [a[0:12] for a in line])
+
+    weights = wqkv[...].astype(F32)
+    wq, wk, wv = [weights[:, i * C : (i + 1) * C].astype(BF) for i in range(3)]
     raw = x_s[...]
     centred = raw - jnp.mean(raw, axis=-1, keepdims=True)
     inv_std = lax.rsqrt(jnp.mean(centred * centred, axis=-1, keepdims=True) + EPS)
@@ -251,14 +250,14 @@
     x_s[...] = normed
     i_s[...] = inv_std
     low_s[...] = low
-    q_s[...] = dot(low, wq[...]).astype(BF)
-    k_s[...] = dot(low, wk[...]).astype(BF)
-    v_s[...] = dot(low, wv[...]).astype(BF)
+    q_s[...] = dot(low, wq).astype(BF)
+    k_s[...] = dot(low, wk).astype(BF)
+    v_s[...] = dot(low, wv).astype(BF)
     up = u_s[...].astype(BF)
     ga_s[...] = dot(up, wo[...], 1, 1).astype(BF)
     att_s[...] = jnp.zeros_like(att_s)
     up_s[...] = jnp.zeros_like(up_s)
-    for w in range(2 * len(aws)):
+    for w in range(2 * len(seconds)):
         up_s[w * KEYS : w * KEYS + WIN, :] = up[w * WIN : (w + 1) * WIN]
 
     lane = lax.broadcasted_iota(jnp.int32, (1, C), 1)
@@ -284,9 +283,8 @@
                 heads.append(jnp.concatenate([main, tail], axis=1))
         return jnp.concatenate(heads, axis=0)
 
-    for w in range(2 * len(aws)):
+    for w in range(2 * len(seconds)):
         rows = slice(w * WIN, (w + 1) * WIN)
-        bias, gb_s = biases[aws[w // 2]], gbs[aws[w // 2]]
         low, q, k, v, ga = low_s[rows, :], q_s[rows, :], k_s[rows, :], v_s[rows, :], ga_s[rows, :]
         qs = stack(q)
         gas = stack(ga)
@@ -316,16 +314,17 @@
     w_s[0:C, :] += dot(low_t, gq)
     w_s[C : 2 * C, :] += dot(low_t, gk)
     w_s[2 * C : 3 * C, :] += dot(low_t, gv)
-    gu = dot(gq, wq[...], 1, 1) + dot(gk, wk[...], 1, 1) + dot(gv, wv[...], 1, 1)
+    gu = dot(gq, wq, 1, 1) + dot(gk, wk, 1, 1) + dot(gv, wv, 1, 1)
     normed = x_s[...]
     centre = jnp.mean(gu, axis=-1, keepdims=True)
     along = jnp.mean(gu * normed, axis=-1, keepdims=True)
     grad = i_s[...] * (gu - centre - normed * along)
     grads[...] = grad.astype(BF)
-    if not second:
+    if aw == 0:
         return
 
-    g_s[...] = grad
+    g_s[0:PAIR, :] = other[...].astype(F32)
+    g_s[PAIR : 2 * PAIR, :] = grad[PAIR : 2 * PAIR]
     for b in range(2):
         for z in range(2):
             for r in range(12):
@@ -348,11 +347,10 @@
                 turned[at + MAIN : at + WIN, 0:72] = tails[h * TAIL : (h + 1) * TAIL]
     folded = jnp.zeros((288, KEYS), F32)
     tgt = target[...]
-    lane = lax.broadcasted_iota(jnp.int32, (KEYS, 72), 0)
     for w1 in range(WW):
         rows = [turned[pl.ds(g * 12 + w1, 24, stride=WIN), :] for g in range(12)]
         full = jnp.concatenate(rows, axis=0)[:, 0:72].astype(BF)
-        hot = jnp.where(lane == tgt[:, 0:72] + w1, 1.0, 0.0).astype(BF)
+        hot = onehot_rows(tgt[:, 0:72], w1)
         folded = folded + dot(full, hot, 1, 1)
     slab[1152:1440, :] = folded[:, 0:128].astype(BF)
     rest = [folded[24 * i : 24 * i + 24, 128:138] for i in range(12)]
@@ -379,35 +377,36 @@
     )(w, gb0, gb1, target, core)
 
 
-def windows(aws, second, *args):
-    tokens = len(aws) * PAIR
+def windows(aw, seconds, *args):
+    tokens = len(seconds) * PAIR
+    padded = 2 * len(seconds) * KEYS
     rows = [pltpu.VMEM((tokens, C), F32)] * 2 + [pltpu.VMEM((tokens, 1), F32)]
     rows += [pltpu.VMEM((tokens, C), BF)] * 8
-    padded = 2 * len(aws) * KEYS
     rows += [pltpu.VMEM((C, padded), BF), pltpu.VMEM((padded, C), BF)]
-    outs = (shape((tokens, C), BF), shape((4 * C, C), F32))
-    outs += (shape((WIN, SPREAD), F32),) * len(aws)
-    if second:
+    outs = (shape((tokens, C), BF), shape((4 * C, C), F32), shape((WIN, SPREAD), F32))
+    if aw == 1:
         outs += (shape((2 * WIN, C), BF),)
-        rows += [pltpu.VMEM((tokens, C), F32), pltpu.VMEM((2 * WIN, C), F32)]
-    return pl.pallas_call(
-        functools.partial(windows_kernel, aws, second),
-        name="windows_second" if second else "windows_upper" if 1 in aws else "windows_lower",
+        rows += [pltpu.VMEM((2 * PAIR, C), F32), pltpu.VMEM((2 * WIN, C), F32)]
+    return pl.pallas_call(
+        functools.partial(windows_kernel, aw, seconds),
+        name="windows_upper" if aw else "windows_lower_second" if seconds[0] else "windows_lower_first",
         out_shape=outs,
         in_specs=[VMEM] * len(args),
         out_specs=(VMEM,) * len(outs),
         scratch_shapes=rows,
         compiler_params=params(28),
-        cost_estimate=cost(3 * 10**9 * len(aws), 4 * 1024 * 1024),
+        cost_estimate=cost(3 * 10**9 * len(seconds), 4 * 1024 * 1024),
     )(*args)
 
 
-def merge_kernel(g_lower, g_upper, g_second, lon_in, own, lev, lat, diag):
+def merge_kernel(g_first, g_second, g_upper, lon_in, own, lev, lat, diag):
     for b in range(2):
         halo = lon_in[b * WIN : (b + 1) * WIN, :].astype(F32)
-        for aw, g_first in enumerate((g_lower, g_upper)):
-            first = g_first[b * WIN : (b + 1) * WIN, :].astype(F32)
-            second = g_second[(aw * 2 + b) * WIN : (aw * 2 + b + 1) * WIN, :].astype(F32)
+        for aw in range(2):
+            at = slice(b * WIN, (b + 1) * WIN)
+            after = slice(PAIR + b * WIN, PAIR + (b + 1) * WIN)
+            first = (g_upper if aw else g_first)[at, :].astype(F32)
+            second = (g_upper[after, :] if aw else g_second[at, :]).astype(F32)
             for z in range(2):
                 for h in range(6):
                     r = aw * 6 + h
@@ -555,15 +554,16 @@
 
 
 def body(fields, upstream, qkv_weight, out_weight, earth_bias):
-    near = from_behind(pack_near(fields, upstream), "lev", -1)
-    far_msg, lat_msg, diag_msg = pack_rest(fields, upstream)
-    far = from_behind(far_msg, "lev", -1)
+    inner = from_behind(pack_lev(fields, upstream), "lev", -1)
+    lon = from_behind(pack_lon(fields, upstream), "lon", -1)
+    diag_msg, edge_msg, lat_msg = pack_rest(fields, upstream, lon)
+    diag = from_corner(diag_msg, -1)
+    edge = from_behind(edge_msg, "lev", -1)
     lat = from_behind(lat_msg, "lat", -1)
-    diag = from_corner(diag_msg, -1)
 
     key = jnp.arange(WIN, dtype=jnp.int32)
     target = (key // WW) * OFFS - key % WW + WW - 1
-    target = jnp.concatenate([target, jnp.full((KEYS - WIN,), -1000, jnp.int32)])[None, :]
+    target = target[None, :MAIN]
     last_lev = lax.axis_index("lev") == lax.axis_size("lev") - 1
     last_lat = lax.axis_index("lat") == lax.axis_size("lat") - 1
     lev_flag = ((key // 72) == 1) & last_lev
@@ -571,25 +571,25 @@
     region = jnp.stack(
         [2 * lev_flag.astype(F32), 2 * lev_flag.astype(F32) + lat_flag.astype(F32)]
     )
-    keys = jnp.concatenate([region, jnp.zeros((2, KEYS - WIN), F32)], axis=1)
-    bias0, bias1 = expand(earth_bias, target, region[:, :, None], keys[:, None, :])
+    ends = jnp.tile(region[:, MAIN:], (1, HEADS))
+    pad = jnp.zeros((2, SPREAD - HEADS * WIN), F32)
+    along = jnp.concatenate([region[:, :MAIN], ends, pad], axis=1)
+    bias0, bias1 = expand(earth_bias, target, region[:, :, None], along[:, None, :])
     core = (lax.axis_index("lon") % 2).astype(jnp.int32).reshape(1, 1)
 
     shared = (
         fields, upstream,
-        qkv_weight[:, 0:C], qkv_weight[:, C : 2 * C], qkv_weight[:, 2 * C :], out_weight,
+        qkv_weight, out_weight,
     )
-    g_lower, w, gb0 = windows((0,), False, *shared, bias0, near)
-    rest = (far, lat, diag)
-    lon = from_behind(pack_lon(fields, upstream, (near,) + rest, g_lower), "lon", -1)
-    g_upper, w, gb1 = windows((1,), False, *shared, bias1, *rest, w)
-    g_second, w, gb0, gb1, lon_back = windows(
-        (0, 1), True, *shared, bias0, bias1, near, *rest, lon, w, gb0, gb1
+    g_first, w, gb0 = windows(0, (False,), *shared, bias0, inner)
+    g_second, w, gb0 = windows(0, (True,), *shared, bias0, inner, lon, edge, w, gb0)
+    g_upper, w, gb1, lon_back = windows(
+        1, (False, True), *shared, bias1, inner, lat, diag, lon, edge, w, g_second
     )
     keep, send = fold(w, gb0, gb1, target, core)
     half, other = reduce_slab(keep, send)
     lon_in = from_behind(lon_back, "lon", 1)
-    own, lev_out, lat_out, diag_out = merge(g_lower, g_upper, g_second, lon_in)
+    own, lev_out, lat_out, diag_out = merge(g_first, g_second, g_upper, lon_in)
     lev_in = from_behind(lev_out, "lev", 1)
     lat_in = from_behind(lat_out, "lat", 1)
     diag_in = from_corner(diag_out, 1)

time: 84.6 us -> 82.8 us (0.979)
  waiting for transfers between devices: 16 us -> 14.6 us
  starting transfers between devices: 30.6 us -> 31.8 us
  Pallas kernels: 18 us -> 16.9 us
    ppermute x7, starting transfers between devices: 12 us -> 13.6 us  [from_behind(): lax.ppermute(x, axis, [(i, (i + by) % devices) for i in range(devices)])]
    ppermute x2, starting transfers between devices: 1.88 us -> 0.44 us  [from_corner(): return lax.ppermute(x, ('lat', 'lev'), pairs)]
    pallas_call x1, Pallas kernels: 3.83 us -> 2.68 us  [expand(): pl.pallas_call(expand_kernel, name='expand_bias', out_shape=(shape((WIN,...]
    ppermute x7, waiting for transfers between devices: 3.54 us -> 2.58 us  [from_behind(): lax.ppermute(x, axis, [(i, (i + by) % devices) for i in range(devices)])]
  transfers between devices with their start and end apart: 13 -> 13, of which waited for: 4 -> 4; matrix products, arithmetic and copies ran while one was open for 1% -> 2% of each run, Pallas kernels for 12% -> 12%
where the time goes in v4:
time: 82.8 us; the launch traced here: 82.4 us
  starting transfers between devices  31.8 us (38%)
  Pallas kernels  16.9 us (20%)
  waiting for transfers between devices  14.6 us (18%)
  blocking collectives  13.8 us (17%)
  local copies, waits for them, and re-layouts  3.99 us (5%)
  between operations  0.95 us (1%)
    all_to_all x1, blocking collectives, reduce_slab(): lax.all_to_all(half.reshape(depth, rows, 128), 'lon', 0, 0, axis_index_gr...  13.8 us
    ppermute x7, starting transfers between devices, from_behind(): lax.ppermute(x, axis, [(i, (i + by) % devices) for i in range(devices)])  13.6 us
    pallas_call x3, Pallas kernels, windows(): pl.pallas_call(functools.partial(windows_kernel, aw, seconds), name='wind...  10.1 us
    all_to_all x1, waiting for transfers between devices, reduce_slab(): lax.all_to_all(jnp.broadcast_to(mine[None], (depth, rows, 128)), 'lon', 0...  8.28 us
    ppermute x2, starting transfers between devices, other_core(): lax.ppermute(x, 'lon', [(i, i ^ 1) for i in range(lax.axis_size('lon'))])  7.73 us
    all_to_all x1, starting transfers between devices, reduce_slab(): lax.all_to_all(jnp.broadcast_to(mine[None], (depth, rows, 128)), 'lon', 0...  5.16 us
    all_to_all x1, starting transfers between devices, reduce_slab(): lax.all_to_all(jnp.broadcast_to(mine[None], (count, rows, 128)), ('lon',...  4.85 us
    pallas_call x1, Pallas kernels, expand(): pl.pallas_call(expand_kernel, name='expand_bias', out_shape=(shape((WIN,...  2.68 us
  transfers between devices with their start and end apart: 13, of which 4 were waited for; matrix products, arithmetic and copies ran while one was open for 2% of the time, Pallas kernels for 12%

profile of v4, /device:TPU:1, one launch (start us, length us, event | category | flops | bytes accessed | tf_op | source)
XLA Modules:
  0.0 82.4 jit_solution(15671000797664180587)
XLA Ops:
  0.6 0.0 copy-start
  0.6 1.1 %copy-done = bf16[2,2,12,24,192]{4,3,2,1,0:T(8,128)(2,1)S(1)} copy-done((bf16[2,2,12,24,192]{4,3,2,1,0:T(8,128)(2,1)S(1)}, bf16[2,2,12,24,192]{4,3,2,1,0:T(8,128)(2,1)}, u32[]{:S(2)}) %copy-start) | copy-done | bytes 442392
  1.7 1.1 %copy-done.2 = bf16[2,2,12,24,192]{4,3,2,1,0:T(8,128)(2,1)S(1)} copy-done((bf16[2,2,12,24,192]{4,3,2,1,0:T(8,128)(2,1)S(1)}, bf16[2,2,12,24,192]{4,3,2,1,0:T(8,128)(2,1)}, u32[]{:S(2)}) %copy-start.2) | copy-done | bytes 442392
  2.8 0.1 pack_lon.1
  2.9 0.0 copy-start.6
  2.9 3.3 %collective-permute-start.1 = (bf16[2,144,384]{2,1,0:T(8,128)(2,1)S(1)}, bf16[2,144,384]{2,1,0:T(8,128)(2,1)S(1)}, u32[]{:S(2)}, u32[]{:S(2)}) collective-permute-start(bf16[2,144,384]{2,1,0:T(8,128)(2,1)S(1)} %pack_lon.1), channel_id=1, source_target_pairs={{0,248},{8,0},{16,8},{24,16},{32,24},{40,32},{48,40},{56,48},{64,5... | collective-permute-start | bytes 663560 | tf_op jit(solution)/shard_map/ppermute | solution.py:507
  6.2 0.1 pack_lev.1
  6.3 0.1 collective-permute-start
  6.6 0.1 tile.10
  6.6 0.1 pad.2.clone
  6.7 0.1 copy.14.region_k
  6.9 0.0 copy-start.1
  6.9 0.0 copy-start.3
  7.0 2.7 %expand_bias.1 = (f32[144,896]{1,0:T(8,128)S(1)}, f32[144,896]{1,0:T(8,128)S(1)}) custom-call(f32[1,2,6,3312]{3,2,1,0:T(8,128)S(1)} %copy.13.eb, s32[1,128]{1,0:T(1,128)S(1)} %slice_bitcast_fusion.target, f32[2,144,1]{2,1,0:T(8,128)S(1)} %copy.14.region_k, f32[2,1,256]{2,1,0:T(1,128)S(1)} %broadcast_in_dim.38.region_q), custom_call_target="tpu_custom_call" | custom-call | flops 4000000000 | bytes 4194304 | tf_op jit(solution)/shard_map/expand_bias/pallas_call | solution.py:184
  9.6 0.0 copy-start.4
  9.7 0.0 copy-start.5
  9.7 2.6 %collective-permute-done.1.lon.refs_6_.refs_8_ = bf16[2,144,384]{2,1,0:T(8,128)(2,1)S(1)} collective-permute-done((bf16[2,144,384]{2,1,0:T(8,128)(2,1)S(1)}, bf16[2,144,384]{2,1,0:T(8,128)(2,1)S(1)}, u32[]{:S(2)}, u32[]{:S(2)}) %collective-permute-start.1) | collective-permute-done | bytes 221216 | tf_op jit(solution)/shard_map/ppermute | solution.py:507
  12.2 0.1 pack_rest.1
  12.4 2.2 %collective-permute-start.2 = (bf16[2,54,384]{2,1,0:T(8,128)(2,1)S(1)}, bf16[2,54,384]{2,1,0:T(8,128)(2,1)S(1)}, u32[]{:S(2)}, u32[]{:S(2)}) collective-permute-start(bf16[2,54,384]{2,1,0:T(8,128)(2,1)S(1)} %get-tuple-element.30), channel_id=1, source_target_pairs={{0,1},{1,0},{2,3},{3,2},{4,5},{5,4},{6,7},{7,6},{8,9},{9,8},{10,11... | collective-permute-start | bytes 248840 | tf_op jit(solution)/shard_map/ppermute | solution.py:507
  14.5 2.5 %collective-permute-start.3 = (bf16[2,3,24,384]{3,2,1,0:T(8,128)(2,1)S(1)}, bf16[2,3,24,384]{3,2,1,0:T(8,128)(2,1)S(1)}, u32[]{:S(2)}, u32[]{:S(2)}) collective-permute-start(bf16[2,3,24,384]{3,2,1,0:T(8,128)(2,1)S(1)} %get-tuple-element.35), channel_id=1, source_target_pairs={{0,6},{2,0},{4,2},{6,4},{1,7},{3,1},{5,3},{7,5},{8,14},{10,8},{12,... | collective-permute-start | bytes 331784 | tf_op jit(solution)/shard_map/ppermute | solution.py:507
  17.0 0.4 collective-permute-start.4
  17.4 0.0 collective-permute-done.refs_5_
  17.4 2.7 %windows_lower_first.1 = (bf16[288,192]{1,0:T(8,128)(2,1)S(1)}, f32[768,192]{1,0:T(8,128)S(1)}, f32[144,896]{1,0:T(8,128)S(1)}) custom-call(bf16[2,2,12,24,192]{4,3,2,1,0:T(8,128)(2,1)S(1)} %copy-done.1, bf16[2,2,12,24,192]{4,3,2,1,0:T(8,128)(2,1)S(1)} %copy-done.3, bf16[192,576]{1,0:T(8,128)(2,1)S(1)} %copy-done.4, bf16[192,192]{1,0:T(8,128)(2,1)S(1)} %copy-done.5, ...), custom_call_target="tpu_custom_call" | custom-call | flops 3000000000 | bytes 4194304 | tf_op jit(solution)/shard_map/windows_lower_first/pallas_call | solution.py:390
  20.0 0.0 collective-permute-done.2.refs_7_.refs_9_
  20.0 2.7 %windows_lower_second.1 = (bf16[288,192]{1,0:T(8,128)(2,1)S(1)}, f32[768,192]{1,0:T(8,128)S(1)}, f32[144,896]{1,0:T(8,128)S(1)}) custom-call(bf16[2,2,12,24,192]{4,3,2,1,0:T(8,128)(2,1)S(1)} %copy-done.1, bf16[2,2,12,24,192]{4,3,2,1,0:T(8,128)(2,1)S(1)} %copy-done.3, bf16[192,576]{1,0:T(8,128)(2,1)S(1)} %copy-done.4, bf16[192,192]{1,0:T(8,128)(2,1)S(1)} %copy-done.5, ...), custom_call_target="tpu_custom_call" | custom-call | flops 3000000000 | bytes 4194304 | tf_op jit(solution)/shard_map/windows_lower_second/pallas_call | solution.py:390
  22.8 0.0 collective-permute-done.4.refs_7_
  22.8 4.7 %windows_upper.1 = (bf16[576,192]{1,0:T(8,128)(2,1)S(1)}, f32[768,192]{1,0:T(8,128)S(1)}, f32[144,896]{1,0:T(8,128)S(1)}, bf16[288,192]{1,0:T(8,128)(2,1)S(1)}) custom-call(bf16[2,2,12,24,192]{4,3,2,1,0:T(8,128)(2,1)S(1)} %copy-done.1, bf16[2,2,12,24,192]{4,3,2,1,0:T(8,128)(2,1)S(1)} %copy-done.3, bf16[192,576]{1,0:T(8,128)(2,1)S(1)} %copy-done.4, ...), custom_call_target="tpu_custom_call" | custom-call | flops 6000000000 | bytes 4194304 | tf_op jit(solution)/shard_map/windows_upper/pallas_call | solution.py:390
  27.5 1.3 %fold.1 = (bf16[768,128]{1,0:T(8,128)(2,1)S(1)}, bf16[768,128]{1,0:T(8,128)(2,1)S(1)}) custom-call(f32[768,192]{1,0:T(8,128)S(1)} %get-tuple-element.44.w_s, f32[144,896]{1,0:T(8,128)S(1)} %get-tuple-element.45.gb0, f32[144,896]{1,0:T(8,128)S(1)} %get-tuple-element.46.gb1, s32[1,128]{1,0:T(1,128)S(1)} %slice_bitcast_fusion.target, s32[1,1]{1,0:T(1,128)} %bitcast.2.core), custom_call_target="tpu_custom_call" | custom-call | flops 2000000000 | bytes 4194304 | tf_op jit(solution)/shard_map/fold/pallas_call | solution.py:365
  28.8 4.5 %collective-permute-start.9 = (bf16[768,128]{1,0:T(8,128)(2,1)S(1)}, bf16[768,128]{1,0:T(8,128)(2,1)S(1)}, u32[]{:S(2)}, u32[]{:S(2)}) collective-permute-start(bf16[768,128]{1,0:T(8,128)(2,1)S(1)} %get-tuple-element.48), channel_id=1, source_target_pairs={{0,8},{8,0},{16,24},{24,16},{32,40},{40,32},{48,56},{56,48},{64,72... | collective-permute-start | bytes 589832 | tf_op jit(solution)/shard_map/ppermute | solution.py:521
  33.3 1.1 %collective-permute-done.9 = bf16[768,128]{1,0:T(8,128)(2,1)S(1)} collective-permute-done((bf16[768,128]{1,0:T(8,128)(2,1)S(1)}, bf16[768,128]{1,0:T(8,128)(2,1)S(1)}, u32[]{:S(2)}, u32[]{:S(2)}) %collective-permute-start.9) | collective-permute-done | bytes 196640 | tf_op jit(solution)/shard_map/ppermute | solution.py:521
  34.4 0.1 add_convert_fusion
  34.4 13.8 %all_to_all.15 = bf16[8,96,128]{2,1,0:T(8,128)(2,1)S(1)} all-to-all(bf16[8,96,128]{2,1,0:T(8,128)(2,1)S(1)} %bitcast.10), channel_id=1, replica_groups={{0,32,64,96,128,160,192,224},{8,40,72,104,136,168,200,232},{16,48,80,11..., dimensions={0} | all-to-all | bytes 393216 | tf_op jit(solution)/shard_map/all_to_all | solution.py:535
  48.3 0.8 broadcast_in_dim.39
  49.1 4.9 %all-to-all-start.1 = ((bf16[16,96,128]{2,1,0:T(8,128)(2,1)}), bf16[16,96,128]{2,1,0:T(8,128)(2,1)S(1)}, u32[]{:S(2)}, u32[]{:S(2)}) async-start(bf16[16,96,128]{2,1,0:T(8,128)(2,1)} %broadcast_in_dim.39), calls=%async_computation.1 | async-start | bytes 786432 | tf_op jit(solution)/shard_map/all_to_all | solution.py:540
  54.0 5.4 %collective-permute-start.5 = (bf16[288,192]{1,0:T(8,128)(2,1)S(1)}, bf16[288,192]{1,0:T(8,128)(2,1)S(1)}, u32[]{:S(2)}, u32[]{:S(2)}) collective-permute-start(bf16[288,192]{1,0:T(8,128)(2,1)S(1)} %get-tuple-element.39), channel_id=1, source_target_pairs={{0,8},{8,16},{16,24},{24,32},{32,40},{40,48},{48,56},{56,64},{64,7... | collective-permute-start | bytes 331784 | tf_op jit(solution)/shard_map/ppermute | solution.py:507
  59.4 2.7 %all-to-all-done.1 = bf16[16,96,128]{2,1,0:T(8,128)(2,1)S(1)} async-done(((bf16[16,96,128]{2,1,0:T(8,128)(2,1)}), bf16[16,96,128]{2,1,0:T(8,128)(2,1)S(1)}, u32[]{:S(2)}, u32[]{:S(2)}) %all-to-all-start.1) | async-done | bytes 393248 | tf_op jit(solution)/shard_map/all_to_all | solution.py:540
  62.0 0.1 multiply_reduce_fusion
  62.2 0.7 broadcast_in_dim.42
  62.9 5.2 %all-to-all-start.2 = ((bf16[8,96,128]{2,1,0:T(8,128)(2,1)}), bf16[8,96,128]{2,1,0:T(8,128)(2,1)S(1)}, u32[]{:S(2)}, u32[]{:S(2)}) async-start(bf16[8,96,128]{2,1,0:T(8,128)(2,1)} %broadcast_in_dim.42), calls=%async_computation.2 | async-start | bytes 393216 | tf_op jit(solution)/shard_map/all_to_all | solution.py:550
  68.1 0.0 collective-permute-done.5.lon_in
  68.1 0.2 merge_lon.1
  68.3 0.1 collective-permute-start.6
  68.4 0.1 collective-permute-start.7
  68.4 0.1 collective-permute-start.8
  68.5 8.3 %all-to-all-done.2 = bf16[8,96,128]{2,1,0:T(8,128)(2,1)S(1)} async-done(((bf16[8,96,128]{2,1,0:T(8,128)(2,1)}), bf16[8,96,128]{2,1,0:T(8,128)(2,1)S(1)}, u32[]{:S(2)}, u32[]{:S(2)}) %all-to-all-start.2) | async-done | bytes 196640 | tf_op jit(solution)/shard_map/all_to_all | solution.py:550
  76.8 3.2 %collective-permute-start.10 = (bf16[768,128]{1,0:T(8,128)(2,1)S(1)}, bf16[768,128]{1,0:T(8,128)(2,1)S(1)}, u32[]{:S(2)}, u32[]{:S(2)}) collective-permute-start(bf16[768,128]{1,0:T(8,128)(2,1)S(1)} %bitcast.8), channel_id=1, source_target_pairs={{0,8},{8,0},{16,24},{24,16},{32,40},{40,32},{48,56},{56,48},{64,72... | collective-permute-start | bytes 589832 | tf_op jit(solution)/shard_map/ppermute | solution.py:521
  80.1 1.1 %place_grad.1 = f32[2,2,12,24,192]{4,3,2,1,0:T(8,128)} custom-call(bf16[2,9,24,192]{3,2,1,0:T(8,128)(2,1)S(1)} %get-tuple-element.40.own, bf16[2,9,24,192]{3,2,1,0:T(8,128)(2,1)S(1)} %collective-permute-done.6.lev, bf16[2,3,24,192]{3,2,1,0:T(8,128)(2,1)S(1)} %collective-permute-done.7.lat, bf16[2,3,24,192]{3,2,1,0:T(8,128)(2,1)S(1)} %collective-permute-done.8.diag), custom_call_target="tpu_custom_call" | custom-call | flops 20000000000 | bytes 2097152 | tf_op jit(solution)/shard_map/place_grad/pallas_call | solution.py:455
  81.2 1.3 %finish_params.1 = (f32[192,576]{1,0:T(8,128)}, f32[192,192]{1,0:T(8,128)}, f32[1,6,2,3312]{3,2,1,0:T(2,128)}) custom-call(bf16[768,128]{1,0:T(8,128)(2,1)S(1)} %bitcast.9, bf16[768,128]{1,0:T(8,128)(2,1)S(1)} %collective-permute-done.10.other, s32[1,1]{1,0:T(1,128)} %bitcast.2.core), custom_call_target="tpu_custom_call" | custom-call | bytes 2097152 | tf_op jit(solution)/shard_map/finish_params/pallas_call | solution.py:489
  (24 shorter events, 0.2 us)
Async XLA Ops:
  0.6 1.1 %copy-start = (bf16[2,2,12,24,192]{4,3,2,1,0:T(8,128)(2,1)S(1)}, bf16[2,2,12,24,192]{4,3,2,1,0:T(8,128)(2,1)}, u32[]{:S(2)}) copy-start(bf16[2,2,12,24,192]{4,3,2,1,0:T(8,128)(2,1)} %refs_0_.5) | copy-start | bytes 1327108
  1.7 1.1 %copy-start.2 = (bf16[2,2,12,24,192]{4,3,2,1,0:T(8,128)(2,1)S(1)}, bf16[2,2,12,24,192]{4,3,2,1,0:T(8,128)(2,1)}, u32[]{:S(2)}) copy-start(bf16[2,2,12,24,192]{4,3,2,1,0:T(8,128)(2,1)} %refs_1_.5) | copy-start | bytes 1327108
  2.9 4.0 %copy-start.6 = (f32[1,2,6,3312]{3,1,2,0:T(2,128)S(1)}, f32[1,2,6,3312]{3,1,2,0:T(2,128)}, u32[]{:S(2)}) copy-start(f32[1,2,6,3312]{3,1,2,0:T(2,128)} %param.9) | copy-start | bytes 476932
  2.9 9.3 %collective-permute-start.1 = (bf16[2,144,384]{2,1,0:T(8,128)(2,1)S(1)}, bf16[2,144,384]{2,1,0:T(8,128)(2,1)S(1)}, u32[]{:S(2)}, u32[]{:S(2)}) collective-permute-start(bf16[2,144,384]{2,1,0:T(8,128)(2,1)S(1)} %pack_lon.1), channel_id=1, source_target_pairs={{0,248},{8,0},{16,8},{24,16},{32,24},{40,32},{48,40},{56,48},{64,5... | collective-permute-start | bytes 663560 | tf_op jit(solution)/shard_map/ppermute | solution.py:507
  6.3 11.0 %collective-permute-start = (bf16[2,162,384]{2,1,0:T(8,128)(2,1)S(1)}, bf16[2,162,384]{2,1,0:T(8,128)(2,1)S(1)}, u32[]{:S(2)}, u32[]{:S(2)}) collective-permute-start(bf16[2,162,384]{2,1,0:T(8,128)(2,1)S(1)} %pack_lev.1), channel_id=1, source_target_pairs={{0,1},{1,0},{2,3},{3,2},{4,5},{5,4},{6,7},{7,6},{8,9},{9,8},{10,11... | collective-permute-start | bytes 746504 | tf_op jit(solution)/shard_map/ppermute | solution.py:507
  6.9 5.3 %copy-start.1 = (bf16[2,2,12,24,192]{4,3,2,1,0:T(8,128)(2,1)S(1)}, bf16[2,2,12,24,192]{4,3,2,1,0:T(8,128)(2,1)}, u32[]{:S(2)}) copy-start(bf16[2,2,12,24,192]{4,3,2,1,0:T(8,128)(2,1)} %refs_0_.5) | copy-start | bytes 1327108
  6.9 5.3 %copy-start.3 = (bf16[2,2,12,24,192]{4,3,2,1,0:T(8,128)(2,1)S(1)}, bf16[2,2,12,24,192]{4,3,2,1,0:T(8,128)(2,1)}, u32[]{:S(2)}) copy-start(bf16[2,2,12,24,192]{4,3,2,1,0:T(8,128)(2,1)} %refs_1_.5) | copy-start | bytes 1327108
  9.6 7.7 %copy-start.4 = (bf16[192,576]{1,0:T(8,128)(2,1)S(1)}, bf16[192,576]{1,0:T(8,128)(2,1)}, u32[]{:S(2)}) copy-start(bf16[192,576]{1,0:T(8,128)(2,1)} %refs_2_.5) | copy-start | bytes 663556
  9.7 7.7 %copy-start.5 = (bf16[192,192]{1,0:T(8,128)(2,1)S(1)}, bf16[192,192]{1,0:T(8,128)(2,1)}, u32[]{:S(2)}) copy-start(bf16[192,192]{1,0:T(8,128)(2,1)} %refs_3_.5) | copy-start | bytes 221188
  12.4 7.7 %collective-permute-start.2 = (bf16[2,54,384]{2,1,0:T(8,128)(2,1)S(1)}, bf16[2,54,384]{2,1,0:T(8,128)(2,1)S(1)}, u32[]{:S(2)}, u32[]{:S(2)}) collective-permute-start(bf16[2,54,384]{2,1,0:T(8,128)(2,1)S(1)} %get-tuple-element.30), channel_id=1, source_target_pairs={{0,1},{1,0},{2,3},{3,2},{4,5},{5,4},{6,7},{7,6},{8,9},{9,8},{10,11... | collective-permute-start | bytes 248840 | tf_op jit(solution)/shard_map/ppermute | solution.py:507
  14.5 8.2 %collective-permute-start.3 = (bf16[2,3,24,384]{3,2,1,0:T(8,128)(2,1)S(1)}, bf16[2,3,24,384]{3,2,1,0:T(8,128)(2,1)S(1)}, u32[]{:S(2)}, u32[]{:S(2)}) collective-permute-start(bf16[2,3,24,384]{3,2,1,0:T(8,128)(2,1)S(1)} %get-tuple-element.35), channel_id=1, source_target_pairs={{0,6},{2,0},{4,2},{6,4},{1,7},{3,1},{5,3},{7,5},{8,14},{10,8},{12,... | collective-permute-start | bytes 331784 | tf_op jit(solution)/shard_map/ppermute | solution.py:507
  17.0 5.8 %collective-permute-start.4 = (bf16[2,3,24,384]{3,2,1,0:T(8,128)(2,1)S(1)}, bf16[2,3,24,384]{3,2,1,0:T(8,128)(2,1)S(1)}, u32[]{:S(2)}, u32[]{:S(2)}) collective-permute-start(bf16[2,3,24,384]{3,2,1,0:T(8,128)(2,1)S(1)} %get-tuple-element.36), channel_id=1, source_target_pairs={{0,7},{1,6},{2,1},{3,0},{4,3},{5,2},{6,5},{7,4},{8,15},{9,14},{10,... | collective-permute-start | bytes 331784 | tf_op jit(solution)/shard_map/ppermute | solution.py:517
  28.8 5.6 %collective-permute-start.9 = (bf16[768,128]{1,0:T(8,128)(2,1)S(1)}, bf16[768,128]{1,0:T(8,128)(2,1)S(1)}, u32[]{:S(2)}, u32[]{:S(2)}) collective-permute-start(bf16[768,128]{1,0:T(8,128)(2,1)S(1)} %get-tuple-element.48), channel_id=1, source_target_pairs={{0,8},{8,0},{16,24},{24,16},{32,40},{40,32},{48,56},{56,48},{64,72... | collective-permute-start | bytes 589832 | tf_op jit(solution)/shard_map/ppermute | solution.py:521
  49.1 12.9 %all-to-all-start.1 = ((bf16[16,96,128]{2,1,0:T(8,128)(2,1)}), bf16[16,96,128]{2,1,0:T(8,128)(2,1)S(1)}, u32[]{:S(2)}, u32[]{:S(2)}) async-start(bf16[16,96,128]{2,1,0:T(8,128)(2,1)} %broadcast_in_dim.39), calls=%async_computation.1 | async-start | bytes 786432 | tf_op jit(solution)/shard_map/all_to_all | solution.py:540
  54.0 14.0 %collective-permute-start.5 = (bf16[288,192]{1,0:T(8,128)(2,1)S(1)}, bf16[288,192]{1,0:T(8,128)(2,1)S(1)}, u32[]{:S(2)}, u32[]{:S(2)}) collective-permute-start(bf16[288,192]{1,0:T(8,128)(2,1)S(1)} %get-tuple-element.39), channel_id=1, source_target_pairs={{0,8},{8,16},{16,24},{24,32},{32,40},{40,48},{48,56},{56,64},{64,7... | collective-permute-start | bytes 331784 | tf_op jit(solution)/shard_map/ppermute | solution.py:507
  62.9 13.9 %all-to-all-start.2 = ((bf16[8,96,128]{2,1,0:T(8,128)(2,1)}), bf16[8,96,128]{2,1,0:T(8,128)(2,1)S(1)}, u32[]{:S(2)}, u32[]{:S(2)}) async-start(bf16[8,96,128]{2,1,0:T(8,128)(2,1)} %broadcast_in_dim.42), calls=%async_computation.2 | async-start | bytes 393216 | tf_op jit(solution)/shard_map/all_to_all | solution.py:550
  68.3 11.8 %collective-permute-start.6 = (bf16[2,9,24,192]{3,2,1,0:T(8,128)(2,1)S(1)}, bf16[2,9,24,192]{3,2,1,0:T(8,128)(2,1)S(1)}, u32[]{:S(2)}, u32[]{:S(2)}) collective-permute-start(bf16[2,9,24,192]{3,2,1,0:T(8,128)(2,1)S(1)} %get-tuple-element.41), channel_id=1, source_target_pairs={{0,1},{1,0},{2,3},{3,2},{4,5},{5,4},{6,7},{7,6},{8,9},{9,8},{10,11... | collective-permute-start | bytes 497672 | tf_op jit(solution)/shard_map/ppermute | solution.py:507
  68.4 11.7 %collective-permute-start.7 = (bf16[2,3,24,192]{3,2,1,0:T(8,128)(2,1)S(1)}, bf16[2,3,24,192]{3,2,1,0:T(8,128)(2,1)S(1)}, u32[]{:S(2)}, u32[]{:S(2)}) collective-permute-start(bf16[2,3,24,192]{3,2,1,0:T(8,128)(2,1)S(1)} %get-tuple-element.42), channel_id=1, source_target_pairs={{0,2},{2,4},{4,6},{6,0},{1,3},{3,5},{5,7},{7,1},{8,10},{10,12},{12... | collective-permute-start | bytes 165896 | tf_op jit(solution)/shard_map/ppermute | solution.py:507
  68.4 11.6 %collective-permute-start.8 = (bf16[2,3,24,192]{3,2,1,0:T(8,128)(2,1)S(1)}, bf16[2,3,24,192]{3,2,1,0:T(8,128)(2,1)S(1)}, u32[]{:S(2)}, u32[]{:S(2)}) collective-permute-start(bf16[2,3,24,192]{3,2,1,0:T(8,128)(2,1)S(1)} %get-tuple-element.43), channel_id=1, source_target_pairs={{0,3},{1,2},{2,5},{3,4},{4,7},{5,6},{6,1},{7,0},{8,11},{9,10},{10,... | collective-permute-start | bytes 165896 | tf_op jit(solution)/shard_map/ppermute | solution.py:517
  76.8 4.3 %collective-permute-start.10 = (bf16[768,128]{1,0:T(8,128)(2,1)S(1)}, bf16[768,128]{1,0:T(8,128)(2,1)S(1)}, u32[]{:S(2)}, u32[]{:S(2)}) collective-permute-start(bf16[768,128]{1,0:T(8,128)(2,1)S(1)} %bitcast.8), channel_id=1, source_target_pairs={{0,8},{8,0},{16,24},{24,16},{32,40},{40,32},{48,56},{56,48},{64,72... | collective-permute-start | bytes 589832 | tf_op jit(solution)/shard_map/ppermute | solution.py:521

commit v5 on v4

--- a/solution.py
+++ b/solution.py
@@ -34,6 +34,7 @@
 TAILS = HEADS * MAIN
 PAIR = 2 * WIN
 BOTH = 2 * C
+SPARE = 8
 VMEM = pl.BlockSpec(memory_space=pltpu.VMEM)
 HBM = pl.BlockSpec(memory_space=pl.ANY)
 SMEM = pl.BlockSpec(memory_space=pltpu.SMEM)
@@ -74,7 +75,7 @@
     for b in range(2):
         for r in range(9):
             tmp[b, r * 18 : r * 18 + 18, :] = both_lines(f, u, b, 0, r + 3)[6:24]
-    out[...] = tmp[...].astype(BF)
+    out[...] = tmp[:, 0 : out.shape[1], :].astype(BF)
 
 
 def pack_lev(fields, upstream):
@@ -84,7 +85,7 @@
         out_shape=shape((2, 162, BOTH), BF),
         in_specs=[VMEM] * 2,
         out_specs=VMEM,
-        scratch_shapes=[pltpu.VMEM((2, 162, BOTH), F32)],
+        scratch_shapes=[pltpu.VMEM((2, 168 + SPARE, BOTH), F32)],
         compiler_params=params(16),
         cost_estimate=cost(0, 2 * 1024 * 1024),
     )(fields, upstream)
@@ -96,7 +97,7 @@
             for row in range(12):
                 at = (level * 12 + row) * 6
                 tmp[b, at : at + 6, :] = both_lines(f, u, b, level, row)[0:6]
-    out[...] = tmp[...].astype(BF)
+    out[...] = tmp[:, 0 : out.shape[1], :].astype(BF)
 
 
 def pack_lon(fields, upstream):
@@ -106,7 +107,7 @@
         out_shape=shape((2, WIN, BOTH), BF),
         in_specs=[VMEM] * 2,
         out_specs=VMEM,
-        scratch_shapes=[pltpu.VMEM((2, WIN, BOTH), F32)],
+        scratch_shapes=[pltpu.VMEM((2, WIN + SPARE, BOTH), F32)],
         compiler_params=params(16),
         cost_estimate=cost(0, 2 * 1024 * 1024),
     )(fields, upstream)
@@ -151,7 +152,7 @@
                 for aw in range(2):
                     at = (z1 * 6 + h1) * 24 + (z2 * 2 + aw) * 6
                     spread[at : at + 6, 0:GROUP] = eb[0, aw, :, off : off + GROUP]
-    full = spread[...]
+    full = spread[0:288, :]
     high = full.astype(BF)
     rest = full - high.astype(F32)
     mid = rest.astype(BF)
@@ -187,7 +188,7 @@
         out_shape=(shape((WIN, SPREAD), F32),) * 2,
         in_specs=[VMEM] * 4,
         out_specs=(VMEM,) * 2,
-        scratch_shapes=[pltpu.VMEM((288, KEYS), F32), pltpu.VMEM((24 * WIN, 128), F32)],
+        scratch_shapes=[pltpu.VMEM((288 + SPARE, KEYS), F32), pltpu.VMEM((25 * WIN, 128), F32)],
         compiler_params=params(16),
         cost_estimate=cost(4 * 10**9, 4 * 1024 * 1024),
     )(earth_bias, target, region_k, region_q)
@@ -242,18 +243,19 @@
 
     weights = wqkv[...].astype(F32)
     wq, wk, wv = [weights[:, i * C : (i + 1) * C].astype(BF) for i in range(3)]
-    raw = x_s[...]
+    tokens = len(seconds) * PAIR
+    raw = x_s[0:tokens, :]
     centred = raw - jnp.mean(raw, axis=-1, keepdims=True)
     inv_std = lax.rsqrt(jnp.mean(centred * centred, axis=-1, keepdims=True) + EPS)
     normed = centred * inv_std
     low = normed.astype(BF)
-    x_s[...] = normed
+    x_s[0:tokens, :] = normed
     i_s[...] = inv_std
     low_s[...] = low
     q_s[...] = dot(low, wq).astype(BF)
     k_s[...] = dot(low, wk).astype(BF)
     v_s[...] = dot(low, wv).astype(BF)
-    up = u_s[...].astype(BF)
+    up = u_s[0:tokens, :].astype(BF)
     ga_s[...] = dot(up, wo[...], 1, 1).astype(BF)
     att_s[...] = jnp.zeros_like(att_s)
     up_s[...] = jnp.zeros_like(up_s)
@@ -315,7 +317,7 @@
     w_s[C : 2 * C, :] += dot(low_t, gk)
     w_s[2 * C : 3 * C, :] += dot(low_t, gv)
     gu = dot(gq, wq, 1, 1) + dot(gk, wk, 1, 1) + dot(gv, wv, 1, 1)
-    normed = x_s[...]
+    normed = x_s[0:tokens, :]
     centre = jnp.mean(gu, axis=-1, keepdims=True)
     along = jnp.mean(gu * normed, axis=-1, keepdims=True)
     grad = i_s[...] * (gu - centre - normed * along)
@@ -331,7 +333,7 @@
                 row = ((r // 6) * 2 + b) * WIN + z * 72 + (r % 6) * 12
                 to = b * WIN + (z * 12 + r) * 6
                 lon_s[to : to + 6, :] = g_s[row + 6 : row + 12, :]
-    lon_back[...] = lon_s[...].astype(BF)
+    lon_back[...] = lon_s[0 : 2 * WIN, :].astype(BF)
 
 
 def fold_kernel(w_s, gb0, gb1, target, core, keep, send, turned, slab):
@@ -369,7 +371,7 @@
         in_specs=[VMEM] * 4 + [SMEM],
         out_specs=(VMEM,) * 2,
         scratch_shapes=[
-            pltpu.VMEM((24 * WIN, 128), F32),
+            pltpu.VMEM((25 * WIN, 128), F32),
             pltpu.VMEM((SLAB, 128), BF),
         ],
         compiler_params=params(24),
@@ -380,13 +382,13 @@
 def windows(aw, seconds, *args):
     tokens = len(seconds) * PAIR
     padded = 2 * len(seconds) * KEYS
-    rows = [pltpu.VMEM((tokens, C), F32)] * 2 + [pltpu.VMEM((tokens, 1), F32)]
+    rows = [pltpu.VMEM((tokens + SPARE, C), F32)] * 2 + [pltpu.VMEM((tokens, 1), F32)]
     rows += [pltpu.VMEM((tokens, C), BF)] * 8
     rows += [pltpu.VMEM((C, padded), BF), pltpu.VMEM((padded, C), BF)]
     outs = (shape((tokens, C), BF), shape((4 * C, C), F32), shape((WIN, SPREAD), F32))
     if aw == 1:
         outs += (shape((2 * WIN, C), BF),)
-        rows += [pltpu.VMEM((2 * PAIR, C), F32), pltpu.VMEM((2 * WIN, C), F32)]
+        rows += [pltpu.VMEM((2 * PAIR + SPARE, C), F32), pltpu.VMEM((2 * WIN + SPARE, C), F32)]
     return pl.pallas_call(
         functools.partial(windows_kernel, aw, seconds),
         name="windows_upper" if aw else "windows_lower_second" if seconds[0] else "windows_lower_first",

time: 82.8 us -> 82.8 us (level)
  no operation moved by 1% of the time
where the time goes in v5:
time: 82.8 us; the launch traced here: 82.4 us
  starting transfers between devices  31.8 us (38%)
  Pallas kernels  16.9 us (20%)
  waiting for transfers between devices  14.6 us (18%)
  blocking collectives  13.9 us (17%)
  local copies, waits for them, and re-layouts  3.99 us (5%)
  between operations  0.95 us (1%)
    all_to_all x1, blocking collectives, reduce_slab(): lax.all_to_all(half.reshape(depth, rows, 128), 'lon', 0, 0, axis_index_gr...  13.9 us
    ppermute x7, starting transfers between devices, from_behind(): lax.ppermute(x, axis, [(i, (i + by) % devices) for i in range(devices)])  13.6 us
    pallas_call x3, Pallas kernels, windows(): pl.pallas_call(functools.partial(windows_kernel, aw, seconds), name='wind...  10.1 us
    all_to_all x1, waiting for transfers between devices, reduce_slab(): lax.all_to_all(jnp.broadcast_to(mine[None], (depth, rows, 128)), 'lon', 0...  8.28 us
    ppermute x2, starting transfers between devices, other_core(): lax.ppermute(x, 'lon', [(i, i ^ 1) for i in range(lax.axis_size('lon'))])  7.71 us
    all_to_all x1, starting transfers between devices, reduce_slab(): lax.all_to_all(jnp.broadcast_to(mine[None], (depth, rows, 128)), 'lon', 0...  5.16 us
    all_to_all x1, starting transfers between devices, reduce_slab(): lax.all_to_all(jnp.broadcast_to(mine[None], (count, rows, 128)), ('lon',...  4.85 us
    pallas_call x1, Pallas kernels, expand(): pl.pallas_call(expand_kernel, name='expand_bias', out_shape=(shape((WIN,...  2.68 us
  transfers between devices with their start and end apart: 13, of which 4 were waited for; matrix products, arithmetic and copies ran while one was open for 2% of the time, Pallas kernels for 12%

profile of v5, /device:TPU:1, one launch (start us, length us, event | category | flops | bytes accessed | tf_op | source)
XLA Modules:
  0.0 82.4 jit_solution(14181795717233506351)
XLA Ops:
  0.6 0.0 copy-start
  0.6 1.1 %copy-done = bf16[2,2,12,24,192]{4,3,2,1,0:T(8,128)(2,1)S(1)} copy-done((bf16[2,2,12,24,192]{4,3,2,1,0:T(8,128)(2,1)S(1)}, bf16[2,2,12,24,192]{4,3,2,1,0:T(8,128)(2,1)}, u32[]{:S(2)}) %copy-start) | copy-done | bytes 442392
  1.7 1.1 %copy-done.2 = bf16[2,2,12,24,192]{4,3,2,1,0:T(8,128)(2,1)S(1)} copy-done((bf16[2,2,12,24,192]{4,3,2,1,0:T(8,128)(2,1)S(1)}, bf16[2,2,12,24,192]{4,3,2,1,0:T(8,128)(2,1)}, u32[]{:S(2)}) %copy-start.2) | copy-done | bytes 442392
  2.8 0.1 pack_lon.1
  2.9 0.0 copy-start.6
  2.9 3.3 %collective-permute-start.1 = (bf16[2,144,384]{2,1,0:T(8,128)(2,1)S(1)}, bf16[2,144,384]{2,1,0:T(8,128)(2,1)S(1)}, u32[]{:S(2)}, u32[]{:S(2)}) collective-permute-start(bf16[2,144,384]{2,1,0:T(8,128)(2,1)S(1)} %pack_lon.1), channel_id=1, source_target_pairs={{0,248},{8,0},{16,8},{24,16},{32,24},{40,32},{48,40},{56,48},{64,5... | collective-permute-start | bytes 663560 | tf_op jit(solution)/shard_map/ppermute | solution.py:509
  6.2 0.1 pack_lev.1
  6.3 0.1 collective-permute-start
  6.6 0.1 tile.10
  6.6 0.1 pad.2.clone
  6.7 0.1 copy.14.region_k
  6.9 0.0 copy-start.1
  6.9 0.0 copy-start.3
  7.0 2.7 %expand_bias.1 = (f32[144,896]{1,0:T(8,128)S(1)}, f32[144,896]{1,0:T(8,128)S(1)}) custom-call(f32[1,2,6,3312]{3,2,1,0:T(8,128)S(1)} %copy.13.eb, s32[1,128]{1,0:T(1,128)S(1)} %slice_bitcast_fusion.target, f32[2,144,1]{2,1,0:T(8,128)S(1)} %copy.14.region_k, f32[2,1,256]{2,1,0:T(1,128)S(1)} %broadcast_in_dim.38.region_q), custom_call_target="tpu_custom_call" | custom-call | flops 4000000000 | bytes 4194304 | tf_op jit(solution)/shard_map/expand_bias/pallas_call | solution.py:185
  9.6 0.0 copy-start.4
  9.7 0.0 copy-start.5
  9.7 2.6 %collective-permute-done.1.lon.refs_6_.refs_8_ = bf16[2,144,384]{2,1,0:T(8,128)(2,1)S(1)} collective-permute-done((bf16[2,144,384]{2,1,0:T(8,128)(2,1)S(1)}, bf16[2,144,384]{2,1,0:T(8,128)(2,1)S(1)}, u32[]{:S(2)}, u32[]{:S(2)}) %collective-permute-start.1) | collective-permute-done | bytes 221216 | tf_op jit(solution)/shard_map/ppermute | solution.py:509
  12.2 0.1 pack_rest.1
  12.4 2.2 %collective-permute-start.2 = (bf16[2,54,384]{2,1,0:T(8,128)(2,1)S(1)}, bf16[2,54,384]{2,1,0:T(8,128)(2,1)S(1)}, u32[]{:S(2)}, u32[]{:S(2)}) collective-permute-start(bf16[2,54,384]{2,1,0:T(8,128)(2,1)S(1)} %get-tuple-element.30), channel_id=1, source_target_pairs={{0,1},{1,0},{2,3},{3,2},{4,5},{5,4},{6,7},{7,6},{8,9},{9,8},{10,11... | collective-permute-start | bytes 248840 | tf_op jit(solution)/shard_map/ppermute | solution.py:509
  14.5 2.5 %collective-permute-start.3 = (bf16[2,3,24,384]{3,2,1,0:T(8,128)(2,1)S(1)}, bf16[2,3,24,384]{3,2,1,0:T(8,128)(2,1)S(1)}, u32[]{:S(2)}, u32[]{:S(2)}) collective-permute-start(bf16[2,3,24,384]{3,2,1,0:T(8,128)(2,1)S(1)} %get-tuple-element.35), channel_id=1, source_target_pairs={{0,6},{2,0},{4,2},{6,4},{1,7},{3,1},{5,3},{7,5},{8,14},{10,8},{12,... | collective-permute-start | bytes 331784 | tf_op jit(solution)/shard_map/ppermute | solution.py:509
  17.0 0.4 collective-permute-start.4
  17.4 0.0 collective-permute-done.refs_5_
  17.4 2.7 %windows_lower_first.1 = (bf16[288,192]{1,0:T(8,128)(2,1)S(1)}, f32[768,192]{1,0:T(8,128)S(1)}, f32[144,896]{1,0:T(8,128)S(1)}) custom-call(bf16[2,2,12,24,192]{4,3,2,1,0:T(8,128)(2,1)S(1)} %copy-done.1, bf16[2,2,12,24,192]{4,3,2,1,0:T(8,128)(2,1)S(1)} %copy-done.3, bf16[192,576]{1,0:T(8,128)(2,1)S(1)} %copy-done.4, bf16[192,192]{1,0:T(8,128)(2,1)S(1)} %copy-done.5, ...), custom_call_target="tpu_custom_call" | custom-call | flops 3000000000 | bytes 4194304 | tf_op jit(solution)/shard_map/windows_lower_first/pallas_call | solution.py:392
  20.0 0.0 collective-permute-done.2.refs_7_.refs_9_
  20.1 2.7 %windows_lower_second.1 = (bf16[288,192]{1,0:T(8,128)(2,1)S(1)}, f32[768,192]{1,0:T(8,128)S(1)}, f32[144,896]{1,0:T(8,128)S(1)}) custom-call(bf16[2,2,12,24,192]{4,3,2,1,0:T(8,128)(2,1)S(1)} %copy-done.1, bf16[2,2,12,24,192]{4,3,2,1,0:T(8,128)(2,1)S(1)} %copy-done.3, bf16[192,576]{1,0:T(8,128)(2,1)S(1)} %copy-done.4, bf16[192,192]{1,0:T(8,128)(2,1)S(1)} %copy-done.5, ...), custom_call_target="tpu_custom_call" | custom-call | flops 3000000000 | bytes 4194304 | tf_op jit(solution)/shard_map/windows_lower_second/pallas_call | solution.py:392
  22.8 0.0 collective-permute-done.3.refs_6_
  22.8 4.7 %windows_upper.1 = (bf16[576,192]{1,0:T(8,128)(2,1)S(1)}, f32[768,192]{1,0:T(8,128)S(1)}, f32[144,896]{1,0:T(8,128)S(1)}, bf16[288,192]{1,0:T(8,128)(2,1)S(1)}) custom-call(bf16[2,2,12,24,192]{4,3,2,1,0:T(8,128)(2,1)S(1)} %copy-done.1, bf16[2,2,12,24,192]{4,3,2,1,0:T(8,128)(2,1)S(1)} %copy-done.3, bf16[192,576]{1,0:T(8,128)(2,1)S(1)} %copy-done.4, ...), custom_call_target="tpu_custom_call" | custom-call | flops 6000000000 | bytes 4194304 | tf_op jit(solution)/shard_map/windows_upper/pallas_call | solution.py:392
  27.5 1.3 %fold.1 = (bf16[768,128]{1,0:T(8,128)(2,1)S(1)}, bf16[768,128]{1,0:T(8,128)(2,1)S(1)}) custom-call(f32[768,192]{1,0:T(8,128)S(1)} %get-tuple-element.44.w_s, f32[144,896]{1,0:T(8,128)S(1)} %get-tuple-element.45.gb0, f32[144,896]{1,0:T(8,128)S(1)} %get-tuple-element.46.gb1, s32[1,128]{1,0:T(1,128)S(1)} %slice_bitcast_fusion.target, s32[1,1]{1,0:T(1,128)} %bitcast.2.core), custom_call_target="tpu_custom_call" | custom-call | flops 2000000000 | bytes 4194304 | tf_op jit(solution)/shard_map/fold/pallas_call | solution.py:367
  28.8 4.5 %collective-permute-start.9 = (bf16[768,128]{1,0:T(8,128)(2,1)S(1)}, bf16[768,128]{1,0:T(8,128)(2,1)S(1)}, u32[]{:S(2)}, u32[]{:S(2)}) collective-permute-start(bf16[768,128]{1,0:T(8,128)(2,1)S(1)} %get-tuple-element.48), channel_id=1, source_target_pairs={{0,8},{8,0},{16,24},{24,16},{32,40},{40,32},{48,56},{56,48},{64,72... | collective-permute-start | bytes 589832 | tf_op jit(solution)/shard_map/ppermute | solution.py:523
  33.3 1.1 %collective-permute-done.9 = bf16[768,128]{1,0:T(8,128)(2,1)S(1)} collective-permute-done((bf16[768,128]{1,0:T(8,128)(2,1)S(1)}, bf16[768,128]{1,0:T(8,128)(2,1)S(1)}, u32[]{:S(2)}, u32[]{:S(2)}) %collective-permute-start.9) | collective-permute-done | bytes 196640 | tf_op jit(solution)/shard_map/ppermute | solution.py:523
  34.4 0.1 add_convert_fusion
  34.4 13.9 %all_to_all.15 = bf16[8,96,128]{2,1,0:T(8,128)(2,1)S(1)} all-to-all(bf16[8,96,128]{2,1,0:T(8,128)(2,1)S(1)} %bitcast.10), channel_id=1, replica_groups={{0,32,64,96,128,160,192,224},{8,40,72,104,136,168,200,232},{16,48,80,11..., dimensions={0} | all-to-all | bytes 393216 | tf_op jit(solution)/shard_map/all_to_all | solution.py:537
  48.3 0.8 broadcast_in_dim.39
  49.1 4.9 %all-to-all-start.1 = ((bf16[16,96,128]{2,1,0:T(8,128)(2,1)}), bf16[16,96,128]{2,1,0:T(8,128)(2,1)S(1)}, u32[]{:S(2)}, u32[]{:S(2)}) async-start(bf16[16,96,128]{2,1,0:T(8,128)(2,1)} %broadcast_in_dim.39), calls=%async_computation.1 | async-start | bytes 786432 | tf_op jit(solution)/shard_map/all_to_all | solution.py:542
  54.0 5.4 %collective-permute-start.5 = (bf16[288,192]{1,0:T(8,128)(2,1)S(1)}, bf16[288,192]{1,0:T(8,128)(2,1)S(1)}, u32[]{:S(2)}, u32[]{:S(2)}) collective-permute-start(bf16[288,192]{1,0:T(8,128)(2,1)S(1)} %get-tuple-element.39), channel_id=1, source_target_pairs={{0,8},{8,16},{16,24},{24,32},{32,40},{40,48},{48,56},{56,64},{64,7... | collective-permute-start | bytes 331784 | tf_op jit(solution)/shard_map/ppermute | solution.py:509
  59.4 2.7 %all-to-all-done.1 = bf16[16,96,128]{2,1,0:T(8,128)(2,1)S(1)} async-done(((bf16[16,96,128]{2,1,0:T(8,128)(2,1)}), bf16[16,96,128]{2,1,0:T(8,128)(2,1)S(1)}, u32[]{:S(2)}, u32[]{:S(2)}) %all-to-all-start.1) | async-done | bytes 393248 | tf_op jit(solution)/shard_map/all_to_all | solution.py:542
  62.0 0.1 multiply_reduce_fusion
  62.2 0.7 broadcast_in_dim.42
  62.9 5.2 %all-to-all-start.2 = ((bf16[8,96,128]{2,1,0:T(8,128)(2,1)}), bf16[8,96,128]{2,1,0:T(8,128)(2,1)S(1)}, u32[]{:S(2)}, u32[]{:S(2)}) async-start(bf16[8,96,128]{2,1,0:T(8,128)(2,1)} %broadcast_in_dim.42), calls=%async_computation.2 | async-start | bytes 393216 | tf_op jit(solution)/shard_map/all_to_all | solution.py:552
  68.0 0.0 collective-permute-done.5.lon_in
  68.1 0.2 merge_lon.1
  68.2 0.1 collective-permute-start.6
  68.3 0.1 collective-permute-start.7
  68.4 0.1 collective-permute-start.8
  68.5 8.3 %all-to-all-done.2 = bf16[8,96,128]{2,1,0:T(8,128)(2,1)S(1)} async-done(((bf16[8,96,128]{2,1,0:T(8,128)(2,1)}), bf16[8,96,128]{2,1,0:T(8,128)(2,1)S(1)}, u32[]{:S(2)}, u32[]{:S(2)}) %all-to-all-start.2) | async-done | bytes 196640 | tf_op jit(solution)/shard_map/all_to_all | solution.py:552
  76.8 3.2 %collective-permute-start.10 = (bf16[768,128]{1,0:T(8,128)(2,1)S(1)}, bf16[768,128]{1,0:T(8,128)(2,1)S(1)}, u32[]{:S(2)}, u32[]{:S(2)}) collective-permute-start(bf16[768,128]{1,0:T(8,128)(2,1)S(1)} %bitcast.8), channel_id=1, source_target_pairs={{0,8},{8,0},{16,24},{24,16},{32,40},{40,32},{48,56},{56,48},{64,72... | collective-permute-start | bytes 589832 | tf_op jit(solution)/shard_map/ppermute | solution.py:523
  80.0 1.1 %place_grad.1 = f32[2,2,12,24,192]{4,3,2,1,0:T(8,128)} custom-call(bf16[2,9,24,192]{3,2,1,0:T(8,128)(2,1)S(1)} %get-tuple-element.40.own, bf16[2,9,24,192]{3,2,1,0:T(8,128)(2,1)S(1)} %collective-permute-done.6.lev, bf16[2,3,24,192]{3,2,1,0:T(8,128)(2,1)S(1)} %collective-permute-done.7.lat, bf16[2,3,24,192]{3,2,1,0:T(8,128)(2,1)S(1)} %collective-permute-done.8.diag), custom_call_target="tpu_custom_call" | custom-call | flops 20000000000 | bytes 2097152 | tf_op jit(solution)/shard_map/place_grad/pallas_call | solution.py:457
  81.1 1.3 %finish_params.1 = (f32[192,576]{1,0:T(8,128)}, f32[192,192]{1,0:T(8,128)}, f32[1,6,2,3312]{3,2,1,0:T(2,128)}) custom-call(bf16[768,128]{1,0:T(8,128)(2,1)S(1)} %bitcast.9, bf16[768,128]{1,0:T(8,128)(2,1)S(1)} %collective-permute-done.10.other, s32[1,1]{1,0:T(1,128)} %bitcast.2.core), custom_call_target="tpu_custom_call" | custom-call | bytes 2097152 | tf_op jit(solution)/shard_map/finish_params/pallas_call | solution.py:491
  (24 shorter events, 0.2 us)
Async XLA Ops:
  0.6 1.1 %copy-start = (bf16[2,2,12,24,192]{4,3,2,1,0:T(8,128)(2,1)S(1)}, bf16[2,2,12,24,192]{4,3,2,1,0:T(8,128)(2,1)}, u32[]{:S(2)}) copy-start(bf16[2,2,12,24,192]{4,3,2,1,0:T(8,128)(2,1)} %refs_0_.5) | copy-start | bytes 1327108
  1.7 1.1 %copy-start.2 = (bf16[2,2,12,24,192]{4,3,2,1,0:T(8,128)(2,1)S(1)}, bf16[2,2,12,24,192]{4,3,2,1,0:T(8,128)(2,1)}, u32[]{:S(2)}) copy-start(bf16[2,2,12,24,192]{4,3,2,1,0:T(8,128)(2,1)} %refs_1_.5) | copy-start | bytes 1327108
  2.9 4.0 %copy-start.6 = (f32[1,2,6,3312]{3,1,2,0:T(2,128)S(1)}, f32[1,2,6,3312]{3,1,2,0:T(2,128)}, u32[]{:S(2)}) copy-start(f32[1,2,6,3312]{3,1,2,0:T(2,128)} %param.9) | copy-start | bytes 476932
  2.9 9.3 %collective-permute-start.1 = (bf16[2,144,384]{2,1,0:T(8,128)(2,1)S(1)}, bf16[2,144,384]{2,1,0:T(8,128)(2,1)S(1)}, u32[]{:S(2)}, u32[]{:S(2)}) collective-permute-start(bf16[2,144,384]{2,1,0:T(8,128)(2,1)S(1)} %pack_lon.1), channel_id=1, source_target_pairs={{0,248},{8,0},{16,8},{24,16},{32,24},{40,32},{48,40},{56,48},{64,5... | collective-permute-start | bytes 663560 | tf_op jit(solution)/shard_map/ppermute | solution.py:509
  6.3 11.0 %collective-permute-start = (bf16[2,162,384]{2,1,0:T(8,128)(2,1)S(1)}, bf16[2,162,384]{2,1,0:T(8,128)(2,1)S(1)}, u32[]{:S(2)}, u32[]{:S(2)}) collective-permute-start(bf16[2,162,384]{2,1,0:T(8,128)(2,1)S(1)} %pack_lev.1), channel_id=1, source_target_pairs={{0,1},{1,0},{2,3},{3,2},{4,5},{5,4},{6,7},{7,6},{8,9},{9,8},{10,11... | collective-permute-start | bytes 746504 | tf_op jit(solution)/shard_map/ppermute | solution.py:509
  6.9 5.3 %copy-start.1 = (bf16[2,2,12,24,192]{4,3,2,1,0:T(8,128)(2,1)S(1)}, bf16[2,2,12,24,192]{4,3,2,1,0:T(8,128)(2,1)}, u32[]{:S(2)}) copy-start(bf16[2,2,12,24,192]{4,3,2,1,0:T(8,128)(2,1)} %refs_0_.5) | copy-start | bytes 1327108
  6.9 5.3 %copy-start.3 = (bf16[2,2,12,24,192]{4,3,2,1,0:T(8,128)(2,1)S(1)}, bf16[2,2,12,24,192]{4,3,2,1,0:T(8,128)(2,1)}, u32[]{:S(2)}) copy-start(bf16[2,2,12,24,192]{4,3,2,1,0:T(8,128)(2,1)} %refs_1_.5) | copy-start | bytes 1327108
  9.6 7.7 %copy-start.4 = (bf16[192,576]{1,0:T(8,128)(2,1)S(1)}, bf16[192,576]{1,0:T(8,128)(2,1)}, u32[]{:S(2)}) copy-start(bf16[192,576]{1,0:T(8,128)(2,1)} %refs_2_.5) | copy-start | bytes 663556
  9.7 7.7 %copy-start.5 = (bf16[192,192]{1,0:T(8,128)(2,1)S(1)}, bf16[192,192]{1,0:T(8,128)(2,1)}, u32[]{:S(2)}) copy-start(bf16[192,192]{1,0:T(8,128)(2,1)} %refs_3_.5) | copy-start | bytes 221188
  12.4 7.7 %collective-permute-start.2 = (bf16[2,54,384]{2,1,0:T(8,128)(2,1)S(1)}, bf16[2,54,384]{2,1,0:T(8,128)(2,1)S(1)}, u32[]{:S(2)}, u32[]{:S(2)}) collective-permute-start(bf16[2,54,384]{2,1,0:T(8,128)(2,1)S(1)} %get-tuple-element.30), channel_id=1, source_target_pairs={{0,1},{1,0},{2,3},{3,2},{4,5},{5,4},{6,7},{7,6},{8,9},{9,8},{10,11... | collective-permute-start | bytes 248840 | tf_op jit(solution)/shard_map/ppermute | solution.py:509
  14.5 8.3 %collective-permute-start.3 = (bf16[2,3,24,384]{3,2,1,0:T(8,128)(2,1)S(1)}, bf16[2,3,24,384]{3,2,1,0:T(8,128)(2,1)S(1)}, u32[]{:S(2)}, u32[]{:S(2)}) collective-permute-start(bf16[2,3,24,384]{3,2,1,0:T(8,128)(2,1)S(1)} %get-tuple-element.35), channel_id=1, source_target_pairs={{0,6},{2,0},{4,2},{6,4},{1,7},{3,1},{5,3},{7,5},{8,14},{10,8},{12,... | collective-permute-start | bytes 331784 | tf_op jit(solution)/shard_map/ppermute | solution.py:509
  17.0 5.8 %collective-permute-start.4 = (bf16[2,3,24,384]{3,2,1,0:T(8,128)(2,1)S(1)}, bf16[2,3,24,384]{3,2,1,0:T(8,128)(2,1)S(1)}, u32[]{:S(2)}, u32[]{:S(2)}) collective-permute-start(bf16[2,3,24,384]{3,2,1,0:T(8,128)(2,1)S(1)} %get-tuple-element.36), channel_id=1, source_target_pairs={{0,7},{1,6},{2,1},{3,0},{4,3},{5,2},{6,5},{7,4},{8,15},{9,14},{10,... | collective-permute-start | bytes 331784 | tf_op jit(solution)/shard_map/ppermute | solution.py:519
  28.8 5.6 %collective-permute-start.9 = (bf16[768,128]{1,0:T(8,128)(2,1)S(1)}, bf16[768,128]{1,0:T(8,128)(2,1)S(1)}, u32[]{:S(2)}, u32[]{:S(2)}) collective-permute-start(bf16[768,128]{1,0:T(8,128)(2,1)S(1)} %get-tuple-element.48), channel_id=1, source_target_pairs={{0,8},{8,0},{16,24},{24,16},{32,40},{40,32},{48,56},{56,48},{64,72... | collective-permute-start | bytes 589832 | tf_op jit(solution)/shard_map/ppermute | solution.py:523
  49.1 12.9 %all-to-all-start.1 = ((bf16[16,96,128]{2,1,0:T(8,128)(2,1)}), bf16[16,96,128]{2,1,0:T(8,128)(2,1)S(1)}, u32[]{:S(2)}, u32[]{:S(2)}) async-start(bf16[16,96,128]{2,1,0:T(8,128)(2,1)} %broadcast_in_dim.39), calls=%async_computation.1 | async-start | bytes 786432 | tf_op jit(solution)/shard_map/all_to_all | solution.py:542
  54.0 14.0 %collective-permute-start.5 = (bf16[288,192]{1,0:T(8,128)(2,1)S(1)}, bf16[288,192]{1,0:T(8,128)(2,1)S(1)}, u32[]{:S(2)}, u32[]{:S(2)}) collective-permute-start(bf16[288,192]{1,0:T(8,128)(2,1)S(1)} %get-tuple-element.39), channel_id=1, source_target_pairs={{0,8},{8,16},{16,24},{24,32},{32,40},{40,48},{48,56},{56,64},{64,7... | collective-permute-start | bytes 331784 | tf_op jit(solution)/shard_map/ppermute | solution.py:509
  62.9 13.9 %all-to-all-start.2 = ((bf16[8,96,128]{2,1,0:T(8,128)(2,1)}), bf16[8,96,128]{2,1,0:T(8,128)(2,1)S(1)}, u32[]{:S(2)}, u32[]{:S(2)}) async-start(bf16[8,96,128]{2,1,0:T(8,128)(2,1)} %broadcast_in_dim.42), calls=%async_computation.2 | async-start | bytes 393216 | tf_op jit(solution)/shard_map/all_to_all | solution.py:552
  68.2 11.8 %collective-permute-start.6 = (bf16[2,9,24,192]{3,2,1,0:T(8,128)(2,1)S(1)}, bf16[2,9,24,192]{3,2,1,0:T(8,128)(2,1)S(1)}, u32[]{:S(2)}, u32[]{:S(2)}) collective-permute-start(bf16[2,9,24,192]{3,2,1,0:T(8,128)(2,1)S(1)} %get-tuple-element.41), channel_id=1, source_target_pairs={{0,1},{1,0},{2,3},{3,2},{4,5},{5,4},{6,7},{7,6},{8,9},{9,8},{10,11... | collective-permute-start | bytes 497672 | tf_op jit(solution)/shard_map/ppermute | solution.py:509
  68.3 11.7 %collective-permute-start.7 = (bf16[2,3,24,192]{3,2,1,0:T(8,128)(2,1)S(1)}, bf16[2,3,24,192]{3,2,1,0:T(8,128)(2,1)S(1)}, u32[]{:S(2)}, u32[]{:S(2)}) collective-permute-start(bf16[2,3,24,192]{3,2,1,0:T(8,128)(2,1)S(1)} %get-tuple-element.42), channel_id=1, source_target_pairs={{0,2},{2,4},{4,6},{6,0},{1,3},{3,5},{5,7},{7,1},{8,10},{10,12},{12... | collective-permute-start | bytes 165896 | tf_op jit(solution)/shard_map/ppermute | solution.py:509
  68.4 11.6 %collective-permute-start.8 = (bf16[2,3,24,192]{3,2,1,0:T(8,128)(2,1)S(1)}, bf16[2,3,24,192]{3,2,1,0:T(8,128)(2,1)S(1)}, u32[]{:S(2)}, u32[]{:S(2)}) collective-permute-start(bf16[2,3,24,192]{3,2,1,0:T(8,128)(2,1)S(1)} %get-tuple-element.43), channel_id=1, source_target_pairs={{0,3},{1,2},{2,5},{3,4},{4,7},{5,6},{6,1},{7,0},{8,11},{9,10},{10,... | collective-permute-start | bytes 165896 | tf_op jit(solution)/shard_map/ppermute | solution.py:519
  76.8 4.3 %collective-permute-start.10 = (bf16[768,128]{1,0:T(8,128)(2,1)S(1)}, bf16[768,128]{1,0:T(8,128)(2,1)S(1)}, u32[]{:S(2)}, u32[]{:S(2)}) collective-permute-start(bf16[768,128]{1,0:T(8,128)(2,1)S(1)} %bitcast.8), channel_id=1, source_target_pairs={{0,8},{8,0},{16,24},{24,16},{32,40},{40,32},{48,56},{56,48},{64,72... | collective-permute-start | bytes 589832 | tf_op jit(solution)/shard_map/ppermute | solution.py:523

commit v6 on v5

--- a/solution.py
+++ b/solution.py
@@ -333,7 +333,7 @@
                 row = ((r // 6) * 2 + b) * WIN + z * 72 + (r % 6) * 12
                 to = b * WIN + (z * 12 + r) * 6
                 lon_s[to : to + 6, :] = g_s[row + 6 : row + 12, :]
-    lon_back[...] = lon_s[0 : 2 * WIN, :].astype(BF)
+    lon_back[...] = join(lon_s[0:WIN, :], lon_s[WIN : 2 * WIN, :]).astype(BF)
 
 
 def fold_kernel(w_s, gb0, gb1, target, core, keep, send, turned, slab):
@@ -387,7 +387,7 @@
     rows += [pltpu.VMEM((C, padded), BF), pltpu.VMEM((padded, C), BF)]
     outs = (shape((tokens, C), BF), shape((4 * C, C), F32), shape((WIN, SPREAD), F32))
     if aw == 1:
-        outs += (shape((2 * WIN, C), BF),)
+        outs += (shape((WIN, BOTH), BF),)
         rows += [pltpu.VMEM((2 * PAIR + SPARE, C), F32), pltpu.VMEM((2 * WIN + SPARE, C), F32)]
     return pl.pallas_call(
         functools.partial(windows_kernel, aw, seconds),
@@ -402,30 +402,35 @@
 
 
 def merge_kernel(g_first, g_second, g_upper, lon_in, own, lev, lat, diag):
-    for b in range(2):
-        halo = lon_in[b * WIN : (b + 1) * WIN, :].astype(F32)
-        for aw in range(2):
+    halos = split(lon_in[...].astype(F32))
+    for aw in range(2):
+        first, second = [], []
+        for b in range(2):
             at = slice(b * WIN, (b + 1) * WIN)
             after = slice(PAIR + b * WIN, PAIR + (b + 1) * WIN)
-            first = (g_upper if aw else g_first)[at, :].astype(F32)
-            second = (g_upper[after, :] if aw else g_second[at, :]).astype(F32)
-            for z in range(2):
-                for h in range(6):
-                    r = aw * 6 + h
-                    off = z * 72 + h * 12
-                    hrow = (z * 12 + r) * 6
-                    line = jnp.concatenate(
-                        [halo[hrow : hrow + 6], first[off : off + 12], second[off : off + 6]], axis=0
-                    ).astype(BF)
-                    if z == 0:
-                        if r < 9:
-                            own[b, r] = line
-                        else:
-                            lat[b, r - 9] = line
-                    elif r < 9:
-                        lev[b, r] = line
-                    else:
-                        diag[b, r - 9] = line
+            first.append((g_upper if aw else g_first)[at, :].astype(F32))
+            second.append((g_upper[after, :] if aw else g_second[at, :]).astype(F32))
+        for z in range(2):
+            for h in range(6):
+                r = aw * 6 + h
+                off = z * 72 + h * 12
+                hrow = (z * 12 + r) * 6
+                lines = [
+                    jnp.concatenate(
+                        [halos[b][hrow : hrow + 6], first[b][off : off + 12], second[b][off : off + 6]],
+                        axis=0,
+                    )
+                    for b in range(2)
+                ]
+                if z == 0 and r < 9:
+                    for b in range(2):
+                        own[b, r] = lines[b].astype(BF)
+                    continue
+                line = join(*lines).astype(BF)
+                if r < 9:
+                    lev[r] = line
+                else:
+                    (diag if z else lat)[r - 9] = line
 
 
 def merge(*args):
@@ -434,9 +439,9 @@
         name="merge_lon",
         out_shape=(
             shape((2, 9, 24, C), BF),
-            shape((2, 9, 24, C), BF),
-            shape((2, 3, 24, C), BF),
-            shape((2, 3, 24, C), BF),
+            shape((9, 24, BOTH), BF),
+            shape((3, 24, BOTH), BF),
+            shape((3, 24, BOTH), BF),
         ),
         in_specs=[VMEM] * 4,
         out_specs=(VMEM,) * 4,
@@ -448,9 +453,10 @@
 def place_kernel(own, lev, lat, diag, out):
     for b in range(2):
         out[b, 1, 3:12] = own[b].astype(F32)
-        out[b, 1, 0:3] = lat[b].astype(F32)
-        out[b, 0, 3:12] = lev[b].astype(F32)
-        out[b, 0, 0:3] = diag[b].astype(F32)
+    for level, first, rows, src in ((0, 3, 9, lev), (1, 0, 3, lat), (0, 0, 3, diag)):
+        for r in range(rows):
+            for b, line in enumerate(split(src[r].astype(F32))):
+                out[b, level, first + r] = line
 
 
 def place(own, lev, lat, diag):

time: 82.8 us -> 82.5 us (level)
  no operation moved by 1% of the time
where the time goes in v6:
time: 82.5 us; the launch traced here: 82.1 us
  starting transfers between devices  31.7 us (38%)
  Pallas kernels  17.1 us (21%)
  waiting for transfers between devices  14.2 us (17%)
  blocking collectives  13.9 us (17%)
  local copies, waits for them, and re-layouts  3.99 us (5%)
  between operations  0.93 us (1%)
    all_to_all x1, blocking collectives, reduce_slab(): lax.all_to_all(half.reshape(depth, rows, 128), 'lon', 0, 0, axis_index_gr...  13.9 us
    ppermute x7, starting transfers between devices, from_behind(): lax.ppermute(x, axis, [(i, (i + by) % devices) for i in range(devices)])  13.6 us
    pallas_call x3, Pallas kernels, windows(): pl.pallas_call(functools.partial(windows_kernel, aw, seconds), name='wind...  10.2 us
    all_to_all x1, waiting for transfers between devices, reduce_slab(): lax.all_to_all(jnp.broadcast_to(mine[None], (depth, rows, 128)), 'lon', 0...  7.93 us
    ppermute x2, starting transfers between devices, other_core(): lax.ppermute(x, 'lon', [(i, i ^ 1) for i in range(lax.axis_size('lon'))])  7.84 us
    all_to_all x1, starting transfers between devices, reduce_slab(): lax.all_to_all(jnp.broadcast_to(mine[None], (count, rows, 128)), ('lon',...  4.84 us
    all_to_all x1, starting transfers between devices, reduce_slab(): lax.all_to_all(jnp.broadcast_to(mine[None], (depth, rows, 128)), 'lon', 0...  4.68 us
    pallas_call x1, Pallas kernels, expand(): pl.pallas_call(expand_kernel, name='expand_bias', out_shape=(shape((WIN,...  2.68 us
  transfers between devices with their start and end apart: 13, of which 4 were waited for; matrix products, arithmetic and copies ran while one was open for 2% of the time, Pallas kernels for 12%

profile of v6, /device:TPU:1, one launch (start us, length us, event | category | flops | bytes accessed | tf_op | source)
XLA Modules:
  0.0 82.1 jit_solution(4661004221516575920)
XLA Ops:
  0.6 0.0 copy-start
  0.6 1.1 %copy-done = bf16[2,2,12,24,192]{4,3,2,1,0:T(8,128)(2,1)S(1)} copy-done((bf16[2,2,12,24,192]{4,3,2,1,0:T(8,128)(2,1)S(1)}, bf16[2,2,12,24,192]{4,3,2,1,0:T(8,128)(2,1)}, u32[]{:S(2)}) %copy-start) | copy-done | bytes 442392
  1.7 1.1 %copy-done.2 = bf16[2,2,12,24,192]{4,3,2,1,0:T(8,128)(2,1)S(1)} copy-done((bf16[2,2,12,24,192]{4,3,2,1,0:T(8,128)(2,1)S(1)}, bf16[2,2,12,24,192]{4,3,2,1,0:T(8,128)(2,1)}, u32[]{:S(2)}) %copy-start.2) | copy-done | bytes 442392
  2.8 0.1 pack_lon.1
  2.9 0.0 copy-start.6
  2.9 3.3 %collective-permute-start.1 = (bf16[2,144,384]{2,1,0:T(8,128)(2,1)S(1)}, bf16[2,144,384]{2,1,0:T(8,128)(2,1)S(1)}, u32[]{:S(2)}, u32[]{:S(2)}) collective-permute-start(bf16[2,144,384]{2,1,0:T(8,128)(2,1)S(1)} %pack_lon.1), channel_id=1, source_target_pairs={{0,248},{8,0},{16,8},{24,16},{32,24},{40,32},{48,40},{56,48},{64,5... | collective-permute-start | bytes 663560 | tf_op jit(solution)/shard_map/ppermute | solution.py:515
  6.2 0.1 pack_lev.1
  6.3 0.1 collective-permute-start
  6.6 0.1 tile.10
  6.6 0.1 pad.2.clone
  6.7 0.1 copy.14.region_k
  6.9 0.0 copy-start.1
  6.9 0.0 copy-start.3
  7.0 2.7 %expand_bias.1 = (f32[144,896]{1,0:T(8,128)S(1)}, f32[144,896]{1,0:T(8,128)S(1)}) custom-call(f32[1,2,6,3312]{3,2,1,0:T(8,128)S(1)} %copy.13.eb, s32[1,128]{1,0:T(1,128)S(1)} %slice_bitcast_fusion.target, f32[2,144,1]{2,1,0:T(8,128)S(1)} %copy.14.region_k, f32[2,1,256]{2,1,0:T(1,128)S(1)} %broadcast_in_dim.38.region_q), custom_call_target="tpu_custom_call" | custom-call | flops 4000000000 | bytes 4194304 | tf_op jit(solution)/shard_map/expand_bias/pallas_call | solution.py:185
  9.6 0.0 copy-start.4
  9.7 0.0 copy-start.5
  9.7 2.6 %collective-permute-done.1.lon.refs_6_.refs_8_ = bf16[2,144,384]{2,1,0:T(8,128)(2,1)S(1)} collective-permute-done((bf16[2,144,384]{2,1,0:T(8,128)(2,1)S(1)}, bf16[2,144,384]{2,1,0:T(8,128)(2,1)S(1)}, u32[]{:S(2)}, u32[]{:S(2)}) %collective-permute-start.1) | collective-permute-done | bytes 221216 | tf_op jit(solution)/shard_map/ppermute | solution.py:515
  12.2 0.1 pack_rest.1
  12.4 2.2 %collective-permute-start.2 = (bf16[2,54,384]{2,1,0:T(8,128)(2,1)S(1)}, bf16[2,54,384]{2,1,0:T(8,128)(2,1)S(1)}, u32[]{:S(2)}, u32[]{:S(2)}) collective-permute-start(bf16[2,54,384]{2,1,0:T(8,128)(2,1)S(1)} %get-tuple-element.30), channel_id=1, source_target_pairs={{0,1},{1,0},{2,3},{3,2},{4,5},{5,4},{6,7},{7,6},{8,9},{9,8},{10,11... | collective-permute-start | bytes 248840 | tf_op jit(solution)/shard_map/ppermute | solution.py:515
  14.5 2.5 %collective-permute-start.3 = (bf16[2,3,24,384]{3,2,1,0:T(8,128)(2,1)S(1)}, bf16[2,3,24,384]{3,2,1,0:T(8,128)(2,1)S(1)}, u32[]{:S(2)}, u32[]{:S(2)}) collective-permute-start(bf16[2,3,24,384]{3,2,1,0:T(8,128)(2,1)S(1)} %get-tuple-element.35), channel_id=1, source_target_pairs={{0,6},{2,0},{4,2},{6,4},{1,7},{3,1},{5,3},{7,5},{8,14},{10,8},{12,... | collective-permute-start | bytes 331784 | tf_op jit(solution)/shard_map/ppermute | solution.py:515
  17.0 0.4 collective-permute-start.4
  17.4 0.0 collective-permute-done.refs_5_
  17.4 2.7 %windows_lower_first.1 = (bf16[288,192]{1,0:T(8,128)(2,1)S(1)}, f32[768,192]{1,0:T(8,128)S(1)}, f32[144,896]{1,0:T(8,128)S(1)}) custom-call(bf16[2,2,12,24,192]{4,3,2,1,0:T(8,128)(2,1)S(1)} %copy-done.1, bf16[2,2,12,24,192]{4,3,2,1,0:T(8,128)(2,1)S(1)} %copy-done.3, bf16[192,576]{1,0:T(8,128)(2,1)S(1)} %copy-done.4, bf16[192,192]{1,0:T(8,128)(2,1)S(1)} %copy-done.5, ...), custom_call_target="tpu_custom_call" | custom-call | flops 3000000000 | bytes 4194304 | tf_op jit(solution)/shard_map/windows_lower_first/pallas_call | solution.py:392
  20.0 2.7 %windows_lower_second.1 = (bf16[288,192]{1,0:T(8,128)(2,1)S(1)}, f32[768,192]{1,0:T(8,128)S(1)}, f32[144,896]{1,0:T(8,128)S(1)}) custom-call(bf16[2,2,12,24,192]{4,3,2,1,0:T(8,128)(2,1)S(1)} %copy-done.1, bf16[2,2,12,24,192]{4,3,2,1,0:T(8,128)(2,1)S(1)} %copy-done.3, bf16[192,576]{1,0:T(8,128)(2,1)S(1)} %copy-done.4, bf16[192,192]{1,0:T(8,128)(2,1)S(1)} %copy-done.5, ...), custom_call_target="tpu_custom_call" | custom-call | flops 3000000000 | bytes 4194304 | tf_op jit(solution)/shard_map/windows_lower_second/pallas_call | solution.py:392
  22.8 0.0 collective-permute-done.3.refs_6_
  22.8 0.0 collective-permute-done.4.refs_7_
  22.8 4.8 %windows_upper.1 = (bf16[576,192]{1,0:T(8,128)(2,1)S(1)}, f32[768,192]{1,0:T(8,128)S(1)}, f32[144,896]{1,0:T(8,128)S(1)}, bf16[144,384]{1,0:T(8,128)(2,1)S(1)}) custom-call(bf16[2,2,12,24,192]{4,3,2,1,0:T(8,128)(2,1)S(1)} %copy-done.1, bf16[2,2,12,24,192]{4,3,2,1,0:T(8,128)(2,1)S(1)} %copy-done.3, bf16[192,576]{1,0:T(8,128)(2,1)S(1)} %copy-done.4, ...), custom_call_target="tpu_custom_call" | custom-call | flops 6000000000 | bytes 4194304 | tf_op jit(solution)/shard_map/windows_upper/pallas_call | solution.py:392
  27.6 1.3 %fold.1 = (bf16[768,128]{1,0:T(8,128)(2,1)S(1)}, bf16[768,128]{1,0:T(8,128)(2,1)S(1)}) custom-call(f32[768,192]{1,0:T(8,128)S(1)} %get-tuple-element.44.w_s, f32[144,896]{1,0:T(8,128)S(1)} %get-tuple-element.45.gb0, f32[144,896]{1,0:T(8,128)S(1)} %get-tuple-element.46.gb1, s32[1,128]{1,0:T(1,128)S(1)} %slice_bitcast_fusion.target, s32[1,1]{1,0:T(1,128)} %bitcast.2.core), custom_call_target="tpu_custom_call" | custom-call | flops 2000000000 | bytes 4194304 | tf_op jit(solution)/shard_map/fold/pallas_call | solution.py:367
  28.9 4.5 %collective-permute-start.9 = (bf16[768,128]{1,0:T(8,128)(2,1)S(1)}, bf16[768,128]{1,0:T(8,128)(2,1)S(1)}, u32[]{:S(2)}, u32[]{:S(2)}) collective-permute-start(bf16[768,128]{1,0:T(8,128)(2,1)S(1)} %get-tuple-element.48), channel_id=1, source_target_pairs={{0,8},{8,0},{16,24},{24,16},{32,40},{40,32},{48,56},{56,48},{64,72... | collective-permute-start | bytes 589832 | tf_op jit(solution)/shard_map/ppermute | solution.py:529
  33.4 1.1 %collective-permute-done.9 = bf16[768,128]{1,0:T(8,128)(2,1)S(1)} collective-permute-done((bf16[768,128]{1,0:T(8,128)(2,1)S(1)}, bf16[768,128]{1,0:T(8,128)(2,1)S(1)}, u32[]{:S(2)}, u32[]{:S(2)}) %collective-permute-start.9) | collective-permute-done | bytes 196640 | tf_op jit(solution)/shard_map/ppermute | solution.py:529
  34.5 0.1 add_convert_fusion
  34.5 13.9 %all_to_all.15 = bf16[8,96,128]{2,1,0:T(8,128)(2,1)S(1)} all-to-all(bf16[8,96,128]{2,1,0:T(8,128)(2,1)S(1)} %bitcast.10), channel_id=1, replica_groups={{0,32,64,96,128,160,192,224},{8,40,72,104,136,168,200,232},{16,48,80,11..., dimensions={0} | all-to-all | bytes 393216 | tf_op jit(solution)/shard_map/all_to_all | solution.py:543
  48.4 0.8 broadcast_in_dim.39
  49.2 4.8 %all-to-all-start.1 = ((bf16[16,96,128]{2,1,0:T(8,128)(2,1)}), bf16[16,96,128]{2,1,0:T(8,128)(2,1)S(1)}, u32[]{:S(2)}, u32[]{:S(2)}) async-start(bf16[16,96,128]{2,1,0:T(8,128)(2,1)} %broadcast_in_dim.39), calls=%async_computation.1 | async-start | bytes 786432 | tf_op jit(solution)/shard_map/all_to_all | solution.py:548
  54.1 5.4 %collective-permute-start.5 = (bf16[144,384]{1,0:T(8,128)(2,1)S(1)}, bf16[144,384]{1,0:T(8,128)(2,1)S(1)}, u32[]{:S(2)}, u32[]{:S(2)}) collective-permute-start(bf16[144,384]{1,0:T(8,128)(2,1)S(1)} %get-tuple-element.39), channel_id=1, source_target_pairs={{0,8},{8,16},{16,24},{24,32},{32,40},{40,48},{48,56},{56,64},{64,7... | collective-permute-start | bytes 331784 | tf_op jit(solution)/shard_map/ppermute | solution.py:515
  59.5 2.7 %all-to-all-done.1 = bf16[16,96,128]{2,1,0:T(8,128)(2,1)S(1)} async-done(((bf16[16,96,128]{2,1,0:T(8,128)(2,1)}), bf16[16,96,128]{2,1,0:T(8,128)(2,1)S(1)}, u32[]{:S(2)}, u32[]{:S(2)}) %all-to-all-start.1) | async-done | bytes 393248 | tf_op jit(solution)/shard_map/all_to_all | solution.py:548
  62.1 0.1 multiply_reduce_fusion
  62.3 0.7 broadcast_in_dim.42
  63.0 4.7 %all-to-all-start.2 = ((bf16[8,96,128]{2,1,0:T(8,128)(2,1)}), bf16[8,96,128]{2,1,0:T(8,128)(2,1)S(1)}, u32[]{:S(2)}, u32[]{:S(2)}) async-start(bf16[8,96,128]{2,1,0:T(8,128)(2,1)} %broadcast_in_dim.42), calls=%async_computation.2 | async-start | bytes 393216 | tf_op jit(solution)/shard_map/all_to_all | solution.py:558
  67.7 0.2 merge_lon.1
  67.9 0.1 collective-permute-start.6
  68.0 0.1 collective-permute-start.7
  68.1 0.4 collective-permute-start.8
  68.5 7.9 %all-to-all-done.2 = bf16[8,96,128]{2,1,0:T(8,128)(2,1)S(1)} async-done(((bf16[8,96,128]{2,1,0:T(8,128)(2,1)}), bf16[8,96,128]{2,1,0:T(8,128)(2,1)S(1)}, u32[]{:S(2)}, u32[]{:S(2)}) %all-to-all-start.2) | async-done | bytes 196640 | tf_op jit(solution)/shard_map/all_to_all | solution.py:558
  76.4 3.3 %collective-permute-start.10 = (bf16[768,128]{1,0:T(8,128)(2,1)S(1)}, bf16[768,128]{1,0:T(8,128)(2,1)S(1)}, u32[]{:S(2)}, u32[]{:S(2)}) collective-permute-start(bf16[768,128]{1,0:T(8,128)(2,1)S(1)} %bitcast.8), channel_id=1, source_target_pairs={{0,8},{8,0},{16,24},{24,16},{32,40},{40,32},{48,56},{56,48},{64,72... | collective-permute-start | bytes 589832 | tf_op jit(solution)/shard_map/ppermute | solution.py:529
  79.7 0.0 collective-permute-done.7.lat
  79.8 1.1 %place_grad.1 = f32[2,2,12,24,192]{4,3,2,1,0:T(8,128)} custom-call(bf16[2,9,24,192]{3,2,1,0:T(8,128)(2,1)S(1)} %get-tuple-element.40.own, bf16[9,24,384]{2,1,0:T(8,128)(2,1)S(1)} %collective-permute-done.6.lev, bf16[3,24,384]{2,1,0:T(8,128)(2,1)S(1)} %collective-permute-done.7.lat, bf16[3,24,384]{2,1,0:T(8,128)(2,1)S(1)} %collective-permute-done.8.diag), custom_call_target="tpu_custom_call" | custom-call | flops 20000000000 | bytes 2097152 | tf_op jit(solution)/shard_map/place_grad/pallas_call | solution.py:463
  80.9 1.3 %finish_params.1 = (f32[192,576]{1,0:T(8,128)}, f32[192,192]{1,0:T(8,128)}, f32[1,6,2,3312]{3,2,1,0:T(2,128)}) custom-call(bf16[768,128]{1,0:T(8,128)(2,1)S(1)} %bitcast.9, bf16[768,128]{1,0:T(8,128)(2,1)S(1)} %collective-permute-done.10.other, s32[1,1]{1,0:T(1,128)} %bitcast.2.core), custom_call_target="tpu_custom_call" | custom-call | bytes 2097152 | tf_op jit(solution)/shard_map/finish_params/pallas_call | solution.py:497
  (24 shorter events, 0.2 us)
Async XLA Ops:
  0.6 1.1 %copy-start = (bf16[2,2,12,24,192]{4,3,2,1,0:T(8,128)(2,1)S(1)}, bf16[2,2,12,24,192]{4,3,2,1,0:T(8,128)(2,1)}, u32[]{:S(2)}) copy-start(bf16[2,2,12,24,192]{4,3,2,1,0:T(8,128)(2,1)} %refs_0_.5) | copy-start | bytes 1327108
  1.7 1.1 %copy-start.2 = (bf16[2,2,12,24,192]{4,3,2,1,0:T(8,128)(2,1)S(1)}, bf16[2,2,12,24,192]{4,3,2,1,0:T(8,128)(2,1)}, u32[]{:S(2)}) copy-start(bf16[2,2,12,24,192]{4,3,2,1,0:T(8,128)(2,1)} %refs_1_.5) | copy-start | bytes 1327108
  2.9 4.0 %copy-start.6 = (f32[1,2,6,3312]{3,1,2,0:T(2,128)S(1)}, f32[1,2,6,3312]{3,1,2,0:T(2,128)}, u32[]{:S(2)}) copy-start(f32[1,2,6,3312]{3,1,2,0:T(2,128)} %param.9) | copy-start | bytes 476932
  2.9 9.3 %collective-permute-start.1 = (bf16[2,144,384]{2,1,0:T(8,128)(2,1)S(1)}, bf16[2,144,384]{2,1,0:T(8,128)(2,1)S(1)}, u32[]{:S(2)}, u32[]{:S(2)}) collective-permute-start(bf16[2,144,384]{2,1,0:T(8,128)(2,1)S(1)} %pack_lon.1), channel_id=1, source_target_pairs={{0,248},{8,0},{16,8},{24,16},{32,24},{40,32},{48,40},{56,48},{64,5... | collective-permute-start | bytes 663560 | tf_op jit(solution)/shard_map/ppermute | solution.py:515
  6.3 11.0 %collective-permute-start = (bf16[2,162,384]{2,1,0:T(8,128)(2,1)S(1)}, bf16[2,162,384]{2,1,0:T(8,128)(2,1)S(1)}, u32[]{:S(2)}, u32[]{:S(2)}) collective-permute-start(bf16[2,162,384]{2,1,0:T(8,128)(2,1)S(1)} %pack_lev.1), channel_id=1, source_target_pairs={{0,1},{1,0},{2,3},{3,2},{4,5},{5,4},{6,7},{7,6},{8,9},{9,8},{10,11... | collective-permute-start | bytes 746504 | tf_op jit(solution)/shard_map/ppermute | solution.py:515
  6.9 5.3 %copy-start.1 = (bf16[2,2,12,24,192]{4,3,2,1,0:T(8,128)(2,1)S(1)}, bf16[2,2,12,24,192]{4,3,2,1,0:T(8,128)(2,1)}, u32[]{:S(2)}) copy-start(bf16[2,2,12,24,192]{4,3,2,1,0:T(8,128)(2,1)} %refs_0_.5) | copy-start | bytes 1327108
  6.9 5.3 %copy-start.3 = (bf16[2,2,12,24,192]{4,3,2,1,0:T(8,128)(2,1)S(1)}, bf16[2,2,12,24,192]{4,3,2,1,0:T(8,128)(2,1)}, u32[]{:S(2)}) copy-start(bf16[2,2,12,24,192]{4,3,2,1,0:T(8,128)(2,1)} %refs_1_.5) | copy-start | bytes 1327108
  9.6 7.7 %copy-start.4 = (bf16[192,576]{1,0:T(8,128)(2,1)S(1)}, bf16[192,576]{1,0:T(8,128)(2,1)}, u32[]{:S(2)}) copy-start(bf16[192,576]{1,0:T(8,128)(2,1)} %refs_2_.5) | copy-start | bytes 663556
  9.7 7.7 %copy-start.5 = (bf16[192,192]{1,0:T(8,128)(2,1)S(1)}, bf16[192,192]{1,0:T(8,128)(2,1)}, u32[]{:S(2)}) copy-start(bf16[192,192]{1,0:T(8,128)(2,1)} %refs_3_.5) | copy-start | bytes 221188
  12.4 7.7 %collective-permute-start.2 = (bf16[2,54,384]{2,1,0:T(8,128)(2,1)S(1)}, bf16[2,54,384]{2,1,0:T(8,128)(2,1)S(1)}, u32[]{:S(2)}, u32[]{:S(2)}) collective-permute-start(bf16[2,54,384]{2,1,0:T(8,128)(2,1)S(1)} %get-tuple-element.30), channel_id=1, source_target_pairs={{0,1},{1,0},{2,3},{3,2},{4,5},{5,4},{6,7},{7,6},{8,9},{9,8},{10,11... | collective-permute-start | bytes 248840 | tf_op jit(solution)/shard_map/ppermute | solution.py:515
  14.5 8.3 %collective-permute-start.3 = (bf16[2,3,24,384]{3,2,1,0:T(8,128)(2,1)S(1)}, bf16[2,3,24,384]{3,2,1,0:T(8,128)(2,1)S(1)}, u32[]{:S(2)}, u32[]{:S(2)}) collective-permute-start(bf16[2,3,24,384]{3,2,1,0:T(8,128)(2,1)S(1)} %get-tuple-element.35), channel_id=1, source_target_pairs={{0,6},{2,0},{4,2},{6,4},{1,7},{3,1},{5,3},{7,5},{8,14},{10,8},{12,... | collective-permute-start | bytes 331784 | tf_op jit(solution)/shard_map/ppermute | solution.py:515
  17.0 5.8 %collective-permute-start.4 = (bf16[2,3,24,384]{3,2,1,0:T(8,128)(2,1)S(1)}, bf16[2,3,24,384]{3,2,1,0:T(8,128)(2,1)S(1)}, u32[]{:S(2)}, u32[]{:S(2)}) collective-permute-start(bf16[2,3,24,384]{3,2,1,0:T(8,128)(2,1)S(1)} %get-tuple-element.36), channel_id=1, source_target_pairs={{0,7},{1,6},{2,1},{3,0},{4,3},{5,2},{6,5},{7,4},{8,15},{9,14},{10,... | collective-permute-start | bytes 331784 | tf_op jit(solution)/shard_map/ppermute | solution.py:525
  28.9 5.6 %collective-permute-start.9 = (bf16[768,128]{1,0:T(8,128)(2,1)S(1)}, bf16[768,128]{1,0:T(8,128)(2,1)S(1)}, u32[]{:S(2)}, u32[]{:S(2)}) collective-permute-start(bf16[768,128]{1,0:T(8,128)(2,1)S(1)} %get-tuple-element.48), channel_id=1, source_target_pairs={{0,8},{8,0},{16,24},{24,16},{32,40},{40,32},{48,56},{56,48},{64,72... | collective-permute-start | bytes 589832 | tf_op jit(solution)/shard_map/ppermute | solution.py:529
  49.2 12.9 %all-to-all-start.1 = ((bf16[16,96,128]{2,1,0:T(8,128)(2,1)}), bf16[16,96,128]{2,1,0:T(8,128)(2,1)S(1)}, u32[]{:S(2)}, u32[]{:S(2)}) async-start(bf16[16,96,128]{2,1,0:T(8,128)(2,1)} %broadcast_in_dim.39), calls=%async_computation.1 | async-start | bytes 786432 | tf_op jit(solution)/shard_map/all_to_all | solution.py:548
  54.1 13.5 %collective-permute-start.5 = (bf16[144,384]{1,0:T(8,128)(2,1)S(1)}, bf16[144,384]{1,0:T(8,128)(2,1)S(1)}, u32[]{:S(2)}, u32[]{:S(2)}) collective-permute-start(bf16[144,384]{1,0:T(8,128)(2,1)S(1)} %get-tuple-element.39), channel_id=1, source_target_pairs={{0,8},{8,16},{16,24},{24,32},{32,40},{40,48},{48,56},{56,64},{64,7... | collective-permute-start | bytes 331784 | tf_op jit(solution)/shard_map/ppermute | solution.py:515
  63.0 13.4 %all-to-all-start.2 = ((bf16[8,96,128]{2,1,0:T(8,128)(2,1)}), bf16[8,96,128]{2,1,0:T(8,128)(2,1)S(1)}, u32[]{:S(2)}, u32[]{:S(2)}) async-start(bf16[8,96,128]{2,1,0:T(8,128)(2,1)} %broadcast_in_dim.42), calls=%async_computation.2 | async-start | bytes 393216 | tf_op jit(solution)/shard_map/all_to_all | solution.py:558
  67.9 11.9 %collective-permute-start.6 = (bf16[9,24,384]{2,1,0:T(8,128)(2,1)S(1)}, bf16[9,24,384]{2,1,0:T(8,128)(2,1)S(1)}, u32[]{:S(2)}, u32[]{:S(2)}) collective-permute-start(bf16[9,24,384]{2,1,0:T(8,128)(2,1)S(1)} %get-tuple-element.41), channel_id=1, source_target_pairs={{0,1},{1,0},{2,3},{3,2},{4,5},{5,4},{6,7},{7,6},{8,9},{9,8},{10,11... | collective-permute-start | bytes 497672 | tf_op jit(solution)/shard_map/ppermute | solution.py:515
  68.0 11.8 %collective-permute-start.7 = (bf16[3,24,384]{2,1,0:T(8,128)(2,1)S(1)}, bf16[3,24,384]{2,1,0:T(8,128)(2,1)S(1)}, u32[]{:S(2)}, u32[]{:S(2)}) collective-permute-start(bf16[3,24,384]{2,1,0:T(8,128)(2,1)S(1)} %get-tuple-element.42), channel_id=1, source_target_pairs={{0,2},{2,4},{4,6},{6,0},{1,3},{3,5},{5,7},{7,1},{8,10},{10,12},{12... | collective-permute-start | bytes 165896 | tf_op jit(solution)/shard_map/ppermute | solution.py:515
  68.1 11.7 %collective-permute-start.8 = (bf16[3,24,384]{2,1,0:T(8,128)(2,1)S(1)}, bf16[3,24,384]{2,1,0:T(8,128)(2,1)S(1)}, u32[]{:S(2)}, u32[]{:S(2)}) collective-permute-start(bf16[3,24,384]{2,1,0:T(8,128)(2,1)S(1)} %get-tuple-element.43), channel_id=1, source_target_pairs={{0,3},{1,2},{2,5},{3,4},{4,7},{5,6},{6,1},{7,0},{8,11},{9,10},{10,... | collective-permute-start | bytes 165896 | tf_op jit(solution)/shard_map/ppermute | solution.py:525
  76.4 4.5 %collective-permute-start.10 = (bf16[768,128]{1,0:T(8,128)(2,1)S(1)}, bf16[768,128]{1,0:T(8,128)(2,1)S(1)}, u32[]{:S(2)}, u32[]{:S(2)}) collective-permute-start(bf16[768,128]{1,0:T(8,128)(2,1)S(1)} %bitcast.8), channel_id=1, source_target_pairs={{0,8},{8,0},{16,24},{24,16},{32,40},{40,32},{48,56},{56,48},{64,72... | collective-permute-start | bytes 589832 | tf_op jit(solution)/shard_map/ppermute | solution.py:529

commit v7 on v6

--- a/solution.py
+++ b/solution.py
@@ -20,6 +20,7 @@
 GROUP = WH * OFFS
 LANES = 384
 KEYS = 256
+SPOTS = 144
 NEG_FILL = -1e30
 EPS = 1e-05
 SCALE = HD**-0.5
@@ -139,7 +140,7 @@
 
 
 def onehot_rows(target, w1):
-    row = lax.broadcasted_iota(jnp.int32, (KEYS, target.shape[1]), 0)
+    row = lax.broadcasted_iota(jnp.int32, (SPOTS, target.shape[1]), 0)
     return jnp.where(row == target + w1, 1.0, 0.0).astype(BF)
 
 
@@ -188,7 +189,7 @@
         out_shape=(shape((WIN, SPREAD), F32),) * 2,
         in_specs=[VMEM] * 4,
         out_specs=(VMEM,) * 2,
-        scratch_shapes=[pltpu.VMEM((288 + SPARE, KEYS), F32), pltpu.VMEM((25 * WIN, 128), F32)],
+        scratch_shapes=[pltpu.VMEM((288 + SPARE, SPOTS), F32), pltpu.VMEM((25 * WIN, 128), F32)],
         compiler_params=params(16),
         cost_estimate=cost(4 * 10**9, 4 * 1024 * 1024),
     )(earth_bias, target, region_k, region_q)
@@ -347,7 +348,7 @@
                 at = ((z2 * HEADS + h) * 2 + aw) * WIN
                 turned[at : at + MAIN, 0:72] = gb[rows, h * MAIN : (h + 1) * MAIN].T
                 turned[at + MAIN : at + WIN, 0:72] = tails[h * TAIL : (h + 1) * TAIL]
-    folded = jnp.zeros((288, KEYS), F32)
+    folded = jnp.zeros((288, SPOTS), F32)
     tgt = target[...]
     for w1 in range(WW):
         rows = [turned[pl.ds(g * 12 + w1, 24, stride=WIN), :] for g in range(12)]

time: 82.5 us -> 82.5 us (level)
  no operation moved by 1% of the time
where the time goes in v7:
time: 82.5 us; the launch traced here: 82.1 us
  starting transfers between devices  31.7 us (38%)
  Pallas kernels  17 us (21%)
  waiting for transfers between devices  14.3 us (17%)
  blocking collectives  13.9 us (17%)
  local copies, waits for them, and re-layouts  3.99 us (5%)
  between operations  0.93 us (1%)
    all_to_all x1, blocking collectives, reduce_slab(): lax.all_to_all(half.reshape(depth, rows, 128), 'lon', 0, 0, axis_index_gr...  13.9 us
    ppermute x7, starting transfers between devices, from_behind(): lax.ppermute(x, axis, [(i, (i + by) % devices) for i in range(devices)])  13.6 us
    pallas_call x3, Pallas kernels, windows(): pl.pallas_call(functools.partial(windows_kernel, aw, seconds), name='wind...  10.2 us
    all_to_all x1, waiting for transfers between devices, reduce_slab(): lax.all_to_all(jnp.broadcast_to(mine[None], (depth, rows, 128)), 'lon', 0...  7.93 us
    ppermute x2, starting transfers between devices, other_core(): lax.ppermute(x, 'lon', [(i, i ^ 1) for i in range(lax.axis_size('lon'))])  7.79 us
    all_to_all x1, starting transfers between devices, reduce_slab(): lax.all_to_all(jnp.broadcast_to(mine[None], (count, rows, 128)), ('lon',...  4.84 us
    all_to_all x1, starting transfers between devices, reduce_slab(): lax.all_to_all(jnp.broadcast_to(mine[None], (depth, rows, 128)), 'lon', 0...  4.68 us
    all_to_all x1, waiting for transfers between devices, reduce_slab(): lax.all_to_all(jnp.broadcast_to(mine[None], (count, rows, 128)), ('lon',...  2.65 us
  transfers between devices with their start and end apart: 13, of which 4 were waited for; matrix products, arithmetic and copies ran while one was open for 2% of the time, Pallas kernels for 12%

profile of v7, /device:TPU:1, one launch (start us, length us, event | category | flops | bytes accessed | tf_op | source)
XLA Modules:
  0.0 82.1 jit_solution(8170364792720876420)
XLA Ops:
  0.6 0.0 copy-start
  0.6 1.1 %copy-done = bf16[2,2,12,24,192]{4,3,2,1,0:T(8,128)(2,1)S(1)} copy-done((bf16[2,2,12,24,192]{4,3,2,1,0:T(8,128)(2,1)S(1)}, bf16[2,2,12,24,192]{4,3,2,1,0:T(8,128)(2,1)}, u32[]{:S(2)}) %copy-start) | copy-done | bytes 442392
  1.7 1.1 %copy-done.2 = bf16[2,2,12,24,192]{4,3,2,1,0:T(8,128)(2,1)S(1)} copy-done((bf16[2,2,12,24,192]{4,3,2,1,0:T(8,128)(2,1)S(1)}, bf16[2,2,12,24,192]{4,3,2,1,0:T(8,128)(2,1)}, u32[]{:S(2)}) %copy-start.2) | copy-done | bytes 442392
  2.8 0.1 pack_lon.1
  2.9 0.0 copy-start.6
  2.9 3.3 %collective-permute-start.1 = (bf16[2,144,384]{2,1,0:T(8,128)(2,1)S(1)}, bf16[2,144,384]{2,1,0:T(8,128)(2,1)S(1)}, u32[]{:S(2)}, u32[]{:S(2)}) collective-permute-start(bf16[2,144,384]{2,1,0:T(8,128)(2,1)S(1)} %pack_lon.1), channel_id=1, source_target_pairs={{0,248},{8,0},{16,8},{24,16},{32,24},{40,32},{48,40},{56,48},{64,5... | collective-permute-start | bytes 663560 | tf_op jit(solution)/shard_map/ppermute | solution.py:516
  6.2 0.1 pack_lev.1
  6.3 0.1 collective-permute-start
  6.6 0.1 tile.10
  6.6 0.1 pad.2.clone
  6.7 0.1 copy.14.region_k
  6.9 0.0 copy-start.1
  6.9 0.0 copy-start.3
  7.0 2.6 %expand_bias.1 = (f32[144,896]{1,0:T(8,128)S(1)}, f32[144,896]{1,0:T(8,128)S(1)}) custom-call(f32[1,2,6,3312]{3,2,1,0:T(8,128)S(1)} %copy.13.eb, s32[1,128]{1,0:T(1,128)S(1)} %slice_bitcast_fusion.target, f32[2,144,1]{2,1,0:T(8,128)S(1)} %copy.14.region_k, f32[2,1,256]{2,1,0:T(1,128)S(1)} %broadcast_in_dim.38.region_q), custom_call_target="tpu_custom_call" | custom-call | flops 4000000000 | bytes 4194304 | tf_op jit(solution)/shard_map/expand_bias/pallas_call | solution.py:186
  9.6 0.0 copy-start.4
  9.6 0.0 copy-start.5
  9.6 2.6 %collective-permute-done.1.lon.refs_6_.refs_8_ = bf16[2,144,384]{2,1,0:T(8,128)(2,1)S(1)} collective-permute-done((bf16[2,144,384]{2,1,0:T(8,128)(2,1)S(1)}, bf16[2,144,384]{2,1,0:T(8,128)(2,1)S(1)}, u32[]{:S(2)}, u32[]{:S(2)}) %collective-permute-start.1) | collective-permute-done | bytes 221216 | tf_op jit(solution)/shard_map/ppermute | solution.py:516
  12.2 0.1 pack_rest.1
  12.4 2.2 %collective-permute-start.2 = (bf16[2,54,384]{2,1,0:T(8,128)(2,1)S(1)}, bf16[2,54,384]{2,1,0:T(8,128)(2,1)S(1)}, u32[]{:S(2)}, u32[]{:S(2)}) collective-permute-start(bf16[2,54,384]{2,1,0:T(8,128)(2,1)S(1)} %get-tuple-element.30), channel_id=1, source_target_pairs={{0,1},{1,0},{2,3},{3,2},{4,5},{5,4},{6,7},{7,6},{8,9},{9,8},{10,11... | collective-permute-start | bytes 248840 | tf_op jit(solution)/shard_map/ppermute | solution.py:516
  14.5 2.5 %collective-permute-start.3 = (bf16[2,3,24,384]{3,2,1,0:T(8,128)(2,1)S(1)}, bf16[2,3,24,384]{3,2,1,0:T(8,128)(2,1)S(1)}, u32[]{:S(2)}, u32[]{:S(2)}) collective-permute-start(bf16[2,3,24,384]{3,2,1,0:T(8,128)(2,1)S(1)} %get-tuple-element.35), channel_id=1, source_target_pairs={{0,6},{2,0},{4,2},{6,4},{1,7},{3,1},{5,3},{7,5},{8,14},{10,8},{12,... | collective-permute-start | bytes 331784 | tf_op jit(solution)/shard_map/ppermute | solution.py:516
  17.0 0.4 collective-permute-start.4
  17.4 0.0 collective-permute-done.refs_5_
  17.4 2.7 %windows_lower_first.1 = (bf16[288,192]{1,0:T(8,128)(2,1)S(1)}, f32[768,192]{1,0:T(8,128)S(1)}, f32[144,896]{1,0:T(8,128)S(1)}) custom-call(bf16[2,2,12,24,192]{4,3,2,1,0:T(8,128)(2,1)S(1)} %copy-done.1, bf16[2,2,12,24,192]{4,3,2,1,0:T(8,128)(2,1)S(1)} %copy-done.3, bf16[192,576]{1,0:T(8,128)(2,1)S(1)} %copy-done.4, bf16[192,192]{1,0:T(8,128)(2,1)S(1)} %copy-done.5, ...), custom_call_target="tpu_custom_call" | custom-call | flops 3000000000 | bytes 4194304 | tf_op jit(solution)/shard_map/windows_lower_first/pallas_call | solution.py:393
  20.0 2.7 %windows_lower_second.1 = (bf16[288,192]{1,0:T(8,128)(2,1)S(1)}, f32[768,192]{1,0:T(8,128)S(1)}, f32[144,896]{1,0:T(8,128)S(1)}) custom-call(bf16[2,2,12,24,192]{4,3,2,1,0:T(8,128)(2,1)S(1)} %copy-done.1, bf16[2,2,12,24,192]{4,3,2,1,0:T(8,128)(2,1)S(1)} %copy-done.3, bf16[192,576]{1,0:T(8,128)(2,1)S(1)} %copy-done.4, bf16[192,192]{1,0:T(8,128)(2,1)S(1)} %copy-done.5, ...), custom_call_target="tpu_custom_call" | custom-call | flops 3000000000 | bytes 4194304 | tf_op jit(solution)/shard_map/windows_lower_second/pallas_call | solution.py:393
  22.8 0.0 collective-permute-done.3.refs_6_
  22.8 0.0 collective-permute-done.4.refs_7_
  22.8 4.8 %windows_upper.1 = (bf16[576,192]{1,0:T(8,128)(2,1)S(1)}, f32[768,192]{1,0:T(8,128)S(1)}, f32[144,896]{1,0:T(8,128)S(1)}, bf16[144,384]{1,0:T(8,128)(2,1)S(1)}) custom-call(bf16[2,2,12,24,192]{4,3,2,1,0:T(8,128)(2,1)S(1)} %copy-done.1, bf16[2,2,12,24,192]{4,3,2,1,0:T(8,128)(2,1)S(1)} %copy-done.3, bf16[192,576]{1,0:T(8,128)(2,1)S(1)} %copy-done.4, ...), custom_call_target="tpu_custom_call" | custom-call | flops 6000000000 | bytes 4194304 | tf_op jit(solution)/shard_map/windows_upper/pallas_call | solution.py:393
  27.6 1.2 %fold.1 = (bf16[768,128]{1,0:T(8,128)(2,1)S(1)}, bf16[768,128]{1,0:T(8,128)(2,1)S(1)}) custom-call(f32[768,192]{1,0:T(8,128)S(1)} %get-tuple-element.44.w_s, f32[144,896]{1,0:T(8,128)S(1)} %get-tuple-element.45.gb0, f32[144,896]{1,0:T(8,128)S(1)} %get-tuple-element.46.gb1, s32[1,128]{1,0:T(1,128)S(1)} %slice_bitcast_fusion.target, s32[1,1]{1,0:T(1,128)} %bitcast.2.core), custom_call_target="tpu_custom_call" | custom-call | flops 2000000000 | bytes 4194304 | tf_op jit(solution)/shard_map/fold/pallas_call | solution.py:368
  28.9 4.5 %collective-permute-start.9 = (bf16[768,128]{1,0:T(8,128)(2,1)S(1)}, bf16[768,128]{1,0:T(8,128)(2,1)S(1)}, u32[]{:S(2)}, u32[]{:S(2)}) collective-permute-start(bf16[768,128]{1,0:T(8,128)(2,1)S(1)} %get-tuple-element.48), channel_id=1, source_target_pairs={{0,8},{8,0},{16,24},{24,16},{32,40},{40,32},{48,56},{56,48},{64,72... | collective-permute-start | bytes 589832 | tf_op jit(solution)/shard_map/ppermute | solution.py:530
  33.3 1.1 %collective-permute-done.9 = bf16[768,128]{1,0:T(8,128)(2,1)S(1)} collective-permute-done((bf16[768,128]{1,0:T(8,128)(2,1)S(1)}, bf16[768,128]{1,0:T(8,128)(2,1)S(1)}, u32[]{:S(2)}, u32[]{:S(2)}) %collective-permute-start.9) | collective-permute-done | bytes 196640 | tf_op jit(solution)/shard_map/ppermute | solution.py:530
  34.4 0.1 add_convert_fusion
  34.4 13.9 %all_to_all.15 = bf16[8,96,128]{2,1,0:T(8,128)(2,1)S(1)} all-to-all(bf16[8,96,128]{2,1,0:T(8,128)(2,1)S(1)} %bitcast.10), channel_id=1, replica_groups={{0,32,64,96,128,160,192,224},{8,40,72,104,136,168,200,232},{16,48,80,11..., dimensions={0} | all-to-all | bytes 393216 | tf_op jit(solution)/shard_map/all_to_all | solution.py:544
  48.4 0.8 broadcast_in_dim.39
  49.2 4.8 %all-to-all-start.1 = ((bf16[16,96,128]{2,1,0:T(8,128)(2,1)}), bf16[16,96,128]{2,1,0:T(8,128)(2,1)S(1)}, u32[]{:S(2)}, u32[]{:S(2)}) async-start(bf16[16,96,128]{2,1,0:T(8,128)(2,1)} %broadcast_in_dim.39), calls=%async_computation.1 | async-start | bytes 786432 | tf_op jit(solution)/shard_map/all_to_all | solution.py:549
  54.1 5.4 %collective-permute-start.5 = (bf16[144,384]{1,0:T(8,128)(2,1)S(1)}, bf16[144,384]{1,0:T(8,128)(2,1)S(1)}, u32[]{:S(2)}, u32[]{:S(2)}) collective-permute-start(bf16[144,384]{1,0:T(8,128)(2,1)S(1)} %get-tuple-element.39), channel_id=1, source_target_pairs={{0,8},{8,16},{16,24},{24,32},{32,40},{40,48},{48,56},{56,64},{64,7... | collective-permute-start | bytes 331784 | tf_op jit(solution)/shard_map/ppermute | solution.py:516
  59.4 2.7 %all-to-all-done.1 = bf16[16,96,128]{2,1,0:T(8,128)(2,1)S(1)} async-done(((bf16[16,96,128]{2,1,0:T(8,128)(2,1)}), bf16[16,96,128]{2,1,0:T(8,128)(2,1)S(1)}, u32[]{:S(2)}, u32[]{:S(2)}) %all-to-all-start.1) | async-done | bytes 393248 | tf_op jit(solution)/shard_map/all_to_all | solution.py:549
  62.1 0.1 multiply_reduce_fusion
  62.2 0.7 broadcast_in_dim.42
  62.9 4.7 %all-to-all-start.2 = ((bf16[8,96,128]{2,1,0:T(8,128)(2,1)}), bf16[8,96,128]{2,1,0:T(8,128)(2,1)S(1)}, u32[]{:S(2)}, u32[]{:S(2)}) async-start(bf16[8,96,128]{2,1,0:T(8,128)(2,1)} %broadcast_in_dim.42), calls=%async_computation.2 | async-start | bytes 393216 | tf_op jit(solution)/shard_map/all_to_all | solution.py:559
  67.6 0.2 merge_lon.1
  67.8 0.1 collective-permute-start.6
  67.9 0.1 collective-permute-start.7
  68.0 0.4 collective-permute-start.8
  68.4 7.9 %all-to-all-done.2 = bf16[8,96,128]{2,1,0:T(8,128)(2,1)S(1)} async-done(((bf16[8,96,128]{2,1,0:T(8,128)(2,1)}), bf16[8,96,128]{2,1,0:T(8,128)(2,1)S(1)}, u32[]{:S(2)}, u32[]{:S(2)}) %all-to-all-start.2) | async-done | bytes 196640 | tf_op jit(solution)/shard_map/all_to_all | solution.py:559
  76.4 3.3 %collective-permute-start.10 = (bf16[768,128]{1,0:T(8,128)(2,1)S(1)}, bf16[768,128]{1,0:T(8,128)(2,1)S(1)}, u32[]{:S(2)}, u32[]{:S(2)}) collective-permute-start(bf16[768,128]{1,0:T(8,128)(2,1)S(1)} %bitcast.8), channel_id=1, source_target_pairs={{0,8},{8,0},{16,24},{24,16},{32,40},{40,32},{48,56},{56,48},{64,72... | collective-permute-start | bytes 589832 | tf_op jit(solution)/shard_map/ppermute | solution.py:530
  79.7 0.0 collective-permute-done.7.lat
  79.7 1.1 %place_grad.1 = f32[2,2,12,24,192]{4,3,2,1,0:T(8,128)} custom-call(bf16[2,9,24,192]{3,2,1,0:T(8,128)(2,1)S(1)} %get-tuple-element.40.own, bf16[9,24,384]{2,1,0:T(8,128)(2,1)S(1)} %collective-permute-done.6.lev, bf16[3,24,384]{2,1,0:T(8,128)(2,1)S(1)} %collective-permute-done.7.lat, bf16[3,24,384]{2,1,0:T(8,128)(2,1)S(1)} %collective-permute-done.8.diag), custom_call_target="tpu_custom_call" | custom-call | flops 20000000000 | bytes 2097152 | tf_op jit(solution)/shard_map/place_grad/pallas_call | solution.py:464
  80.8 1.3 %finish_params.1 = (f32[192,576]{1,0:T(8,128)}, f32[192,192]{1,0:T(8,128)}, f32[1,6,2,3312]{3,2,1,0:T(2,128)}) custom-call(bf16[768,128]{1,0:T(8,128)(2,1)S(1)} %bitcast.9, bf16[768,128]{1,0:T(8,128)(2,1)S(1)} %collective-permute-done.10.other, s32[1,1]{1,0:T(1,128)} %bitcast.2.core), custom_call_target="tpu_custom_call" | custom-call | bytes 2097152 | tf_op jit(solution)/shard_map/finish_params/pallas_call | solution.py:498
  (24 shorter events, 0.2 us)
Async XLA Ops:
  0.6 1.1 %copy-start = (bf16[2,2,12,24,192]{4,3,2,1,0:T(8,128)(2,1)S(1)}, bf16[2,2,12,24,192]{4,3,2,1,0:T(8,128)(2,1)}, u32[]{:S(2)}) copy-start(bf16[2,2,12,24,192]{4,3,2,1,0:T(8,128)(2,1)} %refs_0_.5) | copy-start | bytes 1327108
  1.7 1.1 %copy-start.2 = (bf16[2,2,12,24,192]{4,3,2,1,0:T(8,128)(2,1)S(1)}, bf16[2,2,12,24,192]{4,3,2,1,0:T(8,128)(2,1)}, u32[]{:S(2)}) copy-start(bf16[2,2,12,24,192]{4,3,2,1,0:T(8,128)(2,1)} %refs_1_.5) | copy-start | bytes 1327108
  2.9 4.0 %copy-start.6 = (f32[1,2,6,3312]{3,1,2,0:T(2,128)S(1)}, f32[1,2,6,3312]{3,1,2,0:T(2,128)}, u32[]{:S(2)}) copy-start(f32[1,2,6,3312]{3,1,2,0:T(2,128)} %param.9) | copy-start | bytes 476932
  2.9 9.3 %collective-permute-start.1 = (bf16[2,144,384]{2,1,0:T(8,128)(2,1)S(1)}, bf16[2,144,384]{2,1,0:T(8,128)(2,1)S(1)}, u32[]{:S(2)}, u32[]{:S(2)}) collective-permute-start(bf16[2,144,384]{2,1,0:T(8,128)(2,1)S(1)} %pack_lon.1), channel_id=1, source_target_pairs={{0,248},{8,0},{16,8},{24,16},{32,24},{40,32},{48,40},{56,48},{64,5... | collective-permute-start | bytes 663560 | tf_op jit(solution)/shard_map/ppermute | solution.py:516
  6.3 11.0 %collective-permute-start = (bf16[2,162,384]{2,1,0:T(8,128)(2,1)S(1)}, bf16[2,162,384]{2,1,0:T(8,128)(2,1)S(1)}, u32[]{:S(2)}, u32[]{:S(2)}) collective-permute-start(bf16[2,162,384]{2,1,0:T(8,128)(2,1)S(1)} %pack_lev.1), channel_id=1, source_target_pairs={{0,1},{1,0},{2,3},{3,2},{4,5},{5,4},{6,7},{7,6},{8,9},{9,8},{10,11... | collective-permute-start | bytes 746504 | tf_op jit(solution)/shard_map/ppermute | solution.py:516
  6.9 5.3 %copy-start.1 = (bf16[2,2,12,24,192]{4,3,2,1,0:T(8,128)(2,1)S(1)}, bf16[2,2,12,24,192]{4,3,2,1,0:T(8,128)(2,1)}, u32[]{:S(2)}) copy-start(bf16[2,2,12,24,192]{4,3,2,1,0:T(8,128)(2,1)} %refs_0_.5) | copy-start | bytes 1327108
  6.9 5.3 %copy-start.3 = (bf16[2,2,12,24,192]{4,3,2,1,0:T(8,128)(2,1)S(1)}, bf16[2,2,12,24,192]{4,3,2,1,0:T(8,128)(2,1)}, u32[]{:S(2)}) copy-start(bf16[2,2,12,24,192]{4,3,2,1,0:T(8,128)(2,1)} %refs_1_.5) | copy-start | bytes 1327108
  9.6 7.8 %copy-start.4 = (bf16[192,576]{1,0:T(8,128)(2,1)S(1)}, bf16[192,576]{1,0:T(8,128)(2,1)}, u32[]{:S(2)}) copy-start(bf16[192,576]{1,0:T(8,128)(2,1)} %refs_2_.5) | copy-start | bytes 663556
  9.6 7.8 %copy-start.5 = (bf16[192,192]{1,0:T(8,128)(2,1)S(1)}, bf16[192,192]{1,0:T(8,128)(2,1)}, u32[]{:S(2)}) copy-start(bf16[192,192]{1,0:T(8,128)(2,1)} %refs_3_.5) | copy-start | bytes 221188
  12.4 7.7 %collective-permute-start.2 = (bf16[2,54,384]{2,1,0:T(8,128)(2,1)S(1)}, bf16[2,54,384]{2,1,0:T(8,128)(2,1)S(1)}, u32[]{:S(2)}, u32[]{:S(2)}) collective-permute-start(bf16[2,54,384]{2,1,0:T(8,128)(2,1)S(1)} %get-tuple-element.30), channel_id=1, source_target_pairs={{0,1},{1,0},{2,3},{3,2},{4,5},{5,4},{6,7},{7,6},{8,9},{9,8},{10,11... | collective-permute-start | bytes 248840 | tf_op jit(solution)/shard_map/ppermute | solution.py:516
  14.5 8.3 %collective-permute-start.3 = (bf16[2,3,24,384]{3,2,1,0:T(8,128)(2,1)S(1)}, bf16[2,3,24,384]{3,2,1,0:T(8,128)(2,1)S(1)}, u32[]{:S(2)}, u32[]{:S(2)}) collective-permute-start(bf16[2,3,24,384]{3,2,1,0:T(8,128)(2,1)S(1)} %get-tuple-element.35), channel_id=1, source_target_pairs={{0,6},{2,0},{4,2},{6,4},{1,7},{3,1},{5,3},{7,5},{8,14},{10,8},{12,... | collective-permute-start | bytes 331784 | tf_op jit(solution)/shard_map/ppermute | solution.py:516
  17.0 5.8 %collective-permute-start.4 = (bf16[2,3,24,384]{3,2,1,0:T(8,128)(2,1)S(1)}, bf16[2,3,24,384]{3,2,1,0:T(8,128)(2,1)S(1)}, u32[]{:S(2)}, u32[]{:S(2)}) collective-permute-start(bf16[2,3,24,384]{3,2,1,0:T(8,128)(2,1)S(1)} %get-tuple-element.36), channel_id=1, source_target_pairs={{0,7},{1,6},{2,1},{3,0},{4,3},{5,2},{6,5},{7,4},{8,15},{9,14},{10,... | collective-permute-start | bytes 331784 | tf_op jit(solution)/shard_map/ppermute | solution.py:526
  28.9 5.5 %collective-permute-start.9 = (bf16[768,128]{1,0:T(8,128)(2,1)S(1)}, bf16[768,128]{1,0:T(8,128)(2,1)S(1)}, u32[]{:S(2)}, u32[]{:S(2)}) collective-permute-start(bf16[768,128]{1,0:T(8,128)(2,1)S(1)} %get-tuple-element.48), channel_id=1, source_target_pairs={{0,8},{8,0},{16,24},{24,16},{32,40},{40,32},{48,56},{56,48},{64,72... | collective-permute-start | bytes 589832 | tf_op jit(solution)/shard_map/ppermute | solution.py:530
  49.2 12.9 %all-to-all-start.1 = ((bf16[16,96,128]{2,1,0:T(8,128)(2,1)}), bf16[16,96,128]{2,1,0:T(8,128)(2,1)S(1)}, u32[]{:S(2)}, u32[]{:S(2)}) async-start(bf16[16,96,128]{2,1,0:T(8,128)(2,1)} %broadcast_in_dim.39), calls=%async_computation.1 | async-start | bytes 786432 | tf_op jit(solution)/shard_map/all_to_all | solution.py:549
  54.1 13.5 %collective-permute-start.5 = (bf16[144,384]{1,0:T(8,128)(2,1)S(1)}, bf16[144,384]{1,0:T(8,128)(2,1)S(1)}, u32[]{:S(2)}, u32[]{:S(2)}) collective-permute-start(bf16[144,384]{1,0:T(8,128)(2,1)S(1)} %get-tuple-element.39), channel_id=1, source_target_pairs={{0,8},{8,16},{16,24},{24,32},{32,40},{40,48},{48,56},{56,64},{64,7... | collective-permute-start | bytes 331784 | tf_op jit(solution)/shard_map/ppermute | solution.py:516
  62.9 13.4 %all-to-all-start.2 = ((bf16[8,96,128]{2,1,0:T(8,128)(2,1)}), bf16[8,96,128]{2,1,0:T(8,128)(2,1)S(1)}, u32[]{:S(2)}, u32[]{:S(2)}) async-start(bf16[8,96,128]{2,1,0:T(8,128)(2,1)} %broadcast_in_dim.42), calls=%async_computation.2 | async-start | bytes 393216 | tf_op jit(solution)/shard_map/all_to_all | solution.py:559
  67.8 11.9 %collective-permute-start.6 = (bf16[9,24,384]{2,1,0:T(8,128)(2,1)S(1)}, bf16[9,24,384]{2,1,0:T(8,128)(2,1)S(1)}, u32[]{:S(2)}, u32[]{:S(2)}) collective-permute-start(bf16[9,24,384]{2,1,0:T(8,128)(2,1)S(1)} %get-tuple-element.41), channel_id=1, source_target_pairs={{0,1},{1,0},{2,3},{3,2},{4,5},{5,4},{6,7},{7,6},{8,9},{9,8},{10,11... | collective-permute-start | bytes 497672 | tf_op jit(solution)/shard_map/ppermute | solution.py:516
  67.9 11.8 %collective-permute-start.7 = (bf16[3,24,384]{2,1,0:T(8,128)(2,1)S(1)}, bf16[3,24,384]{2,1,0:T(8,128)(2,1)S(1)}, u32[]{:S(2)}, u32[]{:S(2)}) collective-permute-start(bf16[3,24,384]{2,1,0:T(8,128)(2,1)S(1)} %get-tuple-element.42), channel_id=1, source_target_pairs={{0,2},{2,4},{4,6},{6,0},{1,3},{3,5},{5,7},{7,1},{8,10},{10,12},{12... | collective-permute-start | bytes 165896 | tf_op jit(solution)/shard_map/ppermute | solution.py:516
  68.0 11.7 %collective-permute-start.8 = (bf16[3,24,384]{2,1,0:T(8,128)(2,1)S(1)}, bf16[3,24,384]{2,1,0:T(8,128)(2,1)S(1)}, u32[]{:S(2)}, u32[]{:S(2)}) collective-permute-start(bf16[3,24,384]{2,1,0:T(8,128)(2,1)S(1)} %get-tuple-element.43), channel_id=1, source_target_pairs={{0,3},{1,2},{2,5},{3,4},{4,7},{5,6},{6,1},{7,0},{8,11},{9,10},{10,... | collective-permute-start | bytes 165896 | tf_op jit(solution)/shard_map/ppermute | solution.py:526
  76.4 4.5 %collective-permute-start.10 = (bf16[768,128]{1,0:T(8,128)(2,1)S(1)}, bf16[768,128]{1,0:T(8,128)(2,1)S(1)}, u32[]{:S(2)}, u32[]{:S(2)}) collective-permute-start(bf16[768,128]{1,0:T(8,128)(2,1)S(1)} %bitcast.8), channel_id=1, source_target_pairs={{0,8},{8,0},{16,24},{24,16},{32,40},{40,32},{48,56},{56,48},{64,72... | collective-permute-start | bytes 589832 | tf_op jit(solution)/shard_map/ppermute | solution.py:530
